TPU v7x, 768 devices: a whole 4x8x12 slice. The times are simulated.
768 devices in a mesh: dp: 32 (over y, x), mp: 24 (over z, core).
Axes of the slice: x: 4, y: 8, z: 12, core: 2. Of those that a mesh axis runs over, the one named last changes fastest.
Arguments:
- patches: bfloat16 [9216, 6144], P('dp', 'mp'), may hold values from -6 to 6
- pack_route: int32 [9216, 1], P('dp'), may hold values from 0 to 31, as said below
- pack_slot: int32 [9216, 1], P('dp'), may hold values from 0 to 383, as said below
- project_weight: bfloat16 [6144, 9216], P(None, 'mp'), may hold values from -0.078125 to 0.078125
- cotangent: bfloat16 [12288, 3072], P('dp', 'mp'), may hold values from -6 to 6
Outputs:
- attention: bfloat16 [12288, 3072], P('dp', 'mp')
- weight_grad: float32 [6144, 9216], P('dp', 'mp')
Inputs may be any that keep to these rules, and one draw needn't show every extreme that they name: `pack_route`: loader shard s holds rows s * 288 to (s + 1) * 288 - 1. Each shard sends 288 rows in all and each pack receives 288 rows; among the rows of one shard at most 18 name the same pack, and every shard names some pack exactly 18 times. `pack_slot`: rows that name the same pack name different slots; within each block of 96 slots of a pack the named slots are the first ones; some image fills all 96 slots of its block, in the first block of some pack and in the second block of another.
All inputs are finite; a program needn't handle non-finite values.
Results may differ from a plain program's by a relative error of at most 0.024.
Values may be sent and summed in bfloat16 or wider, within the bound.
No kernel may reach another device: no remote copies, remote signals or barrier semaphores. Data moves between devices by JAX's collectives and lax.ppermute only.
A program may use at most 32 MiB of HBM per device.

v0:
```python
import jax
import jax.numpy as jnp
from jax import lax
from jax.sharding import PartitionSpec as P

CAP = 96


def attend(projected, filled):
    blocks = filled.shape[0]
    capacity = projected.shape[0] // blocks
    head_width_dim = projected.shape[1] // 3
    rounded = projected.astype(jnp.bfloat16).reshape(blocks, capacity, 3, head_width_dim)
    query_matrix = rounded[:, :, 0].astype(jnp.float32)
    key_matrix = rounded[:, :, 1].astype(jnp.float32)
    value_matrix = rounded[:, :, 2].astype(jnp.float32)
    logit_scores = jnp.einsum("lnw,lcw->lnc", query_matrix, key_matrix) * head_width_dim ** (-0.5)
    valid_token_mask = (jnp.arange(capacity, dtype=jnp.int32)[None, :] < filled[:, None]).astype(
        jnp.float32
    )
    expscore = jnp.exp(logit_scores) * valid_token_mask[:, None, :]
    denominator = jnp.sum(expscore, axis=-1) + (1.0 - valid_token_mask)
    softmax_weights = (expscore / denominator[..., None]).astype(jnp.bfloat16)
    attended_values = (
        jnp.einsum("fnp,fpg->fng", softmax_weights.astype(jnp.float32), value_matrix)
        * valid_token_mask[..., None]
    )
    return attended_values.astype(jnp.bfloat16).reshape(blocks * capacity, head_width_dim)


def shards(patches, pack_route, pack_slot, project_weight, cotangent):
    owners = lax.axis_size("dp")
    width_part = patches.shape[1]
    slot_count = cotangent.shape[0]
    send_rows = 2 * patches.shape[0] // owners
    matches = (pack_route == jnp.arange(owners, dtype=jnp.int32)[None, :]).astype(jnp.int32)
    before = jnp.cumsum(matches, axis=0) - matches
    position = jnp.sum(before * matches, axis=1)
    target = pack_route[:, 0] * send_rows + position
    outgoing = jnp.zeros((owners * send_rows, width_part), jnp.bfloat16).at[target].set(patches)
    outgoing = outgoing.reshape(owners, send_rows, width_part)
    slot_ids = (
        jnp.full((owners * send_rows,), slot_count, jnp.int32).at[target].set(pack_slot[:, 0])
    )
    slot_ids = slot_ids.reshape(owners, send_rows)
    arrived, arrived_slots = (
        lax.all_to_all(outgoing, "dp", split_axis=0, concat_axis=0, tiled=True),
        lax.all_to_all(slot_ids, "dp", split_axis=0, concat_axis=0, tiled=True),
    )
    flat_slots = arrived_slots.reshape(-1)
    local_rows = (
        jnp.zeros((slot_count, width_part), jnp.bfloat16)
        .at[flat_slots]
        .set(arrived.reshape(-1, width_part), mode="drop")
    )
    image_count = slot_count // CAP
    filled = jnp.sum(
        (flat_slots[:, None] // CAP == jnp.arange(image_count, dtype=jnp.int32)[None, :]).astype(
            jnp.int32
        ),
        axis=0,
    )
    gathered = lax.all_gather(local_rows, "mp", axis=1, tiled=True)
    projected = jnp.dot(gathered, project_weight, preferred_element_type=jnp.float32)
    attention, pull = jax.vjp(lambda z: attend(z, filled), projected)
    grad_projected = pull(cotangent)[0].astype(jnp.bfloat16)
    weight_grad = lax.psum_scatter(
        lax.dot_general(
            gathered, grad_projected, (((0,), (0,)), ((), ())), preferred_element_type=jnp.float32
        ).astype(jnp.bfloat16),
        "dp",
        scatter_dimension=0,
        tiled=True,
    ).astype(jnp.float32)
    return (attention, weight_grad)


def solution(mesh):
    in_specs = (P("dp", "mp"), P("dp", None), P("dp", None), P(None, "mp"), P("dp", "mp"))
    out_specs = (P("dp", "mp"), P("dp", "mp"))
    return jax.shard_map(shards, mesh=mesh, in_specs=in_specs, out_specs=out_specs, check_vma=False)
```

profile of v0, /device:TPU:1, one launch (start us, length us, event | category | flops | bytes accessed | tf_op | source)
XLA Modules:
  0.0 381.7 jit_solution(9472020061115807368)
XLA Ops:
  7.2 0.7 reduce
  7.9 0.7 reduce.3
  8.6 0.9 reduce-window.6
  9.5 0.2 slice_reduce_fusion
  9.7 0.1 bitcast_bitcast_fusion
  9.9 0.7 fusion.20
  10.6 2.9 scatter_custom_fusion
  13.5 0.7 all_to_all.9
  14.2 10.5 %all-to-all-start = ((s32[32,1,18]{2,1,0:T(1,128)}), s32[32,1,18]{2,1,0:T(1,128)S(1)}, u32[]{:S(2)}, u32[]{:S(2)}) async-start(s32[32,1,18]{2,1,0:T(1,128)} %bitcast.1), calls=%async_computation | async-start | bytes 32768 | tf_op jit(solution)/shard_map/all_to_all | solution.py:48
  24.7 2.0 scatter_custom_fusion.1
  26.7 0.8 reshape.203
  27.6 5.6 %all-to-all-done = s32[32,1,18]{2,1,0:T(1,128)S(1)} async-done(((s32[32,1,18]{2,1,0:T(1,128)}), s32[32,1,18]{2,1,0:T(1,128)S(1)}, u32[]{:S(2)}, u32[]{:S(2)}) %all-to-all-start) | async-done | bytes 2336 | tf_op jit(solution)/shard_map/all_to_all | solution.py:48
  33.2 3.9 %all-to-all-start.1 = ((bf16[32,18,256]{2,1,0:T(8,128)(2,1)}), bf16[32,18,256]{2,1,0:T(8,128)(2,1)S(1)}, u32[]{:S(2)}, u32[]{:S(2)}) async-start(bf16[32,18,256]{2,1,0:T(8,128)(2,1)} %reshape.203), calls=%async_computation.1 | async-start | bytes 786432 | tf_op jit(solution)/shard_map/all_to_all | solution.py:47
  37.1 0.0 all-gather.2.cloned.1.call-start
  37.1 0.5 broadcast.172
  37.7 0.8 fusion.21
  38.4 0.1 reshape.202
  38.6 10.3 %all-to-all-done.1 = bf16[32,18,256]{2,1,0:T(8,128)(2,1)S(1)} async-done(((bf16[32,18,256]{2,1,0:T(8,128)(2,1)}), bf16[32,18,256]{2,1,0:T(8,128)(2,1)S(1)}, u32[]{:S(2)}, u32[]{:S(2)}) %all-to-all-start.1) | async-done | bytes 294944 | tf_op jit(solution)/shard_map/all_to_all | solution.py:47
  48.9 0.1 reshape.230
  49.0 6.0 %scatter_custom_fusion.2 = bf16[384,256]{1,0:T(8,128)(2,1)} fusion(s32[576]{0:T(1024)S(1)} %fusion.16, bf16[576,256]{1,0:T(8,128)(2,1)S(1)} %reshape.230, bf16[]{:T(256)} %constant.12.clone.1), kind=kCustom, calls=%fused_computation.32 | custom fusion | bytes 196610 | tf_op jit(solution)/shard_map/scatter | solution.py:54
  54.9 0.0 all-gather.2.cloned.1.call-update
  55.0 0.2 reduce-scatter.2.cloned.1.call-start
  55.2 0.1 and_reduce_fusion
  55.3 0.1 and.13
  55.4 0.1 div.37
  55.6 0.1 convert_reduce_fusion
  55.7 0.1 fusion.19
  55.8 0.0 copy-start
  55.8 74.8 %all-gather.2.cloned.1.call-done = bf16[384,6144]{1,0:T(8,128)(2,1)} async-done(((bf16[384,256]{1,0:T(8,128)(2,1)}), bf16[384,6144]{1,0:T(8,128)(2,1)}) %all-gather.2.cloned.1.call-update) | async-done | bytes 4718608 | tf_op jit(solution)/shard_map/all_gather | solution.py:63
  130.5 6.4 %convolution_convert_fusion.1 = bf16[384,384]{1,0:T(8,128)(2,1)S(1)} fusion(bf16[384,6144]{1,0:T(8,128)(2,1)} %all-gather.2.cloned.1.call-done, bf16[6144,384]{1,0:T(8,128)(2,1)} %param.8), kind=kOutput, calls=%fused_computation.4 | convolution fusion | flops 1812086784 | bytes 9732096 | tf_op jit(solution)/shard_map/dot_general | solution.py:64
  136.9 0.1 reshape.205
  137.0 0.0 copy-start.1
  137.0 0.4 fusion.22
  137.4 0.2 multiply_reduce_fusion.1
  137.6 0.1 multiply_divide_fusion
  137.7 0.0 copy-done
  137.7 0.3 fusion.3
  138.0 0.3 multiply_reduce_fusion
  138.3 0.3 fusion.5
  138.6 0.2 fusion.4
  138.9 0.3 copy.37
  139.2 0.2 copy-done.1
  139.3 4.7 %convolution_convert_fusion = bf16[6144,384]{1,0:T(8,128)(2,1)} fusion(bf16[384,6144]{1,0:T(8,128)(2,1)S(1)} %copy-done.1, bf16[48,8,3,128]{3,2,1,0:T(4,128)(2,1)S(1)} %bitcast.52), kind=kOutput, calls=%fused_computation.3 | convolution fusion | flops 1814298624 | bytes 9732096 | tf_op jit(solution)/shard_map/dot_general | solution.py:68
  144.0 0.0 reduce-scatter.2.cloned.1.call-update
  144.1 1.0 fusion.1
  145.0 228.2 %reduce-scatter.2.cloned.1.call-done = bf16[192,384]{1,0:T(8,128)(2,1)} async-done(((bf16[6144,384]{1,0:T(8,128)(2,1)}), bf16[192,384]{1,0:T(8,128)(2,1)}) %reduce-scatter.2.cloned.1.call-update) | async-done | bytes 147472 | tf_op jit(solution)/shard_map/reduce_scatter | solution.py:67
  373.2 1.6 convert_element_type.80
  (8 shorter events, 0.1 us)
Async XLA Ops:
  14.2 19.0 %all-to-all-start = ((s32[32,1,18]{2,1,0:T(1,128)}), s32[32,1,18]{2,1,0:T(1,128)S(1)}, u32[]{:S(2)}, u32[]{:S(2)}) async-start(s32[32,1,18]{2,1,0:T(1,128)} %bitcast.1), calls=%async_computation | async-start | bytes 32768 | tf_op jit(solution)/shard_map/all_to_all | solution.py:48
  33.2 15.6 %all-to-all-start.1 = ((bf16[32,18,256]{2,1,0:T(8,128)(2,1)}), bf16[32,18,256]{2,1,0:T(8,128)(2,1)S(1)}, u32[]{:S(2)}, u32[]{:S(2)}) async-start(bf16[32,18,256]{2,1,0:T(8,128)(2,1)} %reshape.203), calls=%async_computation.1 | async-start | bytes 786432 | tf_op jit(solution)/shard_map/all_to_all | solution.py:47
  37.1 93.4 %all-gather.2.cloned.1.call-start = ((), (), s32[]{:S(2)}) async-start(), calls=%async_computation.3 | async-start | bytes 4915200 | tf_op jit(solution)/shard_map/all_gather | solution.py:63
  55.0 318.2 %reduce-scatter.2.cloned.1.call-start = ((), (), s32[]{:S(2)}) async-start(), calls=%async_computation.4 | async-start | bytes 4866048 | tf_op jit(solution)/shard_map/reduce_scatter | solution.py:67
  55.8 82.0 %copy-start = (bf16[384,128]{1,0:T(8,128)(2,1)S(1)}, bf16[384,128]{1,0:T(8,128)(2,1)}, u32[]{:S(2)}) copy-start(bf16[384,128]{1,0:T(8,128)(2,1)} %param.9) | copy-start | bytes 294916
  137.0 2.3 copy-start.1
Sparse Core Ops, SparseCore 0:
  55.1 75.3 all-gather.1
  144.2 228.9 reduce-scatter.1
where the time goes:
time: 385 us; the launch traced here: 382 us
  waiting for transfers between devices  319 us (83%)
  starting transfers between devices  14.6 us (4%)
  local copies, waits for them, and re-layouts  14.5 us (4%)
  between operations  14.2 us (4%)
  matrix products  13.4 us (3%)
  other arithmetic  6.01 us (2%)
    reduce_scatter x1, waiting for transfers between devices, shards(): lax.psum_scatter(lax.dot_general(gathered, grad_projected, (((0,), (0,)),...  228 us
    all_gather x1, waiting for transfers between devices, shards(): gathered = lax.all_gather(local_rows, 'mp', axis=1, tiled=True)  74.8 us
    all_to_all x1, starting transfers between devices, shards(): lax.all_to_all(slot_ids, 'dp', split_axis=0, concat_axis=0, tiled=True)  10.5 us
    all_to_all x1, waiting for transfers between devices, shards(): lax.all_to_all(outgoing, 'dp', split_axis=0, concat_axis=0, tiled=True)  10.3 us
  transfers between devices with their start and end apart: 4, of which 4 were waited for; matrix products, arithmetic and copies ran while one was open for 2% of the time, Pallas kernels for 0%

commit v1 on v0

v1 whole, which is shorter than its diff:
```python
import jax
import jax.numpy as jnp
from jax import lax
from jax.experimental import pallas as pl
from jax.experimental.pallas import tpu as pltpu
from jax.sharding import PartitionSpec as P

CAP = 96
HD = 128
SENT = 18
ROOM = 24
X, Y = 4, 8
F32, BF16, I32 = jnp.float32, jnp.bfloat16, jnp.int32


def iota(shape, dim):
    return lax.broadcasted_iota(I32, shape, dim)


def hot(condition):
    return jnp.where(condition, 1.0, 0.0).astype(BF16)


def mm(a, b, ca=1, cb=0):
    return lax.dot_general(a, b, (((ca,), (cb,)), ((), ())), preferred_element_type=F32)


def send_kernel(patches, route, slot, out):
    rows = patches.shape[0]
    owners = out.shape[0] // ROOM
    pack = route[...]
    place = slot[...]
    matches = hot(pack == iota((rows, owners), 1))
    before = mm(hot(iota((rows, rows), 0) > iota((rows, rows), 1)), matches)
    position = jnp.sum(before * matches.astype(F32), axis=1, keepdims=True).astype(I32)
    spread = hot(pack * ROOM + position == iota((rows, owners * ROOM), 1))
    total = mm(spread, patches[...], 0, 0)
    held = hot(position == iota((rows, 256), 1)).astype(F32)
    high = (held * ((place >> 1) + 1).astype(F32)).astype(BF16)
    low = (held * (place & 1).astype(F32)).astype(BF16)
    line, owner = iota((owners * ROOM, owners), 0), iota((owners * ROOM, owners), 1)
    for row, part in ((SENT, high), (SENT + 1, low)):
        total += mm(hot(line == owner * ROOM + row), mm(matches, part, 0, 0).astype(BF16))
    out[...] = total.astype(BF16)


def receive_kernel(arrived, out, offsets):
    lines = arrived.shape[0]
    owners = lines // ROOM
    rows = out.shape[0]
    data = arrived[...]
    line, owner = iota((owners, lines), 1), iota((owners, lines), 0)
    spread = hot((line >= owner * ROOM) & (line < owner * ROOM + ROOM))
    within = jnp.sum(
        jnp.where((line >= owner * ROOM) & (line < owner * ROOM + ROOM), line - owner * ROOM, 0),
        axis=0,
        keepdims=True,
    )
    chosen = iota((128, lines), 0) == within
    number = []
    for row in (SENT, SENT + 1):
        part = mm(hot(line == owner * ROOM + row), data)[:, :128].astype(BF16)
        wide = mm(part, spread, 0, 0)
        number.append(jnp.sum(jnp.where(chosen, wide, 0.0), axis=0, keepdims=True).astype(I32))
    live = (number[0] > 0) & (within < SENT)
    place = 2 * (number[0] - 1) + number[1]
    image = sum((place >= CAP * j).astype(I32) for j in (1, 2, 3))
    start, starts, base = jnp.zeros((1, 1), I32), [], jnp.zeros_like(place)
    for j in range(3):
        count = jnp.sum(jnp.where(live & (image == j), 1.0, 0.0), axis=1, keepdims=True)
        start = start + count.astype(I32)
        starts.append(start)
        base = jnp.where(image == j + 1, start, base)
    target = jnp.where(live, base + place - CAP * image, -1)
    out[...] = mm(hot(iota((rows, lines), 0) == target), data).astype(BF16)
    lane = iota((8, 128), 1)
    offsets[...] = sum(jnp.where(lane == j, starts[j], 0) for j in range(3))


def places(index, offsets):
    image, base, last = 0, 0, 0
    for j in range(3):
        start = offsets[0:1, j : j + 1]
        past = index >= start
        image = image + past.astype(I32)
        base = base + jnp.where(past, start - last, 0)
        last = start
    return image, index - base + CAP * image


def attend_kernel(features, weight, cotangent, offsets, attention, grads, total):
    step = pl.program_id(0)
    part = mm(features[0], weight[0])
    for k in range(1, features.shape[0]):
        part += mm(features[k], weight[k])

    @pl.when(step == 0)
    def _():
        total[...] = part

    @pl.when(step > 0)
    def _():
        total[...] += part

    @pl.when(step == pl.num_programs(0) - 1)
    def _():
        rows, slots = total.shape[0], attention.shape[0]
        offs = offsets[...]
        image_col, slot_col = places(iota((rows, 1), 0), offs)
        image_row, slot_row = places(iota((1, rows), 1), offs)
        same = image_col == image_row
        cot = mm(hot(slot_col == iota((rows, slots), 1)), cotangent[...]).astype(BF16)
        rounded = total[...].astype(BF16)
        query, key, value = rounded[:, :HD], rounded[:, HD : 2 * HD], rounded[:, 2 * HD :]
        scale = HD ** (-0.5)
        scores = mm(query, key, 1, 1) * scale
        expscore = jnp.where(same, jnp.exp(jnp.where(same, scores, 0.0)), 0.0)
        softmax = expscore / jnp.sum(expscore, axis=1, keepdims=True)
        weights = softmax.astype(BF16)
        result = mm(weights, value).astype(BF16)
        attention[...] = mm(hot(iota((slots, rows), 0) == slot_row), result).astype(BF16)
        d_value = mm(weights, cot, 0, 0)
        d_weights = mm(cot, value, 1, 1).astype(BF16).astype(F32)
        d_weights = jnp.where(same, d_weights, 0.0)
        inner = jnp.sum(d_weights * softmax, axis=1, keepdims=True)
        d_scores = (softmax * (d_weights - inner) * scale).astype(BF16)
        grads[:, :HD] = mm(d_scores, key).astype(BF16)
        grads[:, HD : 2 * HD] = mm(d_scores, query, 0, 0).astype(BF16)
        grads[:, 2 * HD :] = d_value.astype(BF16)


def split_kernel(core, features, out):
    def tile(t):
        return features[t // 2, :, (t % 2) * 128 : (t % 2) * 128 + 128]

    row, col = iota((256, 128), 0), iota((256, 128), 1)
    near = hot(row == jnp.where(col < 64, col, col + 64))
    far = hot(row == jnp.where(col < 64, col + 64, col + 128))
    for x, (whole, cut, pick) in enumerate(((0, 1, near), (2, 1, far), (3, 4, near), (5, 4, far))):
        out[x, :, 0:128] = tile(whole)
        out[x, :, 128:256] = tile(whole + 6)
        both = jnp.concatenate([tile(cut), tile(cut + 6)], axis=1)
        out[x, :, 256:384] = mm(both, pick).astype(BF16)


def weight_kernel(core, own, other, grads, out):
    depth = grads.shape[0] * grads.shape[1]
    right = grads[...].reshape(depth, grads.shape[2])
    for source, side in ((own, core[0]), (other, 1 - core[0])):
        for a in range(2):
            left = source[:, :, a * 384 : a * 384 + 384].reshape(depth, 384)
            term = mm(left, right, 0, 0).astype(BF16)
            at = side * 4 + a * 2
            for b in range(2):
                out[at + b, 0:128] = term[b * 128 : b * 128 + 128]
                out[at + b, 128:192] = term[256 + b * 64 : 320 + b * 64]


def sum_kernel(odd, terms, out):
    total = terms[0].astype(F32)
    for k in range(1, terms.shape[0]):
        total += terms[k].astype(F32)

    @pl.when(odd[0] == 0)
    def _():
        out[...] = total

    @pl.when(odd[0] == 1)
    def _():
        out[0:64] = total[128:192]
        out[64:192] = total[0:128]


def params():
    return pltpu.CompilerParams(vmem_limit_bytes=40 * 1024 * 1024)


def cost(flops, moved):
    return pl.CostEstimate(flops=flops, bytes_accessed=moved, transcendentals=0)


VMEM = pl.BlockSpec(memory_space=pltpu.VMEM)
SMEM = pl.BlockSpec(memory_space=pltpu.SMEM)


def shards(patches, pack_route, pack_slot, project_weight, cotangent):
    owners, heads = lax.axis_size("dp"), lax.axis_size("mp")
    rows, width = patches.shape
    slots = cotangent.shape[0]
    cols = project_weight.shape[1]
    core = (lax.axis_index("mp") % 2).astype(I32).reshape(1)
    odd = (lax.axis_index("dp") % 2).astype(I32).reshape(1)
    along_x = [[y * X + x for x in range(X)] for y in range(Y)]
    along_y = [[y * X + x for y in range(Y)] for x in range(X)]

    outgoing = pl.pallas_call(
        send_kernel,
        out_shape=jax.ShapeDtypeStruct((owners * ROOM, width), BF16),
        in_specs=[VMEM] * 3,
        out_specs=VMEM,
        compiler_params=params(),
        name="send",
    )(patches, pack_route, pack_slot)
    arrived = lax.all_to_all(outgoing.reshape(owners, ROOM, width), "dp", 0, 0, tiled=True)
    compact, offsets = pl.pallas_call(
        receive_kernel,
        out_shape=(
            jax.ShapeDtypeStruct((rows, width), BF16),
            jax.ShapeDtypeStruct((8, 128), I32),
        ),
        in_specs=[VMEM],
        out_specs=(VMEM, VMEM),
        compiler_params=params(),
        name="receive",
    )(arrived.reshape(owners * ROOM, width))

    features = lax.all_gather(compact, "mp", axis=0)

    part = heads // 4
    outbound = pl.pallas_call(
        split_kernel,
        grid_spec=pltpu.PrefetchScalarGridSpec(
            num_scalar_prefetch=1,
            grid=(2,),
            in_specs=[pl.BlockSpec((part, rows, width), lambda a, core: (core[0] * 2 + a, 0, 0))],
            out_specs=pl.BlockSpec((X, rows, 384), lambda a, core: (0, 0, a)),
        ),
        out_shape=jax.ShapeDtypeStruct((X, rows, 768), BF16),
        compiler_params=params(),
        cost_estimate=cost(0, 4 * rows * 768 * 4),
        name="split",
    )(core, features)
    own = lax.all_to_all(outbound, "dp", 0, 0, axis_index_groups=along_x, tiled=True)
    other = lax.ppermute(own, "mp", [(k, k ^ 1) for k in range(heads)])

    step = 4
    attention, grads = pl.pallas_call(
        attend_kernel,
        grid=(heads // step,),
        in_specs=[
            pl.BlockSpec((step, rows, width), lambda k: (k, 0, 0)),
            pl.BlockSpec((step, width, cols), lambda k: (k, 0, 0)),
            pl.BlockSpec((slots, HD), lambda k: (0, 0)),
            pl.BlockSpec((8, 128), lambda k: (0, 0)),
        ],
        out_specs=(
            pl.BlockSpec((slots, HD), lambda k: (0, 0)),
            pl.BlockSpec((rows, cols), lambda k: (0, 0)),
        ),
        out_shape=(
            jax.ShapeDtypeStruct((slots, HD), BF16),
            jax.ShapeDtypeStruct((rows, cols), BF16),
        ),
        scratch_shapes=[pltpu.VMEM((rows, cols), F32)],
        compiler_params=params(),
        cost_estimate=cost(2 * heads * rows * width * cols, 9 * 1024 * 1024),
        name="attend",
    )(features, project_weight.reshape(heads, width, cols), cotangent, offsets)

    all_grads = lax.all_gather(grads, "dp", axis=0, axis_index_groups=along_x)
    terms = pl.pallas_call(
        weight_kernel,
        out_shape=jax.ShapeDtypeStruct((Y, 192, cols), BF16),
        in_specs=[SMEM] + [VMEM] * 3,
        out_specs=VMEM,
        compiler_params=params(),
        cost_estimate=cost(2 * 4 * rows * 1536 * cols, 6 * 1024 * 1024),
        name="weight",
    )(core, own, other, all_grads)
    gathered = lax.all_to_all(terms, "dp", 0, 0, axis_index_groups=along_y, tiled=True)
    weight_grad = pl.pallas_call(
        sum_kernel,
        out_shape=jax.ShapeDtypeStruct((192, cols), F32),
        in_specs=[SMEM, VMEM],
        out_specs=VMEM,
        compiler_params=params(),
        name="sum",
    )(odd, gathered)
    return attention, weight_grad


def solution(mesh):
    in_specs = (P("dp", "mp"), P("dp", None), P("dp", None), P(None, "mp"), P("dp", "mp"))
    out_specs = (P("dp", "mp"), P("dp", "mp"))
    return jax.shard_map(shards, mesh=mesh, in_specs=in_specs, out_specs=out_specs, check_vma=False)
```

time: 385 us -> 203 us (0.53)
  waiting for transfers between devices: 319 us -> 99.7 us
  blocking collectives: 0 us -> 60.6 us
  Pallas kernels: 0 us -> 13.7 us
  matrix products: 13.4 us -> 0 us
  local copies, waits for them, and re-layouts: 14.5 us -> 4.55 us
  other arithmetic: 6.01 us -> 0 us
  starting transfers between devices: 14.6 us -> 9.9 us
    reduce_scatter x1 -> x0, waiting for transfers between devices: 228 us -> none  [shards(): lax.psum_scatter(lax.dot_general(gathered, grad_projected, (((0,), (0,)),...]
    all_to_all x0 -> x2, blocking collectives: none -> 48.1 us  [the longest x1 26.3 us: shards(): lax.all_to_all(outbound, 'dp', 0, 0, axis_index_groups=along_x, tiled=True)]
    all_to_all x2 -> x1, waiting for transfers between devices: 15.9 us -> 32 us  [shards(): lax.all_to_all(terms, 'dp', 0, 0, axis_index_groups=along_y, tiled=True)]
    pallas_call x0 -> x6, Pallas kernels: none -> 13.7 us  [the longest x1 5.32 us: shards(): pl.pallas_call(attend_kernel, grid=(heads // step,), in_specs=[pl.BlockSp...]
    dot_general x8 -> x0, matrix products: 13.4 us -> none  [the longest x1 6.36 us: shards(): jnp.dot(gathered, project_weight, preferred_element_type=jnp.float32)]
    all_gather x0 -> x1, blocking collectives: none -> 12.5 us  [shards(): all_grads = lax.all_gather(grads, 'dp', axis=0, axis_index_groups=along_x)]
    scatter x3 -> x0, local copies, waits for them, and re-layouts: 10.9 us -> none  [the longest x1 5.99 us: shards(): local_rows = jnp.zeros((slot_count, width_part), jnp.bfloat16).at[flat_sl...]
    all_to_all x2 -> x1, starting transfers between devices: 14.4 us -> 6.46 us  [shards(): lax.all_to_all(terms, 'dp', 0, 0, axis_index_groups=along_y, tiled=True)]
  transfers between devices with their start and end apart: 4 -> 3, of which waited for: 4 -> 2; matrix products, arithmetic and copies ran while one was open for 2% -> 0% of each run, Pallas kernels for 0% -> 3%
where the time goes in v1:
time: 203 us
  waiting for transfers between devices  99.7 us (49%)
  blocking collectives  60.6 us (30%)
  between operations  14.1 us (7%)
  Pallas kernels  13.7 us (7%)
  starting transfers between devices  9.9 us (5%)
  local copies, waits for them, and re-layouts  4.55 us (2%)
    all_gather x1, waiting for transfers between devices, shards(): features = lax.all_gather(compact, 'mp', axis=0)  67.7 us
    all_to_all x1, waiting for transfers between devices, shards(): lax.all_to_all(terms, 'dp', 0, 0, axis_index_groups=along_y, tiled=True)  32 us
    all_to_all x1, blocking collectives, shards(): lax.all_to_all(outbound, 'dp', 0, 0, axis_index_groups=along_x, tiled=True)  26.3 us
    all_to_all x1, blocking collectives, shards(): lax.all_to_all(outgoing.reshape(owners, ROOM, width), 'dp', 0, 0, tiled=T...  21.8 us
    all_gather x1, blocking collectives, shards(): all_grads = lax.all_gather(grads, 'dp', axis=0, axis_index_groups=along_x)  12.5 us
    all_to_all x1, starting transfers between devices, shards(): lax.all_to_all(terms, 'dp', 0, 0, axis_index_groups=along_y, tiled=True)  6.46 us
    pallas_call x1, Pallas kernels, shards(): pl.pallas_call(attend_kernel, grid=(heads // step,), in_specs=[pl.BlockSp...  5.32 us
    unnamed x12, local copies, waits for them, and re-layouts  4.55 us
  transfers between devices with their start and end apart: 3, of which 2 were waited for; matrix products, arithmetic and copies ran while one was open for 0% of the time, Pallas kernels for 3%

profile of v1, /device:TPU:1, one launch (start us, length us, event | category | flops | bytes accessed | tf_op | source)
XLA Modules:
  0.0 202.6 jit_solution(1704734029759874787)
XLA Ops:
  7.2 0.0 all-gather.4.cloned.1.call-start
  7.2 0.8 copy.7.route
  8.0 0.8 copy.8.slot
  8.9 0.0 copy-start.3
  8.9 0.9 copy-done.3
  9.8 1.4 send.1
  11.2 21.8 %all_to_all.15 = bf16[32,24,256]{2,1,0:T(8,128)(2,1)S(1)} all-to-all(bf16[32,24,256]{2,1,0:T(8,128)(2,1)S(1)} %bitcast.12), channel_id=1, replica_groups=mesh['dp'=32,'mp'=24] {'dp'}, dimensions={0} | all-to-all | bytes 786432 | tf_op jit(solution)/shard_map/all_to_all | solution.py:204
  32.9 1.9 receive.1
  34.8 0.0 all-gather.4.cloned.1.call-update
  34.9 67.7 %all-gather.4.cloned.1.call-done = bf16[6912,256]{1,0:T(8,128)(2,1)} async-done(((bf16[288,256]{1,0:T(8,128)(2,1)}), bf16[6912,256]{1,0:T(8,128)(2,1)}) %all-gather.4.cloned.1.call-update) | async-done | bytes 3538960 | tf_op jit(solution)/shard_map/all_gather | solution.py:217
  102.6 0.0 copy-start
  102.6 2.0 copy-done
  104.6 0.0 copy-start.2
  104.6 0.0 copy-start.4
  104.6 1.0 split.1
  105.6 0.0 copy-start.1
  105.6 26.3 %all_to_all.16.own = bf16[4,288,768]{2,1,0:T(8,128)(2,1)S(1)} all-to-all(bf16[4,288,768]{2,1,0:T(8,128)(2,1)S(1)} %split.1), channel_id=1, replica_groups={{0,24,48,72},{96,120,144,168},{192,216,240,264},{288,312,336,360},{384,..., dimensions={0} | all-to-all | bytes 3538944 | tf_op jit(solution)/shard_map/all_to_all | solution.py:233
  131.9 3.4 %collective-permute-start = (bf16[4,288,768]{2,1,0:T(8,128)(2,1)S(1)}, bf16[4,288,768]{2,1,0:T(8,128)(2,1)S(1)}, u32[]{:S(2)}, u32[]{:S(2)}) collective-permute-start(bf16[4,288,768]{2,1,0:T(8,128)(2,1)S(1)} %all_to_all.16.own), channel_id=1, source_target_pairs={{0,1},{1,0},{2,3},{3,2},{4,5},{5,4},{6,7},{7,6},{8,9},{9,8},{10,11... | collective-permute-start | bytes 5308424 | tf_op jit(solution)/shard_map/ppermute | solution.py:234
  135.3 0.0 copy-done.2
  135.3 0.0 copy-done.4
  135.3 0.0 copy-done.1
  135.3 5.3 %attend.1 = (bf16[384,128]{1,0:T(8,128)(2,1)}, bf16[288,384]{1,0:T(8,128)(2,1)S(1)}) custom-call(bf16[24,288,256]{2,1,0:T(8,128)(2,1)S(1)} %bitcast.8, bf16[24,256,384]{2,1,0:T(8,128)(2,1)S(1)} %bitcast.9, bf16[384,128]{1,0:T(8,128)(2,1)S(1)} %copy-done.4, s32[8,128]{1,0:T(8,128)S(1)} %get-tuple-element.7.offsets), custom_call_target="tpu_custom_call" | custom-call | flops 1358954496 | bytes 9437184 | tf_op jit(solution)/shard_map/attend/pallas_call | solution.py:237
  140.6 12.5 %all-gather.1 = bf16[1152,384]{1,0:T(8,128)(2,1)S(1)} all-gather(bf16[288,384]{1,0:T(8,128)(2,1)S(1)} %get-tuple-element.9), channel_id=3, replica_groups={{0,24,48,72},{96,120,144,168},{192,216,240,264},{288,312,336,360},{384,..., dimensions={0}, use_global_device_ids=true | all-gather | bytes 1105920 | tf_op jit(solution)/shard_map/all_gather | solution.py:260
  153.2 0.0 collective-permute-done.other
  153.2 3.2 %weight.1 = bf16[8,192,384]{2,1,0:T(8,128)(2,1)} custom-call(s32[1]{0:T(128)} %bitcast.5.core, bf16[4,288,768]{2,1,0:T(8,128)(2,1)S(1)} %all_to_all.16.own, bf16[4,288,768]{2,1,0:T(8,128)(2,1)S(1)} %collective-permute-done.other, bf16[4,288,384]{2,1,0:T(8,128)(2,1)S(1)} %bitcast.10), custom_call_target="tpu_custom_call" | custom-call | flops 1358954496 | bytes 6291456 | tf_op jit(solution)/shard_map/weight/pallas_call | solution.py:261
  156.4 6.5 %all-to-all-start.2 = ((bf16[8,192,384]{2,1,0:T(8,128)(2,1)}), bf16[8,192,384]{2,1,0:T(8,128)(2,1)S(1)}, u32[]{:S(2)}, u32[]{:S(2)}) async-start(bf16[8,192,384]{2,1,0:T(8,128)(2,1)} %weight.1), calls=%async_computation.2 | async-start | bytes 2359296 | tf_op jit(solution)/shard_map/all_to_all | solution.py:270
  162.8 32.0 %all-to-all-done.2.terms = bf16[8,192,384]{2,1,0:T(8,128)(2,1)S(1)} async-done(((bf16[8,192,384]{2,1,0:T(8,128)(2,1)}), bf16[8,192,384]{2,1,0:T(8,128)(2,1)S(1)}, u32[]{:S(2)}, u32[]{:S(2)}) %all-to-all-start.2) | async-done | bytes 1179680 | tf_op jit(solution)/shard_map/all_to_all | solution.py:270
  194.8 0.9 sum.1
Async XLA Ops:
  7.2 95.4 %all-gather.4.cloned.1.call-start = ((), (), s32[]{:S(2)}) async-start(), calls=%async_computation.3 | async-start | bytes 3686400 | tf_op jit(solution)/shard_map/all_gather | solution.py:217
  8.9 0.9 copy-start.3
  102.6 2.0 copy-start
  104.6 30.7 %copy-start.2 = (bf16[6144,384]{1,0:T(8,128)(2,1)S(1)}, bf16[6144,384]{1,0:T(8,128)(2,1)}, u32[]{:S(2)}) copy-start(bf16[6144,384]{1,0:T(8,128)(2,1)} %param.8) | copy-start | bytes 14155780
  104.6 30.7 %copy-start.4 = (bf16[384,128]{1,0:T(8,128)(2,1)S(1)}, bf16[384,128]{1,0:T(8,128)(2,1)}, u32[]{:S(2)}) copy-start(bf16[384,128]{1,0:T(8,128)(2,1)} %cotangent.1) | copy-start | bytes 294916
  105.6 29.7 %copy-start.1 = (bf16[6912,256]{1,0:T(8,128)(2,1)S(1)}, bf16[6912,256]{1,0:T(8,128)(2,1)}, u32[]{:S(2)}) copy-start(bf16[6912,256]{1,0:T(8,128)(2,1)} %all-gather.4.cloned.1.call-done) | copy-start | bytes 10616836
  131.9 21.3 %collective-permute-start = (bf16[4,288,768]{2,1,0:T(8,128)(2,1)S(1)}, bf16[4,288,768]{2,1,0:T(8,128)(2,1)S(1)}, u32[]{:S(2)}, u32[]{:S(2)}) collective-permute-start(bf16[4,288,768]{2,1,0:T(8,128)(2,1)S(1)} %all_to_all.16.own), channel_id=1, source_target_pairs={{0,1},{1,0},{2,3},{3,2},{4,5},{5,4},{6,7},{7,6},{8,9},{9,8},{10,11... | collective-permute-start | bytes 5308424 | tf_op jit(solution)/shard_map/ppermute | solution.py:234
  156.4 38.5 %all-to-all-start.2 = ((bf16[8,192,384]{2,1,0:T(8,128)(2,1)}), bf16[8,192,384]{2,1,0:T(8,128)(2,1)S(1)}, u32[]{:S(2)}, u32[]{:S(2)}) async-start(bf16[8,192,384]{2,1,0:T(8,128)(2,1)} %weight.1), calls=%async_computation.2 | async-start | bytes 2359296 | tf_op jit(solution)/shard_map/all_to_all | solution.py:270
Sparse Core Ops, SparseCore 0:
  34.9 67.5 all-gather.3

commit v2 on v1

--- a/solution.py
+++ b/solution.py
@@ -44,10 +44,11 @@
     out[...] = total.astype(BF16)
 
 
-def receive_kernel(arrived, out, offsets):
+def receive_kernel(arrived, first, second, offsets):
     lines = arrived.shape[0]
     owners = lines // ROOM
-    rows = out.shape[0]
+    half = first.shape[0]
+    rows = 2 * half
     data = arrived[...]
     line, owner = iota((owners, lines), 1), iota((owners, lines), 0)
     spread = hot((line >= owner * ROOM) & (line < owner * ROOM + ROOM))
@@ -72,7 +73,9 @@
         starts.append(start)
         base = jnp.where(image == j + 1, start, base)
     target = jnp.where(live, base + place - CAP * image, -1)
-    out[...] = mm(hot(iota((rows, lines), 0) == target), data).astype(BF16)
+    both = mm(hot(iota((rows, lines), 0) == target), data).astype(BF16)
+    first[...] = both[:half]
+    second[...] = both[half:]
     lane = iota((8, 128), 1)
     offsets[...] = sum(jnp.where(lane == j, starts[j], 0) for j in range(3))
 
@@ -88,19 +91,27 @@
     return image, index - base + CAP * image
 
 
-def attend_kernel(features, weight, cotangent, offsets, attention, grads, total):
+def attend_kernel(
+    core, own1, own2, far1, far2, weight, cotangent, offsets, attention, grads, total
+):
     step = pl.program_id(0)
-    part = mm(features[0], weight[0])
-    for k in range(1, features.shape[0]):
-        part += mm(features[k], weight[k])
+    half = own1.shape[1]
+    parts = [None, None]
+    for k in range(own1.shape[0]):
+        near_weight, far_weight = weight[k, core[0]], weight[k, 1 - core[0]]
+        for i, (near, far) in enumerate(((own1, far1), (own2, far2))):
+            term = mm(near[k], near_weight) + mm(far[k], far_weight)
+            parts[i] = term if k == 0 else parts[i] + term
 
     @pl.when(step == 0)
     def _():
-        total[...] = part
+        total[:half] = parts[0]
+        total[half:] = parts[1]
 
     @pl.when(step > 0)
     def _():
-        total[...] += part
+        total[:half] += parts[0]
+        total[half:] += parts[1]
 
     @pl.when(step == pl.num_programs(0) - 1)
     def _():
@@ -129,31 +140,46 @@
         grads[:, 2 * HD :] = d_value.astype(BF16)
 
 
+PICKS = (((0, 1), (4, 1), (5, 2), (3, 2)), ((2, 3), (0, 3), (1, 4), (5, 4)))
+
+
 def split_kernel(core, features, out):
-    def tile(t):
-        return features[t // 2, :, (t % 2) * 128 : (t % 2) * 128 + 128]
-
     row, col = iota((256, 128), 0), iota((256, 128), 1)
-    near = hot(row == jnp.where(col < 64, col, col + 64))
-    far = hot(row == jnp.where(col < 64, col + 64, col + 128))
-    for x, (whole, cut, pick) in enumerate(((0, 1, near), (2, 1, far), (3, 4, near), (5, 4, far))):
-        out[x, :, 0:128] = tile(whole)
-        out[x, :, 128:256] = tile(whole + 6)
-        both = jnp.concatenate([tile(cut), tile(cut + 6)], axis=1)
-        out[x, :, 256:384] = mm(both, pick).astype(BF16)
-
-
-def weight_kernel(core, own, other, grads, out):
-    depth = grads.shape[0] * grads.shape[1]
-    right = grads[...].reshape(depth, grads.shape[2])
-    for source, side in ((own, core[0]), (other, 1 - core[0])):
+    low = hot(row == jnp.where(col < 64, col, col + 64))
+    high = hot(row == jnp.where(col < 64, col + 64, col + 128))
+
+    def tile(group, t):
+        return features[3 * group + t // 2, :, (t % 2) * 128 : (t % 2) * 128 + 128]
+
+    for side, picks in enumerate(PICKS):
+
+        @pl.when(core[0] == side)
+        def _(picks=picks):
+            for x, (whole, cut) in enumerate(picks):
+                for a in range(2):
+                    at = a * 384
+                    out[x, :, at : at + 128] = tile(2 * a, whole)
+                    out[x, :, at + 128 : at + 256] = tile(2 * a + 1, whole)
+                    both = jnp.concatenate([tile(2 * a, cut), tile(2 * a + 1, cut)], axis=1)
+                    out[x, :, at + 256 : at + 384] = mm(both, (low, high)[x % 2]).astype(BF16)
+
+
+def weight_kernel(core, inner, own1, own2, far1, far2, grads, out):
+    packs, half = own1.shape[0], own1.shape[1]
+    depth = packs * half
+    right1 = grads[:, :half].reshape(depth, grads.shape[2])
+    right2 = grads[:, half:].reshape(depth, grads.shape[2])
+    for left1, left2, side in ((own1, own2, core[0]), (far1, far2, 1 - core[0])):
+        whole_side = jnp.where(inner[0] == 1, 1 - side, side)
         for a in range(2):
-            left = source[:, :, a * 384 : a * 384 + 384].reshape(depth, 384)
-            term = mm(left, right, 0, 0).astype(BF16)
-            at = side * 4 + a * 2
+            at = slice(a * 384, a * 384 + 384)
+            term = mm(left1[:, :, at].reshape(depth, 384), right1, 0, 0)
+            term += mm(left2[:, :, at].reshape(depth, 384), right2, 0, 0)
+            term = term.astype(BF16)
             for b in range(2):
-                out[at + b, 0:128] = term[b * 128 : b * 128 + 128]
-                out[at + b, 128:192] = term[256 + b * 64 : 320 + b * 64]
+                group = 2 * a + b
+                out[2 * group + whole_side, 0:128] = term[b * 128 : b * 128 + 128]
+                out[2 * group + side, 128:192] = term[256 + b * 64 : 320 + b * 64]
 
 
 def sum_kernel(odd, terms, out):
@@ -189,6 +215,8 @@
     slots = cotangent.shape[0]
     cols = project_weight.shape[1]
     core = (lax.axis_index("mp") % 2).astype(I32).reshape(1)
+    x_index = lax.axis_index("dp") % X
+    inner = ((x_index == 1) | (x_index == 2)).astype(I32).reshape(1)
     odd = (lax.axis_index("dp") % 2).astype(I32).reshape(1)
     along_x = [[y * X + x for x in range(X)] for y in range(Y)]
     along_y = [[y * X + x for y in range(Y)] for x in range(X)]
@@ -202,71 +230,92 @@
         name="send",
     )(patches, pack_route, pack_slot)
     arrived = lax.all_to_all(outgoing.reshape(owners, ROOM, width), "dp", 0, 0, tiled=True)
-    compact, offsets = pl.pallas_call(
+    half = rows // 2
+    first, second, offsets = pl.pallas_call(
         receive_kernel,
         out_shape=(
-            jax.ShapeDtypeStruct((rows, width), BF16),
+            jax.ShapeDtypeStruct((half, width), BF16),
+            jax.ShapeDtypeStruct((half, width), BF16),
             jax.ShapeDtypeStruct((8, 128), I32),
         ),
         in_specs=[VMEM],
-        out_specs=(VMEM, VMEM),
+        out_specs=(VMEM, VMEM, VMEM),
         compiler_params=params(),
         name="receive",
     )(arrived.reshape(owners * ROOM, width))
 
-    features = lax.all_gather(compact, "mp", axis=0)
-
-    part = heads // 4
-    outbound = pl.pallas_call(
-        split_kernel,
+    depth = heads // 2
+    same_core = [[2 * z + c for z in range(depth)] for c in range(2)]
+    sibling = [(k, k ^ 1) for k in range(heads)]
+
+    def split(features):
+        return pl.pallas_call(
+            split_kernel,
+            out_shape=jax.ShapeDtypeStruct((X, half, 768), BF16),
+            in_specs=[SMEM, VMEM],
+            out_specs=VMEM,
+            compiler_params=params(),
+            cost_estimate=cost(0, 2 * half * 768 * 4),
+            name="split",
+        )(core, features)
+
+    def over_x(block):
+        return lax.all_to_all(block, "dp", 0, 0, axis_index_groups=along_x, tiled=True)
+
+    own1 = lax.all_gather(first, "mp", axis=0, axis_index_groups=same_core)
+    out1 = split(own1)
+    second, out1 = lax.optimization_barrier((second, out1))
+    near1 = over_x(out1)
+    far1 = lax.ppermute(own1, "mp", sibling)
+    own2 = lax.all_gather(second, "mp", axis=0, axis_index_groups=same_core)
+    out2 = split(own2)
+    near2 = over_x(out2)
+    far2 = lax.ppermute(own2, "mp", sibling)
+
+    step = 2
+    block = pl.BlockSpec((step, half, width), lambda k, core: (k, 0, 0))
+    attention, grads = pl.pallas_call(
+        attend_kernel,
         grid_spec=pltpu.PrefetchScalarGridSpec(
             num_scalar_prefetch=1,
-            grid=(2,),
-            in_specs=[pl.BlockSpec((part, rows, width), lambda a, core: (core[0] * 2 + a, 0, 0))],
-            out_specs=pl.BlockSpec((X, rows, 384), lambda a, core: (0, 0, a)),
-        ),
-        out_shape=jax.ShapeDtypeStruct((X, rows, 768), BF16),
-        compiler_params=params(),
-        cost_estimate=cost(0, 4 * rows * 768 * 4),
-        name="split",
-    )(core, features)
-    own = lax.all_to_all(outbound, "dp", 0, 0, axis_index_groups=along_x, tiled=True)
-    other = lax.ppermute(own, "mp", [(k, k ^ 1) for k in range(heads)])
-
-    step = 4
-    attention, grads = pl.pallas_call(
-        attend_kernel,
-        grid=(heads // step,),
-        in_specs=[
-            pl.BlockSpec((step, rows, width), lambda k: (k, 0, 0)),
-            pl.BlockSpec((step, width, cols), lambda k: (k, 0, 0)),
-            pl.BlockSpec((slots, HD), lambda k: (0, 0)),
-            pl.BlockSpec((8, 128), lambda k: (0, 0)),
-        ],
-        out_specs=(
-            pl.BlockSpec((slots, HD), lambda k: (0, 0)),
-            pl.BlockSpec((rows, cols), lambda k: (0, 0)),
+            grid=(depth // step,),
+            in_specs=[block] * 4
+            + [
+                pl.BlockSpec((step, 2, width, cols), lambda k, core: (k, 0, 0, 0)),
+                pl.BlockSpec((slots, HD), lambda k, core: (0, 0)),
+                pl.BlockSpec((8, 128), lambda k, core: (0, 0)),
+            ],
+            out_specs=(
+                pl.BlockSpec((slots, HD), lambda k, core: (0, 0)),
+                pl.BlockSpec((rows, cols), lambda k, core: (0, 0)),
+            ),
+            scratch_shapes=[pltpu.VMEM((rows, cols), F32)],
         ),
         out_shape=(
             jax.ShapeDtypeStruct((slots, HD), BF16),
             jax.ShapeDtypeStruct((rows, cols), BF16),
         ),
-        scratch_shapes=[pltpu.VMEM((rows, cols), F32)],
         compiler_params=params(),
         cost_estimate=cost(2 * heads * rows * width * cols, 9 * 1024 * 1024),
         name="attend",
-    )(features, project_weight.reshape(heads, width, cols), cotangent, offsets)
-
+    )(
+        core, own1, own2, far1, far2,
+        project_weight.reshape(depth, 2, width, cols), cotangent, offsets,
+    )
+
+    cross1 = lax.ppermute(near1, "mp", sibling)
+    near2, grads = lax.optimization_barrier((near2, grads))
+    cross2 = lax.ppermute(near2, "mp", sibling)
     all_grads = lax.all_gather(grads, "dp", axis=0, axis_index_groups=along_x)
     terms = pl.pallas_call(
         weight_kernel,
         out_shape=jax.ShapeDtypeStruct((Y, 192, cols), BF16),
-        in_specs=[SMEM] + [VMEM] * 3,
+        in_specs=[SMEM] * 2 + [VMEM] * 5,
         out_specs=VMEM,
         compiler_params=params(),
         cost_estimate=cost(2 * 4 * rows * 1536 * cols, 6 * 1024 * 1024),
         name="weight",
-    )(core, own, other, all_grads)
+    )(core, inner, near1, near2, cross1, cross2, all_grads)
     gathered = lax.all_to_all(terms, "dp", 0, 0, axis_index_groups=along_y, tiled=True)
     weight_grad = pl.pallas_call(
         sum_kernel,

time: 203 us -> 180 us (0.89)
  waiting for transfers between devices: 99.7 us -> 43.4 us
  starting transfers between devices: 9.9 us -> 41.2 us
  between operations: 14.1 us -> 0.81 us
  blocking collectives: 60.6 us -> 68.6 us
  Pallas kernels: 13.7 us -> 18.9 us
    all_gather x1 -> x0, waiting for transfers between devices: 67.7 us -> none  [shards(): features = lax.all_gather(compact, 'mp', axis=0)]
    all_gather x0 -> x2, blocking collectives: none -> 56.4 us  [the longest x1 34.9 us: shards(): own1 = lax.all_gather(first, 'mp', axis=0, axis_index_groups=same_core)]
    all_to_all x2 -> x0, blocking collectives: 48.1 us -> none  [the longest x1 26.3 us: shards(): lax.all_to_all(outbound, 'dp', 0, 0, axis_index_groups=along_x, tiled=True)]
    all_to_all x0 -> x3, starting transfers between devices: none -> 18.4 us  [the longest x1 10.5 us: shards(): lax.all_to_all(outgoing.reshape(owners, ROOM, width), 'dp', 0, 0, tiled=T...]
    ppermute x1 -> x4, starting transfers between devices: 3.41 us -> 19.2 us  [the longest x1 8.81 us: shards(): far1 = lax.ppermute(own1, 'mp', sibling)]
    all_to_all x0 -> x3, waiting for transfers between devices: none -> 11.4 us  [the longest x1 11.4 us: shards(): lax.all_to_all(outgoing.reshape(owners, ROOM, width), 'dp', 0, 0, tiled=T...]
    all_to_all x1, starting transfers between devices: 6.46 us -> 3.56 us  [shards(): lax.all_to_all(terms, 'dp', 0, 0, axis_index_groups=along_y, tiled=True)]
    pallas_call x3 -> x4, Pallas kernels: 8.19 us -> 11.1 us  [the longest x1 7.25 us: shards(): pl.pallas_call(attend_kernel, grid_spec=pltpu.PrefetchScalarGridSpec(num_...]
  transfers between devices with their start and end apart: 3 -> 8, of which waited for: 2 -> 2; matrix products, arithmetic and copies ran while one was open for 0% -> 0% of each run, Pallas kernels for 3% -> 6%
where the time goes in v2:
time: 180 us; the launch traced here: 179 us
  blocking collectives  68.6 us (38%)
  waiting for transfers between devices  43.4 us (24%)
  starting transfers between devices  41.2 us (23%)
  Pallas kernels  18.9 us (10%)
  local copies, waits for them, and re-layouts  6.44 us (4%)
    all_gather x1, blocking collectives, shards(): own1 = lax.all_gather(first, 'mp', axis=0, axis_index_groups=same_core)  34.9 us
    all_to_all x1, waiting for transfers between devices, shards(): lax.all_to_all(terms, 'dp', 0, 0, axis_index_groups=along_y, tiled=True)  31.9 us
    all_gather x1, blocking collectives, shards(): own2 = lax.all_gather(second, 'mp', axis=0, axis_index_groups=same_core)  21.5 us
    all_gather x1, blocking collectives, shards(): all_grads = lax.all_gather(grads, 'dp', axis=0, axis_index_groups=along_x)  12.2 us
    all_to_all x1, waiting for transfers between devices, shards(): lax.all_to_all(outgoing.reshape(owners, ROOM, width), 'dp', 0, 0, tiled=T...  11.4 us
    all_to_all x1, starting transfers between devices, shards(): lax.all_to_all(outgoing.reshape(owners, ROOM, width), 'dp', 0, 0, tiled=T...  10.5 us
    ppermute x1, starting transfers between devices, shards(): far1 = lax.ppermute(own1, 'mp', sibling)  8.81 us
    all_to_all x2, starting transfers between devices, over_x(): lax.all_to_all(block, 'dp', 0, 0, axis_index_groups=along_x, tiled=True)  7.89 us
  transfers between devices with their start and end apart: 8, of which 2 were waited for; matrix products, arithmetic and copies ran while one was open for 0% of the time, Pallas kernels for 6%

profile of v2, /device:TPU:1, one launch (start us, length us, event | category | flops | bytes accessed | tf_op | source)
XLA Modules:
  0.0 179.3 jit_solution(17493748407456390614)
XLA Ops:
  0.6 0.8 copy.7.route
  1.4 0.8 copy.8.slot
  2.3 0.0 copy-start.2
  2.3 0.9 copy-done.2
  3.2 2.1 %send.1 = bf16[768,256]{1,0:T(8,128)(2,1)} custom-call(bf16[288,256]{1,0:T(8,128)(2,1)S(1)} %copy-done.2, s32[288,1]{1,0:T(8,128)S(1)} %copy.7.route, s32[288,1]{1,0:T(8,128)S(1)} %copy.8.slot), custom_call_target="tpu_custom_call" | custom-call | tf_op jit(solution)/shard_map/send/pallas_call | solution.py:224
  5.3 10.5 %all-to-all-start = ((bf16[32,24,256]{2,1,0:T(8,128)(2,1)}), bf16[32,24,256]{2,1,0:T(8,128)(2,1)S(1)}, u32[]{:S(2)}, u32[]{:S(2)}) async-start(bf16[32,24,256]{2,1,0:T(8,128)(2,1)} %bitcast.1), calls=%async_computation | async-start | bytes 786432 | tf_op jit(solution)/shard_map/all_to_all | solution.py:232
  15.9 11.4 %all-to-all-done = bf16[32,24,256]{2,1,0:T(8,128)(2,1)S(1)} async-done(((bf16[32,24,256]{2,1,0:T(8,128)(2,1)}), bf16[32,24,256]{2,1,0:T(8,128)(2,1)S(1)}, u32[]{:S(2)}, u32[]{:S(2)}) %all-to-all-start) | async-done | bytes 393248 | tf_op jit(solution)/shard_map/all_to_all | solution.py:232
  27.3 1.2 receive.1
  28.5 34.9 %all-gather = bf16[1728,256]{1,0:T(8,128)(2,1)S(1)} all-gather(bf16[144,256]{1,0:T(8,128)(2,1)S(1)} %get-tuple-element.11), channel_id=2, replica_groups={{0,2,4,6,8,10,12,14,16,18,20,22},{1,3,5,7,9,11,13,15,17,19,21,23},{24,2..., dimensions={0}, use_global_device_ids=true | all-gather | bytes 958464 | tf_op jit(solution)/shard_map/all_gather | solution.py:265
  63.4 8.8 %collective-permute-start = (bf16[12,144,256]{2,1,0:T(8,128)(2,1)S(1)}, bf16[12,144,256]{2,1,0:T(8,128)(2,1)}, u32[]{:S(2)}, u32[]{:S(2)}) collective-permute-start(bf16[12,144,256]{2,1,0:T(8,128)(2,1)S(1)} %bitcast.9), channel_id=1, source_target_pairs={{0,1},{1,0},{2,3},{3,2},{4,5},{5,4},{6,7},{7,6},{8,9},{9,8},{10,11... | collective-permute-start | bytes 2654216 | tf_op jit(solution)/shard_map/ppermute | solution.py:269
  72.3 1.3 split.2
  73.6 3.5 %all-to-all-start.1 = ((bf16[4,144,768]{2,1,0:T(8,128)(2,1)}), bf16[4,144,768]{2,1,0:T(8,128)(2,1)S(1)}, u32[]{:S(2)}, u32[]{:S(2)}) async-start(bf16[4,144,768]{2,1,0:T(8,128)(2,1)} %split.2), calls=%async_computation.1 | async-start | bytes 1769472 | tf_op jit(solution)/shard_map/all_to_all | solution.py:263
  77.1 21.5 %all-gather.1 = bf16[1728,256]{1,0:T(8,128)(2,1)S(1)} all-gather(bf16[144,256]{1,0:T(8,128)(2,1)S(1)} %get-tuple-element.13), channel_id=3, replica_groups={{0,2,4,6,8,10,12,14,16,18,20,22},{1,3,5,7,9,11,13,15,17,19,21,23},{24,2..., dimensions={0}, use_global_device_ids=true | all-gather | bytes 958464 | tf_op jit(solution)/shard_map/all_gather | solution.py:270
  98.5 5.4 %collective-permute-start.1 = (bf16[12,144,256]{2,1,0:T(8,128)(2,1)S(1)}, bf16[12,144,256]{2,1,0:T(8,128)(2,1)}, u32[]{:S(2)}, u32[]{:S(2)}) collective-permute-start(bf16[12,144,256]{2,1,0:T(8,128)(2,1)S(1)} %bitcast.12), channel_id=1, source_target_pairs={{0,1},{1,0},{2,3},{3,2},{4,5},{5,4},{6,7},{7,6},{8,9},{9,8},{10,11... | collective-permute-start | bytes 2654216 | tf_op jit(solution)/shard_map/ppermute | solution.py:273
  104.0 1.3 split.3
  105.3 0.0 all-to-all-done.1.own1
  105.3 4.4 %all-to-all-start.2 = ((bf16[4,144,768]{2,1,0:T(8,128)(2,1)}), bf16[4,144,768]{2,1,0:T(8,128)(2,1)S(1)}, u32[]{:S(2)}, u32[]{:S(2)}) async-start(bf16[4,144,768]{2,1,0:T(8,128)(2,1)} %split.3), calls=%async_computation.2 | async-start | bytes 1769472 | tf_op jit(solution)/shard_map/all_to_all | solution.py:263
  109.7 2.2 %collective-permute-start.2 = (bf16[4,144,768]{2,1,0:T(8,128)(2,1)S(1)}, bf16[4,144,768]{2,1,0:T(8,128)(2,1)}, u32[]{:S(2)}, u32[]{:S(2)}) collective-permute-start(bf16[4,144,768]{2,1,0:T(8,128)(2,1)S(1)} %all-to-all-done.1.own1), channel_id=1, source_target_pairs={{0,1},{1,0},{2,3},{3,2},{4,5},{5,4},{6,7},{7,6},{8,9},{9,8},{10,11... | collective-permute-start | bytes 2654216 | tf_op jit(solution)/shard_map/ppermute | solution.py:306
  111.9 0.0 collective-permute-done.far1
  111.9 0.0 collective-permute-done.1.far2
  111.9 0.0 copy-start
  111.9 2.3 %copy-done = bf16[6144,384]{1,0:T(8,128)(2,1)S(1)} copy-done((bf16[6144,384]{1,0:T(8,128)(2,1)S(1)}, bf16[6144,384]{1,0:T(8,128)(2,1)}, u32[]{:S(2)}) %copy-start) | copy-done | bytes 4718616
  114.3 0.0 copy-start.3
  114.3 0.9 copy-done.3
  115.1 7.3 %attend.1 = (bf16[384,128]{1,0:T(8,128)(2,1)}, bf16[288,384]{1,0:T(8,128)(2,1)S(1)}) custom-call(s32[1]{0:T(128)} %bitcast.core, bf16[12,144,256]{2,1,0:T(8,128)(2,1)S(1)} %bitcast.11, bf16[12,144,256]{2,1,0:T(8,128)(2,1)S(1)} %bitcast.14, bf16[12,144,256]{2,1,0:T(8,128)(2,1)} %collective-permute-done.far1, ...), custom_call_target="tpu_custom_call" | custom-call | flops 1358954496 | bytes 9437184 | tf_op jit(solution)/shard_map/attend/pallas_call | solution.py:277
  122.4 0.0 copy-start.1
  122.4 0.7 copy-done.1
  123.1 0.0 all-to-all-done.2.own2
  123.1 2.8 %collective-permute-start.3 = (bf16[4,144,768]{2,1,0:T(8,128)(2,1)S(1)}, bf16[4,144,768]{2,1,0:T(8,128)(2,1)S(1)}, u32[]{:S(2)}, u32[]{:S(2)}) collective-permute-start(bf16[4,144,768]{2,1,0:T(8,128)(2,1)S(1)} %all-to-all-done.2.own2), channel_id=1, source_target_pairs={{0,1},{1,0},{2,3},{3,2},{4,5},{5,4},{6,7},{7,6},{8,9},{9,8},{10,11... | collective-permute-start | bytes 2654216 | tf_op jit(solution)/shard_map/ppermute | solution.py:308
  125.9 12.2 %all-gather.2 = bf16[1152,384]{1,0:T(8,128)(2,1)S(1)} all-gather(bf16[288,384]{1,0:T(8,128)(2,1)} %copy-done.1), channel_id=4, replica_groups={{0,24,48,72},{96,120,144,168},{192,216,240,264},{288,312,336,360},{384,..., dimensions={0}, use_global_device_ids=true | all-gather | bytes 1105920 | tf_op jit(solution)/shard_map/all_gather | solution.py:309
  138.1 0.0 collective-permute-done.2.far1
  138.1 0.0 collective-permute-done.3.far2
  138.1 4.7 %weight.1 = bf16[8,192,384]{2,1,0:T(8,128)(2,1)} custom-call(s32[1]{0:T(128)} %bitcast.core, s32[1]{0:T(128)} %bitcast.7.inner, bf16[4,144,768]{2,1,0:T(8,128)(2,1)S(1)} %all-to-all-done.1.own1, bf16[4,144,768]{2,1,0:T(8,128)(2,1)S(1)} %all-to-all-done.2.own2, bf16[4,144,768]{2,1,0:T(8,128)(2,1)} %collective-permute-done.2.far1, ...), custom_call_target="tpu_custom_call" | custom-call | flops 1358954496 | bytes 6291456 | tf_op jit(solution)/shard_map/weight/pallas_call | solution.py:310
  142.9 3.6 %all-to-all-start.3 = ((bf16[8,192,384]{2,1,0:T(8,128)(2,1)}), bf16[8,192,384]{2,1,0:T(8,128)(2,1)S(1)}, u32[]{:S(2)}, u32[]{:S(2)}) async-start(bf16[8,192,384]{2,1,0:T(8,128)(2,1)} %weight.1), calls=%async_computation.3 | async-start | bytes 2359296 | tf_op jit(solution)/shard_map/all_to_all | solution.py:319
  146.5 31.9 %all-to-all-done.3.terms = bf16[8,192,384]{2,1,0:T(8,128)(2,1)S(1)} async-done(((bf16[8,192,384]{2,1,0:T(8,128)(2,1)}), bf16[8,192,384]{2,1,0:T(8,128)(2,1)S(1)}, u32[]{:S(2)}, u32[]{:S(2)}) %all-to-all-start.3) | async-done | bytes 1179680 | tf_op jit(solution)/shard_map/all_to_all | solution.py:319
  178.4 0.9 sum.1
Async XLA Ops:
  2.3 0.9 copy-start.2
  5.3 22.0 %all-to-all-start = ((bf16[32,24,256]{2,1,0:T(8,128)(2,1)}), bf16[32,24,256]{2,1,0:T(8,128)(2,1)S(1)}, u32[]{:S(2)}, u32[]{:S(2)}) async-start(bf16[32,24,256]{2,1,0:T(8,128)(2,1)} %bitcast.1), calls=%async_computation | async-start | bytes 786432 | tf_op jit(solution)/shard_map/all_to_all | solution.py:232
  63.4 48.5 %collective-permute-start = (bf16[12,144,256]{2,1,0:T(8,128)(2,1)S(1)}, bf16[12,144,256]{2,1,0:T(8,128)(2,1)}, u32[]{:S(2)}, u32[]{:S(2)}) collective-permute-start(bf16[12,144,256]{2,1,0:T(8,128)(2,1)S(1)} %bitcast.9), channel_id=1, source_target_pairs={{0,1},{1,0},{2,3},{3,2},{4,5},{5,4},{6,7},{7,6},{8,9},{9,8},{10,11... | collective-permute-start | bytes 2654216 | tf_op jit(solution)/shard_map/ppermute | solution.py:269
  73.6 31.8 %all-to-all-start.1 = ((bf16[4,144,768]{2,1,0:T(8,128)(2,1)}), bf16[4,144,768]{2,1,0:T(8,128)(2,1)S(1)}, u32[]{:S(2)}, u32[]{:S(2)}) async-start(bf16[4,144,768]{2,1,0:T(8,128)(2,1)} %split.2), calls=%async_computation.1 | async-start | bytes 1769472 | tf_op jit(solution)/shard_map/all_to_all | solution.py:263
  98.5 13.4 %collective-permute-start.1 = (bf16[12,144,256]{2,1,0:T(8,128)(2,1)S(1)}, bf16[12,144,256]{2,1,0:T(8,128)(2,1)}, u32[]{:S(2)}, u32[]{:S(2)}) collective-permute-start(bf16[12,144,256]{2,1,0:T(8,128)(2,1)S(1)} %bitcast.12), channel_id=1, source_target_pairs={{0,1},{1,0},{2,3},{3,2},{4,5},{5,4},{6,7},{7,6},{8,9},{9,8},{10,11... | collective-permute-start | bytes 2654216 | tf_op jit(solution)/shard_map/ppermute | solution.py:273
  105.3 17.8 %all-to-all-start.2 = ((bf16[4,144,768]{2,1,0:T(8,128)(2,1)}), bf16[4,144,768]{2,1,0:T(8,128)(2,1)S(1)}, u32[]{:S(2)}, u32[]{:S(2)}) async-start(bf16[4,144,768]{2,1,0:T(8,128)(2,1)} %split.3), calls=%async_computation.2 | async-start | bytes 1769472 | tf_op jit(solution)/shard_map/all_to_all | solution.py:263
  109.7 28.4 %collective-permute-start.2 = (bf16[4,144,768]{2,1,0:T(8,128)(2,1)S(1)}, bf16[4,144,768]{2,1,0:T(8,128)(2,1)}, u32[]{:S(2)}, u32[]{:S(2)}) collective-permute-start(bf16[4,144,768]{2,1,0:T(8,128)(2,1)S(1)} %all-to-all-done.1.own1), channel_id=1, source_target_pairs={{0,1},{1,0},{2,3},{3,2},{4,5},{5,4},{6,7},{7,6},{8,9},{9,8},{10,11... | collective-permute-start | bytes 2654216 | tf_op jit(solution)/shard_map/ppermute | solution.py:306
  111.9 2.3 %copy-start = (bf16[6144,384]{1,0:T(8,128)(2,1)S(1)}, bf16[6144,384]{1,0:T(8,128)(2,1)}, u32[]{:S(2)}) copy-start(bf16[6144,384]{1,0:T(8,128)(2,1)} %param.8) | copy-start | bytes 14155780
  114.3 0.9 copy-start.3
  122.4 0.7 copy-start.1
  123.1 15.1 %collective-permute-start.3 = (bf16[4,144,768]{2,1,0:T(8,128)(2,1)S(1)}, bf16[4,144,768]{2,1,0:T(8,128)(2,1)S(1)}, u32[]{:S(2)}, u32[]{:S(2)}) collective-permute-start(bf16[4,144,768]{2,1,0:T(8,128)(2,1)S(1)} %all-to-all-done.2.own2), channel_id=1, source_target_pairs={{0,1},{1,0},{2,3},{3,2},{4,5},{5,4},{6,7},{7,6},{8,9},{9,8},{10,11... | collective-permute-start | bytes 2654216 | tf_op jit(solution)/shard_map/ppermute | solution.py:308
  142.9 35.5 %all-to-all-start.3 = ((bf16[8,192,384]{2,1,0:T(8,128)(2,1)}), bf16[8,192,384]{2,1,0:T(8,128)(2,1)S(1)}, u32[]{:S(2)}, u32[]{:S(2)}) async-start(bf16[8,192,384]{2,1,0:T(8,128)(2,1)} %weight.1), calls=%async_computation.3 | async-start | bytes 2359296 | tf_op jit(solution)/shard_map/all_to_all | solution.py:319

commit v3 on v1

--- a/solution.py
+++ b/solution.py
@@ -10,6 +10,7 @@
 SENT = 18
 ROOM = 24
 X, Y = 4, 8
+ATTEND_VMEM = 40
 F32, BF16, I32 = jnp.float32, jnp.bfloat16, jnp.int32
 
 
@@ -88,11 +89,14 @@
     return image, index - base + CAP * image
 
 
-def attend_kernel(features, weight, cotangent, offsets, attention, grads, total):
+def attend_kernel(
+    where, base, up, down, far, far_up, far_down, weight, cotangent, offsets, attention, grads, total
+):
     step = pl.program_id(0)
-    part = mm(features[0], weight[0])
-    for k in range(1, features.shape[0]):
-        part += mm(features[k], weight[k])
+    core = where[0]
+    part = mm(base[0], weight[0, where[1], core]) + mm(far[0], weight[0, where[1], 1 - core])
+    part += mm(up[0], weight[0, where[2], core]) + mm(far_up[0], weight[0, where[2], 1 - core])
+    part += mm(down[0], weight[0, where[3], core]) + mm(far_down[0], weight[0, where[3], 1 - core])
 
     @pl.when(step == 0)
     def _():
@@ -129,46 +133,42 @@
         grads[:, 2 * HD :] = d_value.astype(BF16)
 
 
-def split_kernel(core, features, out):
-    def tile(t):
-        return features[t // 2, :, (t % 2) * 128 : (t % 2) * 128 + 128]
-
-    row, col = iota((256, 128), 0), iota((256, 128), 1)
-    near = hot(row == jnp.where(col < 64, col, col + 64))
-    far = hot(row == jnp.where(col < 64, col + 64, col + 128))
-    for x, (whole, cut, pick) in enumerate(((0, 1, near), (2, 1, far), (3, 4, near), (5, 4, far))):
-        out[x, :, 0:128] = tile(whole)
-        out[x, :, 128:256] = tile(whole + 6)
-        both = jnp.concatenate([tile(cut), tile(cut + 6)], axis=1)
-        out[x, :, 256:384] = mm(both, pick).astype(BF16)
-
-
-def weight_kernel(core, own, other, grads, out):
+def split_kernel(*refs):
+    out = refs[-1]
+    row, col = iota((256, 512), 0), iota((256, 512), 1)
+    source = ((col >> 4) & 3) * 64 + (col >> 7) * 16 + (col & 15)
+    left = hot((row == source) & ((col & 64) == 0))
+    right = hot((row == source) & ((col & 64) == 64))
+    at = 0
+    for features in refs[:-1]:
+        for m in range(0, features.shape[0], 2):
+            both = (mm(features[m], left) + mm(features[m + 1], right)).astype(BF16)
+            for x in range(X):
+                out[x, :, at : at + 128] = both[:, x * 128 : x * 128 + 128]
+            at += 128
+
+
+def weight_kernel(where, near1, near2, cross1, cross2, grads, out):
     depth = grads.shape[0] * grads.shape[1]
     right = grads[...].reshape(depth, grads.shape[2])
-    for source, side in ((own, core[0]), (other, 1 - core[0])):
-        for a in range(2):
-            left = source[:, :, a * 384 : a * 384 + 384].reshape(depth, 384)
+    core = where[0]
+    for first, second, side in ((near1, near2, core), (cross1, cross2, 1 - core)):
+        for held, at, turn in ((first, 0, where[1]), (second, 0, where[2]), (second, 256, where[3])):
+            left = held[:, :, at : at + 256].reshape(depth, 256)
             term = mm(left, right, 0, 0).astype(BF16)
-            at = side * 4 + a * 2
-            for b in range(2):
-                out[at + b, 0:128] = term[b * 128 : b * 128 + 128]
-                out[at + b, 128:192] = term[256 + b * 64 : 320 + b * 64]
-
-
-def sum_kernel(odd, terms, out):
-    total = terms[0].astype(F32)
-    for k in range(1, terms.shape[0]):
-        total += terms[k].astype(F32)
-
-    @pl.when(odd[0] == 0)
-    def _():
-        out[...] = total
-
-    @pl.when(odd[0] == 1)
-    def _():
-        out[0:64] = total[128:192]
-        out[64:192] = total[0:128]
+            for m in range(4):
+                slice_index = 6 * m + 2 * turn + side
+                rows = pl.ds(pl.multiple_of(slice_index * 64, 64), 64)
+                out[rows, :] = term[m * 64 : m * 64 + 64]
+
+
+def sum_kernel(terms, out):
+    for x in range(X):
+        total = terms[x].astype(F32)
+        for k in range(X + x, terms.shape[0], X):
+            total += terms[k].astype(F32)
+        for v in range(3):
+            out[64 * v + 16 * x : 64 * v + 16 * x + 16] = total[16 * v : 16 * v + 16]
 
 
 def params():
@@ -188,10 +188,10 @@
     rows, width = patches.shape
     slots = cotangent.shape[0]
     cols = project_weight.shape[1]
-    core = (lax.axis_index("mp") % 2).astype(I32).reshape(1)
-    odd = (lax.axis_index("dp") % 2).astype(I32).reshape(1)
+    place = lax.axis_index("mp")
+    turn = (place // 2) % 3
+    where = jnp.stack([place % 2, turn, (turn + 2) % 3, (turn + 1) % 3]).astype(I32)
     along_x = [[y * X + x for x in range(X)] for y in range(Y)]
-    along_y = [[y * X + x for y in range(Y)] for x in range(X)]
 
     outgoing = pl.pallas_call(
         send_kernel,
@@ -214,68 +214,90 @@
         name="receive",
     )(arrived.reshape(owners * ROOM, width))
 
-    features = lax.all_gather(compact, "mp", axis=0)
-
-    part = heads // 4
-    outbound = pl.pallas_call(
-        split_kernel,
+    thirds = [[6 * m + r for m in range(heads // 6)] for r in range(6)]
+
+    def shift(block, by):
+        return lax.ppermute(block, "mp", [(k, (k + by) % heads) for k in range(heads)])
+
+    def swap(block):
+        return lax.ppermute(block, "mp", [(k, k ^ 1) for k in range(heads)])
+
+    def split(*blocks):
+        wide = 64 * sum(block.shape[0] for block in blocks)
+        return pl.pallas_call(
+            split_kernel,
+            out_shape=jax.ShapeDtypeStruct((X, rows, wide), BF16),
+            in_specs=[VMEM] * len(blocks),
+            out_specs=VMEM,
+            compiler_params=params(),
+            cost_estimate=cost(0, 4 * rows * wide * 4),
+            name="split",
+        )(*blocks)
+
+    def over_x(block):
+        return lax.all_to_all(block, "dp", 0, 0, axis_index_groups=along_x, tiled=True)
+
+    base = lax.all_gather(compact, "mp", axis=0, axis_index_groups=thirds)
+    up, down, far = shift(base, 2), shift(base, -2), swap(base)
+    near1 = over_x(split(base))
+    far_up, far_down = swap(up), swap(down)
+    near2 = over_x(split(up, down))
+    near1, far_down = lax.optimization_barrier((near1, far_down))
+    cross1 = swap(near1)
+
+    steps = heads // 6
+    block = pl.BlockSpec((1, rows, width), lambda k, where: (k, 0, 0))
+    attention, grads = pl.pallas_call(
+        attend_kernel,
         grid_spec=pltpu.PrefetchScalarGridSpec(
             num_scalar_prefetch=1,
-            grid=(2,),
-            in_specs=[pl.BlockSpec((part, rows, width), lambda a, core: (core[0] * 2 + a, 0, 0))],
-            out_specs=pl.BlockSpec((X, rows, 384), lambda a, core: (0, 0, a)),
-        ),
-        out_shape=jax.ShapeDtypeStruct((X, rows, 768), BF16),
-        compiler_params=params(),
-        cost_estimate=cost(0, 4 * rows * 768 * 4),
-        name="split",
-    )(core, features)
-    own = lax.all_to_all(outbound, "dp", 0, 0, axis_index_groups=along_x, tiled=True)
-    other = lax.ppermute(own, "mp", [(k, k ^ 1) for k in range(heads)])
-
-    step = 4
-    attention, grads = pl.pallas_call(
-        attend_kernel,
-        grid=(heads // step,),
-        in_specs=[
-            pl.BlockSpec((step, rows, width), lambda k: (k, 0, 0)),
-            pl.BlockSpec((step, width, cols), lambda k: (k, 0, 0)),
-            pl.BlockSpec((slots, HD), lambda k: (0, 0)),
-            pl.BlockSpec((8, 128), lambda k: (0, 0)),
-        ],
-        out_specs=(
-            pl.BlockSpec((slots, HD), lambda k: (0, 0)),
-            pl.BlockSpec((rows, cols), lambda k: (0, 0)),
+            grid=(steps,),
+            in_specs=[block] * 6
+            + [
+                pl.BlockSpec((1, 3, 2, width, cols), lambda k, where: (k, 0, 0, 0, 0)),
+                pl.BlockSpec((slots, HD), lambda k, where: (0, 0)),
+                pl.BlockSpec((8, 128), lambda k, where: (0, 0)),
+            ],
+            out_specs=(
+                pl.BlockSpec((slots, HD), lambda k, where: (0, 0)),
+                pl.BlockSpec((rows, cols), lambda k, where: (0, 0)),
+            ),
+            scratch_shapes=[pltpu.VMEM((rows, cols), F32)],
         ),
         out_shape=(
             jax.ShapeDtypeStruct((slots, HD), BF16),
             jax.ShapeDtypeStruct((rows, cols), BF16),
         ),
-        scratch_shapes=[pltpu.VMEM((rows, cols), F32)],
-        compiler_params=params(),
+        compiler_params=pltpu.CompilerParams(vmem_limit_bytes=ATTEND_VMEM * 1024 * 1024),
         cost_estimate=cost(2 * heads * rows * width * cols, 9 * 1024 * 1024),
         name="attend",
-    )(features, project_weight.reshape(heads, width, cols), cotangent, offsets)
-
+    )(
+        where, base, up, down, far, far_up, far_down,
+        project_weight.reshape(steps, 3, 2, width, cols), cotangent, offsets,
+    )
+
+    grads, cross1 = lax.optimization_barrier((grads, cross1))
     all_grads = lax.all_gather(grads, "dp", axis=0, axis_index_groups=along_x)
+    near2, all_grads = lax.optimization_barrier((near2, all_grads))
+    cross2 = swap(near2)
     terms = pl.pallas_call(
         weight_kernel,
-        out_shape=jax.ShapeDtypeStruct((Y, 192, cols), BF16),
-        in_specs=[SMEM] + [VMEM] * 3,
+        out_shape=jax.ShapeDtypeStruct((1536, cols), BF16),
+        in_specs=[SMEM] + [VMEM] * 5,
         out_specs=VMEM,
         compiler_params=params(),
         cost_estimate=cost(2 * 4 * rows * 1536 * cols, 6 * 1024 * 1024),
         name="weight",
-    )(core, own, other, all_grads)
-    gathered = lax.all_to_all(terms, "dp", 0, 0, axis_index_groups=along_y, tiled=True)
+    )(where, near1, near2, cross1, cross2, all_grads)
+    gathered = lax.all_to_all(terms.reshape(owners, 48, cols), "dp", 0, 0, tiled=True)
     weight_grad = pl.pallas_call(
         sum_kernel,
         out_shape=jax.ShapeDtypeStruct((192, cols), F32),
-        in_specs=[SMEM, VMEM],
+        in_specs=[VMEM],
         out_specs=VMEM,
         compiler_params=params(),
         name="sum",
-    )(odd, gathered)
+    )(gathered)
     return attention, weight_grad
 
 

time: 203 us -> 178 us (0.88)
  waiting for transfers between devices: 99.7 us -> 15.7 us
  blocking collectives: 60.6 us -> 103 us
  starting transfers between devices: 9.9 us -> 33.6 us
  between operations: 14.1 us -> 0.85 us
  Pallas kernels: 13.7 us -> 17.8 us
    all_gather x1 -> x0, waiting for transfers between devices: 67.7 us -> none  [shards(): features = lax.all_gather(compact, 'mp', axis=0)]
    all_gather x0 -> x1, blocking collectives: none -> 29.2 us  [shards(): base = lax.all_gather(compact, 'mp', axis=0, axis_index_groups=thirds)]
    all_to_all x1 -> x2, waiting for transfers between devices: 32 us -> 5.68 us  [over_x(): lax.all_to_all(block, 'dp', 0, 0, axis_index_groups=along_x, tiled=True)]
    ppermute x1 -> x7, starting transfers between devices: 3.41 us -> 25.2 us  [the longest x5 17.4 us: swap(): return lax.ppermute(block, 'mp', [(k, k ^ 1) for k in range(heads)])]
    all_to_all x1, blocking collectives: 26.3 us -> 37.5 us  [shards(): lax.all_to_all(terms.reshape(owners, 48, cols), 'dp', 0, 0, tiled=True)]
    ppermute x1 -> x7, waiting for transfers between devices: 0.01 us -> 10 us  [the longest x2 7.54 us: shift(): lax.ppermute(block, 'mp', [(k, (k + by) % heads) for k in range(heads)])]
    pallas_call x3 -> x4, Pallas kernels: 9.51 us -> 14.3 us  [the longest x1 6.87 us: shards(): pl.pallas_call(attend_kernel, grid_spec=pltpu.PrefetchScalarGridSpec(num_...]
    all_gather x1, blocking collectives: 12.5 us -> 15 us  [shards(): all_grads = lax.all_gather(grads, 'dp', axis=0, axis_index_groups=along_x)]
  transfers between devices with their start and end apart: 3 -> 9, of which waited for: 2 -> 3; matrix products, arithmetic and copies ran while one was open for 0% -> 0% of each run, Pallas kernels for 3% -> 6%
where the time goes in v3:
time: 178 us; the launch traced here: 177 us
  blocking collectives  103 us (58%)
  starting transfers between devices  33.6 us (19%)
  Pallas kernels  17.8 us (10%)
  waiting for transfers between devices  15.7 us (9%)
  local copies, waits for them, and re-layouts  5.94 us (3%)
    all_to_all x1, blocking collectives, shards(): lax.all_to_all(terms.reshape(owners, 48, cols), 'dp', 0, 0, tiled=True)  37.5 us
    all_gather x1, blocking collectives, shards(): base = lax.all_gather(compact, 'mp', axis=0, axis_index_groups=thirds)  29.2 us
    all_to_all x1, blocking collectives, shards(): lax.all_to_all(outgoing.reshape(owners, ROOM, width), 'dp', 0, 0, tiled=T...  21.8 us
    ppermute x5, starting transfers between devices, swap(): return lax.ppermute(block, 'mp', [(k, k ^ 1) for k in range(heads)])  17.4 us
    all_gather x1, blocking collectives, shards(): all_grads = lax.all_gather(grads, 'dp', axis=0, axis_index_groups=along_x)  15 us
    all_to_all x2, starting transfers between devices, over_x(): lax.all_to_all(block, 'dp', 0, 0, axis_index_groups=along_x, tiled=True)  8.33 us
    ppermute x2, starting transfers between devices, shift(): lax.ppermute(block, 'mp', [(k, (k + by) % heads) for k in range(heads)])  7.82 us
    ppermute x2, waiting for transfers between devices, shift(): lax.ppermute(block, 'mp', [(k, (k + by) % heads) for k in range(heads)])  7.54 us
  transfers between devices with their start and end apart: 9, of which 3 were waited for; matrix products, arithmetic and copies ran while one was open for 0% of the time, Pallas kernels for 6%

profile of v3, /device:TPU:1, one launch (start us, length us, event | category | flops | bytes accessed | tf_op | source)
XLA Modules:
  0.0 177.3 jit_solution(16384325739406370395)
XLA Ops:
  0.6 0.8 copy.7.route
  1.4 0.8 copy.8.slot
  2.3 0.0 copy-start.3
  2.3 0.9 copy-done.3
  3.2 1.4 send.1
  4.6 21.8 %all_to_all.20 = bf16[32,24,256]{2,1,0:T(8,128)(2,1)S(1)} all-to-all(bf16[32,24,256]{2,1,0:T(8,128)(2,1)S(1)} %bitcast.19), channel_id=1, replica_groups=mesh['dp'=32,'mp'=24] {'dp'}, dimensions={0} | all-to-all | bytes 786432 | tf_op jit(solution)/shard_map/all_to_all | solution.py:204
  26.3 1.2 receive.1
  27.6 29.2 %all-gather = bf16[1152,256]{1,0:T(8,128)(2,1)S(1)} all-gather(bf16[288,256]{1,0:T(8,128)(2,1)S(1)} %get-tuple-element.12), channel_id=2, replica_groups={{0,6,12,18},{1,7,13,19},{2,8,14,20},{3,9,15,21},{4,10,16,22},{5,11,17,2..., dimensions={0}, use_global_device_ids=true | all-gather | bytes 737280 | tf_op jit(solution)/shard_map/all_gather | solution.py:240
  56.8 5.9 %collective-permute-start.1 = (bf16[4,288,256]{2,1,0:T(8,128)(2,1)S(1)}, bf16[4,288,256]{2,1,0:T(8,128)(2,1)S(1)}, u32[]{:S(2)}, u32[]{:S(2)}) collective-permute-start(bf16[4,288,256]{2,1,0:T(8,128)(2,1)S(1)} %bitcast.10), channel_id=1, source_target_pairs={{0,22},{1,23},{2,0},{3,1},{4,2},{5,3},{6,4},{7,5},{8,6},{9,7},{10,... | collective-permute-start | bytes 1769480 | tf_op jit(solution)/shard_map/ppermute | solution.py:220
  62.7 1.9 %collective-permute-start = (bf16[4,288,256]{2,1,0:T(8,128)(2,1)S(1)}, bf16[4,288,256]{2,1,0:T(8,128)(2,1)}, u32[]{:S(2)}, u32[]{:S(2)}) collective-permute-start(bf16[4,288,256]{2,1,0:T(8,128)(2,1)S(1)} %bitcast.11), channel_id=1, source_target_pairs={{0,2},{1,3},{2,4},{3,5},{4,6},{5,7},{6,8},{7,9},{8,10},{9,11},{10,... | collective-permute-start | bytes 1769480 | tf_op jit(solution)/shard_map/ppermute | solution.py:220
  64.6 7.5 %collective-permute-done.1.down.refs_1_ = bf16[4,288,256]{2,1,0:T(8,128)(2,1)S(1)} collective-permute-done((bf16[4,288,256]{2,1,0:T(8,128)(2,1)S(1)}, bf16[4,288,256]{2,1,0:T(8,128)(2,1)S(1)}, u32[]{:S(2)}, u32[]{:S(2)}) %collective-permute-start.1) | collective-permute-done | bytes 589856 | tf_op jit(solution)/shard_map/ppermute | solution.py:220
  72.1 6.6 %collective-permute-start.4 = (bf16[4,288,256]{2,1,0:T(8,128)(2,1)S(1)}, bf16[4,288,256]{2,1,0:T(8,128)(2,1)S(1)}, u32[]{:S(2)}, u32[]{:S(2)}) collective-permute-start(bf16[4,288,256]{2,1,0:T(8,128)(2,1)S(1)} %collective-permute-done.1.down.refs_1_), channel_id=1, source_target_pairs={{0,1},{1,0},{2,3},{3,2},{4,5},{5,4},{6,7},{7,6},{8,9},{9,8},{10,11... | collective-permute-start | bytes 1769480 | tf_op jit(solution)/shard_map/ppermute | solution.py:223
  78.7 1.3 split.2
  80.0 4.7 %all-to-all-start.1 = ((bf16[4,288,256]{2,1,0:T(8,128)(2,1)}), bf16[4,288,256]{2,1,0:T(8,128)(2,1)S(1)}, u32[]{:S(2)}, u32[]{:S(2)}) async-start(bf16[4,288,256]{2,1,0:T(8,128)(2,1)} %split.2), calls=%async_computation.1 | async-start | bytes 1179648 | tf_op jit(solution)/shard_map/all_to_all | solution.py:238
  84.7 2.2 %collective-permute-start.2 = (bf16[4,288,256]{2,1,0:T(8,128)(2,1)S(1)}, bf16[4,288,256]{2,1,0:T(8,128)(2,1)}, u32[]{:S(2)}, u32[]{:S(2)}) collective-permute-start(bf16[4,288,256]{2,1,0:T(8,128)(2,1)S(1)} %bitcast.13), channel_id=1, source_target_pairs={{0,1},{1,0},{2,3},{3,2},{4,5},{5,4},{6,7},{7,6},{8,9},{9,8},{10,11... | collective-permute-start | bytes 1769480 | tf_op jit(solution)/shard_map/ppermute | solution.py:223
  86.9 0.0 collective-permute-done.up.refs_0_
  86.9 2.1 %collective-permute-start.3 = (bf16[4,288,256]{2,1,0:T(8,128)(2,1)}, bf16[4,288,256]{2,1,0:T(8,128)(2,1)}, u32[]{:S(2)}, u32[]{:S(2)}) collective-permute-start(bf16[4,288,256]{2,1,0:T(8,128)(2,1)} %collective-permute-done.up.refs_0_), channel_id=1, source_target_pairs={{0,1},{1,0},{2,3},{3,2},{4,5},{5,4},{6,7},{7,6},{8,9},{9,8},{10,11... | collective-permute-start | bytes 1769480 | tf_op jit(solution)/shard_map/ppermute | solution.py:223
  89.1 5.7 %all-to-all-done.1.near1 = bf16[4,288,256]{2,1,0:T(8,128)(2,1)S(1)} async-done(((bf16[4,288,256]{2,1,0:T(8,128)(2,1)}), bf16[4,288,256]{2,1,0:T(8,128)(2,1)S(1)}, u32[]{:S(2)}, u32[]{:S(2)}) %all-to-all-start.1) | async-done | bytes 589856 | tf_op jit(solution)/shard_map/all_to_all | solution.py:238
  94.7 0.0 collective-permute-done.4.far_down
  94.7 0.0 copy-start.1
  94.7 3.0 %collective-permute-start.5 = (bf16[4,288,256]{2,1,0:T(8,128)(2,1)S(1)}, bf16[4,288,256]{2,1,0:T(8,128)(2,1)}, u32[]{:S(2)}, u32[]{:S(2)}) collective-permute-start(bf16[4,288,256]{2,1,0:T(8,128)(2,1)S(1)} %all-to-all-done.1.near1), channel_id=1, source_target_pairs={{0,1},{1,0},{2,3},{3,2},{4,5},{5,4},{6,7},{7,6},{8,9},{9,8},{10,11... | collective-permute-start | bytes 1769480 | tf_op jit(solution)/shard_map/ppermute | solution.py:223
  97.8 2.9 %split.3 = bf16[4,288,512]{2,1,0:T(8,128)(2,1)} custom-call(bf16[4,288,256]{2,1,0:T(8,128)(2,1)} %collective-permute-done.up.refs_0_, bf16[4,288,256]{2,1,0:T(8,128)(2,1)S(1)} %collective-permute-done.1.down.refs_1_), custom_call_target="tpu_custom_call" | custom-call | bytes 2359296 | tf_op jit(solution)/shard_map/split/pallas_call | solution.py:227
  100.7 0.0 copy-start.4
  100.7 0.0 copy-done.1
  100.7 3.7 %all-to-all-start.2 = ((bf16[4,288,512]{2,1,0:T(8,128)(2,1)}), bf16[4,288,512]{2,1,0:T(8,128)(2,1)S(1)}, u32[]{:S(2)}, u32[]{:S(2)}) async-start(bf16[4,288,512]{2,1,0:T(8,128)(2,1)} %split.3), calls=%async_computation.2 | async-start | bytes 2359296 | tf_op jit(solution)/shard_map/all_to_all | solution.py:238
  104.4 0.1 pad_add_fusion.where
  104.5 0.0 collective-permute-done.2.far
  104.5 0.0 collective-permute-done.3.far_up
  104.5 0.0 copy-done.4
  104.5 0.0 copy-start
  104.5 2.3 %copy-done = bf16[6144,384]{1,0:T(8,128)(2,1)S(1)} copy-done((bf16[6144,384]{1,0:T(8,128)(2,1)S(1)}, bf16[6144,384]{1,0:T(8,128)(2,1)}, u32[]{:S(2)}) %copy-start) | copy-done | bytes 4718616
  106.9 0.0 copy-start.2
  106.9 1.1 copy-done.2
  107.9 6.9 %attend.1 = (bf16[384,128]{1,0:T(8,128)(2,1)}, bf16[288,384]{1,0:T(8,128)(2,1)S(1)}) custom-call(s32[4]{0:T(128)S(1)} %pad_add_fusion.where, bf16[4,288,256]{2,1,0:T(8,128)(2,1)S(1)} %bitcast.14, bf16[4,288,256]{2,1,0:T(8,128)(2,1)} %collective-permute-done.up.refs_0_, bf16[4,288,256]{2,1,0:T(8,128)(2,1)S(1)} %collective-permute-done.1.down.refs_1_, ...), custom_call_target="tpu_custom_call" | custom-call | flops 1358954496 | bytes 9437184 | tf_op jit(solution)/shard_map/attend/pallas_call | solution.py:250
  114.8 0.0 collective-permute-done.5.cross1
  114.8 15.0 %all-gather.1 = bf16[1152,384]{1,0:T(8,128)(2,1)S(1)} all-gather(bf16[288,384]{1,0:T(8,128)(2,1)S(1)} %get-tuple-element.18), channel_id=3, replica_groups={{0,24,48,72},{96,120,144,168},{192,216,240,264},{288,312,336,360},{384,..., dimensions={0}, use_global_device_ids=true | all-gather | bytes 1105920 | tf_op jit(solution)/shard_map/all_gather | solution.py:280
  129.8 0.0 all-to-all-done.2.near2
  129.8 3.5 %collective-permute-start.6 = (bf16[4,288,512]{2,1,0:T(8,128)(2,1)S(1)}, bf16[4,288,512]{2,1,0:T(8,128)(2,1)S(1)}, u32[]{:S(2)}, u32[]{:S(2)}) collective-permute-start(bf16[4,288,512]{2,1,0:T(8,128)(2,1)S(1)} %all-to-all-done.2.near2), channel_id=1, source_target_pairs={{0,1},{1,0},{2,3},{3,2},{4,5},{5,4},{6,7},{7,6},{8,9},{9,8},{10,11... | collective-permute-start | bytes 3538952 | tf_op jit(solution)/shard_map/ppermute | solution.py:223
  133.3 2.5 %collective-permute-done.6.cross2 = bf16[4,288,512]{2,1,0:T(8,128)(2,1)S(1)} collective-permute-done((bf16[4,288,512]{2,1,0:T(8,128)(2,1)S(1)}, bf16[4,288,512]{2,1,0:T(8,128)(2,1)S(1)}, u32[]{:S(2)}, u32[]{:S(2)}) %collective-permute-start.6) | collective-permute-done | bytes 1179680 | tf_op jit(solution)/shard_map/ppermute | solution.py:223
  135.8 3.2 %weight.1 = bf16[1536,384]{1,0:T(8,128)(2,1)S(1)} custom-call(s32[4]{0:T(128)S(1)} %pad_add_fusion.where, bf16[4,288,256]{2,1,0:T(8,128)(2,1)S(1)} %all-to-all-done.1.near1, bf16[4,288,512]{2,1,0:T(8,128)(2,1)S(1)} %all-to-all-done.2.near2, bf16[4,288,256]{2,1,0:T(8,128)(2,1)} %collective-permute-done.5.cross1, ...), custom_call_target="tpu_custom_call" | custom-call | flops 1358954496 | bytes 6291456 | tf_op jit(solution)/shard_map/weight/pallas_call | solution.py:283
  139.0 37.5 %all_to_all.21.terms = bf16[32,48,384]{2,1,0:T(8,128)(2,1)S(1)} all-to-all(bf16[32,48,384]{2,1,0:T(8,128)(2,1)S(1)} %bitcast.16), channel_id=1, replica_groups=mesh['dp'=32,'mp'=24] {'dp'}, dimensions={0} | all-to-all | bytes 2359296 | tf_op jit(solution)/shard_map/all_to_all | solution.py:292
  176.5 0.9 sum.1
Async XLA Ops:
  2.3 0.9 copy-start.3
  56.8 15.4 %collective-permute-start.1 = (bf16[4,288,256]{2,1,0:T(8,128)(2,1)S(1)}, bf16[4,288,256]{2,1,0:T(8,128)(2,1)S(1)}, u32[]{:S(2)}, u32[]{:S(2)}) collective-permute-start(bf16[4,288,256]{2,1,0:T(8,128)(2,1)S(1)} %bitcast.10), channel_id=1, source_target_pairs={{0,22},{1,23},{2,0},{3,1},{4,2},{5,3},{6,4},{7,5},{8,6},{9,7},{10,... | collective-permute-start | bytes 1769480 | tf_op jit(solution)/shard_map/ppermute | solution.py:220
  62.7 24.3 %collective-permute-start = (bf16[4,288,256]{2,1,0:T(8,128)(2,1)S(1)}, bf16[4,288,256]{2,1,0:T(8,128)(2,1)}, u32[]{:S(2)}, u32[]{:S(2)}) collective-permute-start(bf16[4,288,256]{2,1,0:T(8,128)(2,1)S(1)} %bitcast.11), channel_id=1, source_target_pairs={{0,2},{1,3},{2,4},{3,5},{4,6},{5,7},{6,8},{7,9},{8,10},{9,11},{10,... | collective-permute-start | bytes 1769480 | tf_op jit(solution)/shard_map/ppermute | solution.py:220
  72.1 22.6 %collective-permute-start.4 = (bf16[4,288,256]{2,1,0:T(8,128)(2,1)S(1)}, bf16[4,288,256]{2,1,0:T(8,128)(2,1)S(1)}, u32[]{:S(2)}, u32[]{:S(2)}) collective-permute-start(bf16[4,288,256]{2,1,0:T(8,128)(2,1)S(1)} %collective-permute-done.1.down.refs_1_), channel_id=1, source_target_pairs={{0,1},{1,0},{2,3},{3,2},{4,5},{5,4},{6,7},{7,6},{8,9},{9,8},{10,11... | collective-permute-start | bytes 1769480 | tf_op jit(solution)/shard_map/ppermute | solution.py:223
  80.0 14.7 %all-to-all-start.1 = ((bf16[4,288,256]{2,1,0:T(8,128)(2,1)}), bf16[4,288,256]{2,1,0:T(8,128)(2,1)S(1)}, u32[]{:S(2)}, u32[]{:S(2)}) async-start(bf16[4,288,256]{2,1,0:T(8,128)(2,1)} %split.2), calls=%async_computation.1 | async-start | bytes 1179648 | tf_op jit(solution)/shard_map/all_to_all | solution.py:238
  84.7 19.8 %collective-permute-start.2 = (bf16[4,288,256]{2,1,0:T(8,128)(2,1)S(1)}, bf16[4,288,256]{2,1,0:T(8,128)(2,1)}, u32[]{:S(2)}, u32[]{:S(2)}) collective-permute-start(bf16[4,288,256]{2,1,0:T(8,128)(2,1)S(1)} %bitcast.13), channel_id=1, source_target_pairs={{0,1},{1,0},{2,3},{3,2},{4,5},{5,4},{6,7},{7,6},{8,9},{9,8},{10,11... | collective-permute-start | bytes 1769480 | tf_op jit(solution)/shard_map/ppermute | solution.py:223
  86.9 17.6 %collective-permute-start.3 = (bf16[4,288,256]{2,1,0:T(8,128)(2,1)}, bf16[4,288,256]{2,1,0:T(8,128)(2,1)}, u32[]{:S(2)}, u32[]{:S(2)}) collective-permute-start(bf16[4,288,256]{2,1,0:T(8,128)(2,1)} %collective-permute-done.up.refs_0_), channel_id=1, source_target_pairs={{0,1},{1,0},{2,3},{3,2},{4,5},{5,4},{6,7},{7,6},{8,9},{9,8},{10,11... | collective-permute-start | bytes 1769480 | tf_op jit(solution)/shard_map/ppermute | solution.py:223
  94.7 5.9 %copy-start.1 = (bf16[4,288,256]{2,1,0:T(8,128)(2,1)}, bf16[4,288,256]{2,1,0:T(8,128)(2,1)S(1)}, u32[]{:S(2)}) copy-start(bf16[4,288,256]{2,1,0:T(8,128)(2,1)S(1)} %collective-permute-done.4.far_down) | copy-start | bytes 1769476
  94.7 20.0 %collective-permute-start.5 = (bf16[4,288,256]{2,1,0:T(8,128)(2,1)S(1)}, bf16[4,288,256]{2,1,0:T(8,128)(2,1)}, u32[]{:S(2)}, u32[]{:S(2)}) collective-permute-start(bf16[4,288,256]{2,1,0:T(8,128)(2,1)S(1)} %all-to-all-done.1.near1), channel_id=1, source_target_pairs={{0,1},{1,0},{2,3},{3,2},{4,5},{5,4},{6,7},{7,6},{8,9},{9,8},{10,11... | collective-permute-start | bytes 1769480 | tf_op jit(solution)/shard_map/ppermute | solution.py:223
  100.7 3.8 %copy-start.4 = (bf16[384,128]{1,0:T(8,128)(2,1)S(1)}, bf16[384,128]{1,0:T(8,128)(2,1)}, u32[]{:S(2)}) copy-start(bf16[384,128]{1,0:T(8,128)(2,1)} %cotangent.1) | copy-start | bytes 294916
  100.7 29.1 %all-to-all-start.2 = ((bf16[4,288,512]{2,1,0:T(8,128)(2,1)}), bf16[4,288,512]{2,1,0:T(8,128)(2,1)S(1)}, u32[]{:S(2)}, u32[]{:S(2)}) async-start(bf16[4,288,512]{2,1,0:T(8,128)(2,1)} %split.3), calls=%async_computation.2 | async-start | bytes 2359296 | tf_op jit(solution)/shard_map/all_to_all | solution.py:238
  104.5 2.3 %copy-start = (bf16[6144,384]{1,0:T(8,128)(2,1)S(1)}, bf16[6144,384]{1,0:T(8,128)(2,1)}, u32[]{:S(2)}) copy-start(bf16[6144,384]{1,0:T(8,128)(2,1)} %param.8) | copy-start | bytes 14155780
  106.9 1.1 copy-start.2
  129.8 6.0 %collective-permute-start.6 = (bf16[4,288,512]{2,1,0:T(8,128)(2,1)S(1)}, bf16[4,288,512]{2,1,0:T(8,128)(2,1)S(1)}, u32[]{:S(2)}, u32[]{:S(2)}) collective-permute-start(bf16[4,288,512]{2,1,0:T(8,128)(2,1)S(1)} %all-to-all-done.2.near2), channel_id=1, source_target_pairs={{0,1},{1,0},{2,3},{3,2},{4,5},{5,4},{6,7},{7,6},{8,9},{9,8},{10,11... | collective-permute-start | bytes 3538952 | tf_op jit(solution)/shard_map/ppermute | solution.py:223

commit v4 on v3

--- a/solution.py
+++ b/solution.py
@@ -10,7 +10,7 @@
 SENT = 18
 ROOM = 24
 X, Y = 4, 8
-ATTEND_VMEM = 40
+ATTEND_VMEM = 48
 F32, BF16, I32 = jnp.float32, jnp.bfloat16, jnp.int32
 
 
@@ -133,42 +133,61 @@
         grads[:, 2 * HD :] = d_value.astype(BF16)
 
 
-def split_kernel(*refs):
-    out = refs[-1]
-    row, col = iota((256, 512), 0), iota((256, 512), 1)
-    source = ((col >> 4) & 3) * 64 + (col >> 7) * 16 + (col & 15)
-    left = hot((row == source) & ((col & 64) == 0))
-    right = hot((row == source) & ((col & 64) == 64))
-    at = 0
-    for features in refs[:-1]:
-        for m in range(0, features.shape[0], 2):
-            both = (mm(features[m], left) + mm(features[m + 1], right)).astype(BF16)
-            for x in range(X):
-                out[x, :, at : at + 128] = both[:, x * 128 : x * 128 + 128]
-            at += 128
-
-
-def weight_kernel(where, near1, near2, cross1, cross2, grads, out):
+PICKS = (((0, 1), (4, 1), (5, 2), (3, 2)), ((2, 3), (0, 3), (1, 4), (5, 4)))
+
+
+def split_kernel(where, base, up, down, out):
+    row, col = iota((256, 128), 0), iota((256, 128), 1)
+    low = hot(row == jnp.where(col < 64, col, col + 64))
+    high = hot(row == jnp.where(col < 64, col + 64, col + 128))
+
+    def spread(picks, held):
+        def tile(group, t):
+            return held[t // 2][group, :, (t % 2) * 128 : (t % 2) * 128 + 128]
+
+        for x, (whole, cut) in enumerate(picks):
+            for a in range(2):
+                at = a * 384
+                out[x, :, at : at + 128] = tile(2 * a, whole)
+                out[x, :, at + 128 : at + 256] = tile(2 * a + 1, whole)
+                both = jnp.concatenate([tile(2 * a, cut), tile(2 * a + 1, cut)], axis=1)
+                out[x, :, at + 256 : at + 384] = mm(both, (low, high)[x % 2]).astype(BF16)
+
+    for side, picks in enumerate(PICKS):
+        for turn, held in enumerate(((base, down, up), (up, base, down), (down, up, base))):
+
+            @pl.when((where[0] == side) & (where[1] == turn))
+            def _(picks=picks, held=held):
+                spread(picks, held)
+
+
+def weight_kernel(where, near, cross, grads, out):
     depth = grads.shape[0] * grads.shape[1]
     right = grads[...].reshape(depth, grads.shape[2])
-    core = where[0]
-    for first, second, side in ((near1, near2, core), (cross1, cross2, 1 - core)):
-        for held, at, turn in ((first, 0, where[1]), (second, 0, where[2]), (second, 256, where[3])):
-            left = held[:, :, at : at + 256].reshape(depth, 256)
+    for held, side in ((near, where[0]), (cross, 1 - where[0])):
+        whole_side = jnp.where(where[4] == 1, 1 - side, side)
+        for a in range(2):
+            left = held[:, :, a * 384 : a * 384 + 384].reshape(depth, 384)
             term = mm(left, right, 0, 0).astype(BF16)
-            for m in range(4):
-                slice_index = 6 * m + 2 * turn + side
-                rows = pl.ds(pl.multiple_of(slice_index * 64, 64), 64)
-                out[rows, :] = term[m * 64 : m * 64 + 64]
-
-
-def sum_kernel(terms, out):
-    for x in range(X):
-        total = terms[x].astype(F32)
-        for k in range(X + x, terms.shape[0], X):
-            total += terms[k].astype(F32)
-        for v in range(3):
-            out[64 * v + 16 * x : 64 * v + 16 * x + 16] = total[16 * v : 16 * v + 16]
+            for b in range(2):
+                group = 2 * a + b
+                out[2 * group + whole_side, 0:128] = term[b * 128 : b * 128 + 128]
+                out[2 * group + side, 128:192] = term[256 + b * 64 : 320 + b * 64]
+
+
+def sum_kernel(where, terms, out):
+    total = terms[0].astype(F32)
+    for k in range(1, terms.shape[0]):
+        total += terms[k].astype(F32)
+
+    @pl.when(where[5] == 0)
+    def _():
+        out[...] = total
+
+    @pl.when(where[5] == 1)
+    def _():
+        out[0:64] = total[128:192]
+        out[64:192] = total[0:128]
 
 
 def params():
@@ -190,8 +209,12 @@
     cols = project_weight.shape[1]
     place = lax.axis_index("mp")
     turn = (place // 2) % 3
-    where = jnp.stack([place % 2, turn, (turn + 2) % 3, (turn + 1) % 3]).astype(I32)
+    x_index = lax.axis_index("dp") % X
+    inner = (x_index == 1) | (x_index == 2)
+    where = [place % 2, turn, (turn + 2) % 3, (turn + 1) % 3, inner, x_index % 2]
+    where = jnp.stack([value.astype(I32) for value in where])
     along_x = [[y * X + x for x in range(X)] for y in range(Y)]
+    along_y = [[y * X + x for y in range(Y)] for x in range(X)]
 
     outgoing = pl.pallas_call(
         send_kernel,
@@ -222,28 +245,20 @@
     def swap(block):
         return lax.ppermute(block, "mp", [(k, k ^ 1) for k in range(heads)])
 
-    def split(*blocks):
-        wide = 64 * sum(block.shape[0] for block in blocks)
-        return pl.pallas_call(
-            split_kernel,
-            out_shape=jax.ShapeDtypeStruct((X, rows, wide), BF16),
-            in_specs=[VMEM] * len(blocks),
-            out_specs=VMEM,
-            compiler_params=params(),
-            cost_estimate=cost(0, 4 * rows * wide * 4),
-            name="split",
-        )(*blocks)
-
-    def over_x(block):
-        return lax.all_to_all(block, "dp", 0, 0, axis_index_groups=along_x, tiled=True)
-
     base = lax.all_gather(compact, "mp", axis=0, axis_index_groups=thirds)
     up, down, far = shift(base, 2), shift(base, -2), swap(base)
-    near1 = over_x(split(base))
+    up, down, far = lax.optimization_barrier((up, down, far))
     far_up, far_down = swap(up), swap(down)
-    near2 = over_x(split(up, down))
-    near1, far_down = lax.optimization_barrier((near1, far_down))
-    cross1 = swap(near1)
+    outbound = pl.pallas_call(
+        split_kernel,
+        out_shape=jax.ShapeDtypeStruct((X, rows, 768), BF16),
+        in_specs=[SMEM] + [VMEM] * 3,
+        out_specs=VMEM,
+        compiler_params=params(),
+        cost_estimate=cost(0, 4 * rows * 768 * 4),
+        name="split",
+    )(where, base, up, down)
+    near = lax.all_to_all(outbound, "dp", 0, 0, axis_index_groups=along_x, tiled=True)
 
     steps = heads // 6
     block = pl.BlockSpec((1, rows, width), lambda k, where: (k, 0, 0))
@@ -276,28 +291,27 @@
         project_weight.reshape(steps, 3, 2, width, cols), cotangent, offsets,
     )
 
-    grads, cross1 = lax.optimization_barrier((grads, cross1))
     all_grads = lax.all_gather(grads, "dp", axis=0, axis_index_groups=along_x)
-    near2, all_grads = lax.optimization_barrier((near2, all_grads))
-    cross2 = swap(near2)
+    near, all_grads = lax.optimization_barrier((near, all_grads))
+    cross = swap(near)
     terms = pl.pallas_call(
         weight_kernel,
-        out_shape=jax.ShapeDtypeStruct((1536, cols), BF16),
-        in_specs=[SMEM] + [VMEM] * 5,
+        out_shape=jax.ShapeDtypeStruct((Y, 192, cols), BF16),
+        in_specs=[SMEM] + [VMEM] * 3,
         out_specs=VMEM,
         compiler_params=params(),
         cost_estimate=cost(2 * 4 * rows * 1536 * cols, 6 * 1024 * 1024),
         name="weight",
-    )(where, near1, near2, cross1, cross2, all_grads)
-    gathered = lax.all_to_all(terms.reshape(owners, 48, cols), "dp", 0, 0, tiled=True)
+    )(where, near, cross, all_grads)
+    gathered = lax.all_to_all(terms, "dp", 0, 0, axis_index_groups=along_y, tiled=True)
     weight_grad = pl.pallas_call(
         sum_kernel,
         out_shape=jax.ShapeDtypeStruct((192, cols), F32),
-        in_specs=[VMEM],
+        in_specs=[SMEM, VMEM],
         out_specs=VMEM,
         compiler_params=params(),
         name="sum",
-    )(gathered)
+    )(where, gathered)
     return attention, weight_grad
 
 

time: 178 us -> 171 us (0.961)
  starting transfers between devices: 33.6 us -> 27.9 us
  waiting for transfers between devices: 15.7 us -> 20.9 us
  blocking collectives: 103 us -> 99.8 us
    ppermute x2, waiting for transfers between devices: 7.54 us -> 15.6 us  [shift(): lax.ppermute(block, 'mp', [(k, (k + by) % heads) for k in range(heads)])]
    all_to_all x2 -> x1, waiting for transfers between devices: 5.68 us -> 0.01 us  [shards(): lax.all_to_all(outbound, 'dp', 0, 0, axis_index_groups=along_x, tiled=True)]
    all_to_all x2 -> x1, starting transfers between devices: 8.33 us -> 3.58 us  [shards(): lax.all_to_all(outbound, 'dp', 0, 0, axis_index_groups=along_x, tiled=True)]
    all_to_all x1, blocking collectives: 37.5 us -> 33.3 us  [shards(): lax.all_to_all(terms, 'dp', 0, 0, axis_index_groups=along_y, tiled=True)]
    ppermute x5 -> x4, waiting for transfers between devices: 2.46 us -> 5.26 us  [swap(): return lax.ppermute(block, 'mp', [(k, k ^ 1) for k in range(heads)])]
    ppermute x5 -> x4, starting transfers between devices: 17.4 us -> 14.8 us  [swap(): return lax.ppermute(block, 'mp', [(k, k ^ 1) for k in range(heads)])]
    pallas_call x3 -> x2, Pallas kernels: 7.45 us -> 5.08 us  [the longest x1 2.68 us: shards(): pl.pallas_call(weight_kernel, out_shape=jax.ShapeDtypeStruct((Y, 192, col...]
    unnamed x12 -> x10, local copies, waits for them, and re-layouts: 5.94 us -> 4.49 us
  transfers between devices with their start and end apart: 9 -> 7, of which waited for: 3 -> 4; matrix products, arithmetic and copies ran while one was open for 0% -> 0% of each run, Pallas kernels for 6% -> 4%
where the time goes in v4:
time: 171 us
  blocking collectives  99.8 us (58%)
  starting transfers between devices  27.9 us (16%)
  waiting for transfers between devices  20.9 us (12%)
  Pallas kernels  16.5 us (10%)
  local copies, waits for them, and re-layouts  4.58 us (3%)
    all_to_all x1, blocking collectives, shards(): lax.all_to_all(terms, 'dp', 0, 0, axis_index_groups=along_y, tiled=True)  33.3 us
    all_gather x1, blocking collectives, shards(): base = lax.all_gather(compact, 'mp', axis=0, axis_index_groups=thirds)  29.2 us
    all_to_all x1, blocking collectives, shards(): lax.all_to_all(outgoing.reshape(owners, ROOM, width), 'dp', 0, 0, tiled=T...  21.8 us
    ppermute x2, waiting for transfers between devices, shift(): lax.ppermute(block, 'mp', [(k, (k + by) % heads) for k in range(heads)])  15.6 us
    all_gather x1, blocking collectives, shards(): all_grads = lax.all_gather(grads, 'dp', axis=0, axis_index_groups=along_x)  15.6 us
    ppermute x4, starting transfers between devices, swap(): return lax.ppermute(block, 'mp', [(k, k ^ 1) for k in range(heads)])  14.8 us
    ppermute x2, starting transfers between devices, shift(): lax.ppermute(block, 'mp', [(k, (k + by) % heads) for k in range(heads)])  9.55 us
    pallas_call x1, Pallas kernels, shards(): pl.pallas_call(attend_kernel, grid_spec=pltpu.PrefetchScalarGridSpec(num_...  7.36 us
  transfers between devices with their start and end apart: 7, of which 4 were waited for; matrix products, arithmetic and copies ran while one was open for 0% of the time, Pallas kernels for 4%

profile of v4, /device:TPU:1, one launch (start us, length us, event | category | flops | bytes accessed | tf_op | source)
XLA Modules:
  0.0 170.6 jit_solution(8267361762232301960)
XLA Ops:
  0.6 0.8 copy.7.route
  1.4 0.8 copy.8.slot
  2.3 0.0 copy-start.2
  2.3 0.9 copy-done.2
  3.2 1.4 send.1
  4.6 21.8 %all_to_all.15 = bf16[32,24,256]{2,1,0:T(8,128)(2,1)S(1)} all-to-all(bf16[32,24,256]{2,1,0:T(8,128)(2,1)S(1)} %bitcast.18), channel_id=1, replica_groups=mesh['dp'=32,'mp'=24] {'dp'}, dimensions={0} | all-to-all | bytes 786432 | tf_op jit(solution)/shard_map/all_to_all | solution.py:227
  26.3 1.2 receive.1
  27.6 29.2 %all-gather = bf16[1152,256]{1,0:T(8,128)(2,1)S(1)} all-gather(bf16[288,256]{1,0:T(8,128)(2,1)S(1)} %get-tuple-element.11), channel_id=2, replica_groups={{0,6,12,18},{1,7,13,19},{2,8,14,20},{3,9,15,21},{4,10,16,22},{5,11,17,2..., dimensions={0}, use_global_device_ids=true | all-gather | bytes 737280 | tf_op jit(solution)/shard_map/all_gather | solution.py:248
  56.8 6.5 %collective-permute-start.2 = (bf16[4,288,256]{2,1,0:T(8,128)(2,1)S(1)}, bf16[4,288,256]{2,1,0:T(8,128)(2,1)S(1)}, u32[]{:S(2)}, u32[]{:S(2)}) collective-permute-start(bf16[4,288,256]{2,1,0:T(8,128)(2,1)S(1)} %bitcast.11), channel_id=1, source_target_pairs={{0,1},{1,0},{2,3},{3,2},{4,5},{5,4},{6,7},{7,6},{8,9},{9,8},{10,11... | collective-permute-start | bytes 1769480 | tf_op jit(solution)/shard_map/ppermute | solution.py:246
  63.3 7.6 %collective-permute-start.1 = (bf16[4,288,256]{2,1,0:T(8,128)(2,1)S(1)}, bf16[4,288,256]{2,1,0:T(8,128)(2,1)S(1)}, u32[]{:S(2)}, u32[]{:S(2)}) collective-permute-start(bf16[4,288,256]{2,1,0:T(8,128)(2,1)S(1)} %bitcast.12), channel_id=1, source_target_pairs={{0,22},{1,23},{2,0},{3,1},{4,2},{5,3},{6,4},{7,5},{8,6},{9,7},{10,... | collective-permute-start | bytes 1769480 | tf_op jit(solution)/shard_map/ppermute | solution.py:243
  70.9 1.9 %collective-permute-start = (bf16[4,288,256]{2,1,0:T(8,128)(2,1)S(1)}, bf16[4,288,256]{2,1,0:T(8,128)(2,1)S(1)}, u32[]{:S(2)}, u32[]{:S(2)}) collective-permute-start(bf16[4,288,256]{2,1,0:T(8,128)(2,1)S(1)} %bitcast.13), channel_id=1, source_target_pairs={{0,2},{1,3},{2,4},{3,5},{4,6},{5,7},{6,8},{7,9},{8,10},{9,11},{10,... | collective-permute-start | bytes 1769480 | tf_op jit(solution)/shard_map/ppermute | solution.py:243
  72.9 0.1 stack.31.where
  73.0 0.0 collective-permute-done.2.far
  73.0 0.0 copy-start
  73.0 10.6 %collective-permute-done.1.down = bf16[4,288,256]{2,1,0:T(8,128)(2,1)S(1)} collective-permute-done((bf16[4,288,256]{2,1,0:T(8,128)(2,1)S(1)}, bf16[4,288,256]{2,1,0:T(8,128)(2,1)S(1)}, u32[]{:S(2)}, u32[]{:S(2)}) %collective-permute-start.1) | collective-permute-done | bytes 589856 | tf_op jit(solution)/shard_map/ppermute | solution.py:243
  83.6 5.0 %collective-permute-done.up = bf16[4,288,256]{2,1,0:T(8,128)(2,1)S(1)} collective-permute-done((bf16[4,288,256]{2,1,0:T(8,128)(2,1)S(1)}, bf16[4,288,256]{2,1,0:T(8,128)(2,1)S(1)}, u32[]{:S(2)}, u32[]{:S(2)}) %collective-permute-start) | collective-permute-done | bytes 589856 | tf_op jit(solution)/shard_map/ppermute | solution.py:243
  88.6 2.4 %split.1 = bf16[4,288,768]{2,1,0:T(8,128)(2,1)} custom-call(s32[6]{0:T(128)S(1)} %stack.31.where, bf16[4,288,256]{2,1,0:T(8,128)(2,1)S(1)} %bitcast.14, bf16[4,288,256]{2,1,0:T(8,128)(2,1)S(1)} %collective-permute-done.up, bf16[4,288,256]{2,1,0:T(8,128)(2,1)S(1)} %collective-permute-done.1.down), custom_call_target="tpu_custom_call" | custom-call | bytes 3538944 | tf_op jit(solution)/shard_map/split/pallas_call | solution.py:252
  91.0 0.0 copy-done
  91.0 3.6 %all-to-all-start.1 = ((bf16[4,288,768]{2,1,0:T(8,128)(2,1)}), bf16[4,288,768]{2,1,0:T(8,128)(2,1)S(1)}, u32[]{:S(2)}, u32[]{:S(2)}) async-start(bf16[4,288,768]{2,1,0:T(8,128)(2,1)} %split.1), calls=%async_computation.1 | async-start | bytes 3538944 | tf_op jit(solution)/shard_map/all_to_all | solution.py:261
  94.6 3.0 %collective-permute-start.3 = (bf16[4,288,256]{2,1,0:T(8,128)(2,1)S(1)}, bf16[4,288,256]{2,1,0:T(8,128)(2,1)S(1)}, u32[]{:S(2)}, u32[]{:S(2)}) collective-permute-start(bf16[4,288,256]{2,1,0:T(8,128)(2,1)S(1)} %collective-permute-done.up), channel_id=1, source_target_pairs={{0,1},{1,0},{2,3},{3,2},{4,5},{5,4},{6,7},{7,6},{8,9},{9,8},{10,11... | collective-permute-start | bytes 1769480 | tf_op jit(solution)/shard_map/ppermute | solution.py:246
  97.6 1.9 %collective-permute-start.4 = (bf16[4,288,256]{2,1,0:T(8,128)(2,1)S(1)}, bf16[4,288,256]{2,1,0:T(8,128)(2,1)S(1)}, u32[]{:S(2)}, u32[]{:S(2)}) collective-permute-start(bf16[4,288,256]{2,1,0:T(8,128)(2,1)S(1)} %collective-permute-done.1.down), channel_id=1, source_target_pairs={{0,1},{1,0},{2,3},{3,2},{4,5},{5,4},{6,7},{7,6},{8,9},{9,8},{10,11... | collective-permute-start | bytes 1769480 | tf_op jit(solution)/shard_map/ppermute | solution.py:246
  99.6 0.0 collective-permute-done.3.far_up
  99.6 2.0 %collective-permute-done.4.far_down = bf16[4,288,256]{2,1,0:T(8,128)(2,1)S(1)} collective-permute-done((bf16[4,288,256]{2,1,0:T(8,128)(2,1)S(1)}, bf16[4,288,256]{2,1,0:T(8,128)(2,1)S(1)}, u32[]{:S(2)}, u32[]{:S(2)}) %collective-permute-start.4) | collective-permute-done | bytes 589856 | tf_op jit(solution)/shard_map/ppermute | solution.py:246
  101.5 0.0 copy-start.1
  101.5 1.1 copy-done.1
  102.6 0.0 copy-start.3
  102.6 0.9 copy-done.3
  103.5 7.4 %attend.1 = (bf16[384,128]{1,0:T(8,128)(2,1)}, bf16[288,384]{1,0:T(8,128)(2,1)S(1)}) custom-call(s32[6]{0:T(128)S(1)} %stack.31.where, bf16[4,288,256]{2,1,0:T(8,128)(2,1)S(1)} %bitcast.15, bf16[4,288,256]{2,1,0:T(8,128)(2,1)S(1)} %collective-permute-done.up, bf16[4,288,256]{2,1,0:T(8,128)(2,1)S(1)} %collective-permute-done.1.down, ...), custom_call_target="tpu_custom_call" | custom-call | flops 1358954496 | bytes 9437184 | tf_op jit(solution)/shard_map/attend/pallas_call | solution.py:265
  110.9 15.6 %all-gather.1 = bf16[1152,384]{1,0:T(8,128)(2,1)S(1)} all-gather(bf16[288,384]{1,0:T(8,128)(2,1)S(1)} %get-tuple-element.17), channel_id=3, replica_groups={{0,24,48,72},{96,120,144,168},{192,216,240,264},{288,312,336,360},{384,..., dimensions={0}, use_global_device_ids=true | all-gather | bytes 1105920 | tf_op jit(solution)/shard_map/all_gather | solution.py:294
  126.4 0.0 all-to-all-done.1.near
  126.4 3.4 %collective-permute-start.5 = (bf16[4,288,768]{2,1,0:T(8,128)(2,1)S(1)}, bf16[4,288,768]{2,1,0:T(8,128)(2,1)S(1)}, u32[]{:S(2)}, u32[]{:S(2)}) collective-permute-start(bf16[4,288,768]{2,1,0:T(8,128)(2,1)S(1)} %all-to-all-done.1.near), channel_id=1, source_target_pairs={{0,1},{1,0},{2,3},{3,2},{4,5},{5,4},{6,7},{7,6},{8,9},{9,8},{10,11... | collective-permute-start | bytes 5308424 | tf_op jit(solution)/shard_map/ppermute | solution.py:246
  129.8 3.3 %collective-permute-done.5.cross = bf16[4,288,768]{2,1,0:T(8,128)(2,1)S(1)} collective-permute-done((bf16[4,288,768]{2,1,0:T(8,128)(2,1)S(1)}, bf16[4,288,768]{2,1,0:T(8,128)(2,1)S(1)}, u32[]{:S(2)}, u32[]{:S(2)}) %collective-permute-start.5) | collective-permute-done | bytes 1769504 | tf_op jit(solution)/shard_map/ppermute | solution.py:246
  133.1 2.7 %weight.1 = bf16[8,192,384]{2,1,0:T(8,128)(2,1)S(1)} custom-call(s32[6]{0:T(128)S(1)} %stack.31.where, bf16[4,288,768]{2,1,0:T(8,128)(2,1)S(1)} %all-to-all-done.1.near, bf16[4,288,768]{2,1,0:T(8,128)(2,1)S(1)} %collective-permute-done.5.cross, bf16[4,288,384]{2,1,0:T(8,128)(2,1)S(1)} %bitcast.16), custom_call_target="tpu_custom_call" | custom-call | flops 1358954496 | bytes 6291456 | tf_op jit(solution)/shard_map/weight/pallas_call | solution.py:297
  135.8 33.3 %all_to_all.16.terms = bf16[8,192,384]{2,1,0:T(8,128)(2,1)S(1)} all-to-all(bf16[8,192,384]{2,1,0:T(8,128)(2,1)S(1)} %weight.1), channel_id=1, replica_groups={{0,96,192,288,384,480,576,672},{24,120,216,312,408,504,600,696},{48,144..., dimensions={0} | all-to-all | bytes 2359296 | tf_op jit(solution)/shard_map/all_to_all | solution.py:306
  169.1 1.5 sum.1
Async XLA Ops:
  2.3 0.9 copy-start.2
  56.8 16.2 %collective-permute-start.2 = (bf16[4,288,256]{2,1,0:T(8,128)(2,1)S(1)}, bf16[4,288,256]{2,1,0:T(8,128)(2,1)S(1)}, u32[]{:S(2)}, u32[]{:S(2)}) collective-permute-start(bf16[4,288,256]{2,1,0:T(8,128)(2,1)S(1)} %bitcast.11), channel_id=1, source_target_pairs={{0,1},{1,0},{2,3},{3,2},{4,5},{5,4},{6,7},{7,6},{8,9},{9,8},{10,11... | collective-permute-start | bytes 1769480 | tf_op jit(solution)/shard_map/ppermute | solution.py:246
  63.3 20.4 %collective-permute-start.1 = (bf16[4,288,256]{2,1,0:T(8,128)(2,1)S(1)}, bf16[4,288,256]{2,1,0:T(8,128)(2,1)S(1)}, u32[]{:S(2)}, u32[]{:S(2)}) collective-permute-start(bf16[4,288,256]{2,1,0:T(8,128)(2,1)S(1)} %bitcast.12), channel_id=1, source_target_pairs={{0,22},{1,23},{2,0},{3,1},{4,2},{5,3},{6,4},{7,5},{8,6},{9,7},{10,... | collective-permute-start | bytes 1769480 | tf_op jit(solution)/shard_map/ppermute | solution.py:243
  70.9 17.7 %collective-permute-start = (bf16[4,288,256]{2,1,0:T(8,128)(2,1)S(1)}, bf16[4,288,256]{2,1,0:T(8,128)(2,1)S(1)}, u32[]{:S(2)}, u32[]{:S(2)}) collective-permute-start(bf16[4,288,256]{2,1,0:T(8,128)(2,1)S(1)} %bitcast.13), channel_id=1, source_target_pairs={{0,2},{1,3},{2,4},{3,5},{4,6},{5,7},{6,8},{7,9},{8,10},{9,11},{10,... | collective-permute-start | bytes 1769480 | tf_op jit(solution)/shard_map/ppermute | solution.py:243
  73.0 18.0 %copy-start = (bf16[4,288,256]{2,1,0:T(8,128)(2,1)}, bf16[4,288,256]{2,1,0:T(8,128)(2,1)S(1)}, u32[]{:S(2)}) copy-start(bf16[4,288,256]{2,1,0:T(8,128)(2,1)S(1)} %collective-permute-done.2.far) | copy-start | bytes 1769476
  91.0 35.4 %all-to-all-start.1 = ((bf16[4,288,768]{2,1,0:T(8,128)(2,1)}), bf16[4,288,768]{2,1,0:T(8,128)(2,1)S(1)}, u32[]{:S(2)}, u32[]{:S(2)}) async-start(bf16[4,288,768]{2,1,0:T(8,128)(2,1)} %split.1), calls=%async_computation.1 | async-start | bytes 3538944 | tf_op jit(solution)/shard_map/all_to_all | solution.py:261
  94.6 5.0 %collective-permute-start.3 = (bf16[4,288,256]{2,1,0:T(8,128)(2,1)S(1)}, bf16[4,288,256]{2,1,0:T(8,128)(2,1)S(1)}, u32[]{:S(2)}, u32[]{:S(2)}) collective-permute-start(bf16[4,288,256]{2,1,0:T(8,128)(2,1)S(1)} %collective-permute-done.up), channel_id=1, source_target_pairs={{0,1},{1,0},{2,3},{3,2},{4,5},{5,4},{6,7},{7,6},{8,9},{9,8},{10,11... | collective-permute-start | bytes 1769480 | tf_op jit(solution)/shard_map/ppermute | solution.py:246
  97.6 3.9 %collective-permute-start.4 = (bf16[4,288,256]{2,1,0:T(8,128)(2,1)S(1)}, bf16[4,288,256]{2,1,0:T(8,128)(2,1)S(1)}, u32[]{:S(2)}, u32[]{:S(2)}) collective-permute-start(bf16[4,288,256]{2,1,0:T(8,128)(2,1)S(1)} %collective-permute-done.1.down), channel_id=1, source_target_pairs={{0,1},{1,0},{2,3},{3,2},{4,5},{5,4},{6,7},{7,6},{8,9},{9,8},{10,11... | collective-permute-start | bytes 1769480 | tf_op jit(solution)/shard_map/ppermute | solution.py:246
  101.5 1.1 copy-start.1
  102.6 0.9 copy-start.3
  126.4 6.7 %collective-permute-start.5 = (bf16[4,288,768]{2,1,0:T(8,128)(2,1)S(1)}, bf16[4,288,768]{2,1,0:T(8,128)(2,1)S(1)}, u32[]{:S(2)}, u32[]{:S(2)}) collective-permute-start(bf16[4,288,768]{2,1,0:T(8,128)(2,1)S(1)} %all-to-all-done.1.near), channel_id=1, source_target_pairs={{0,1},{1,0},{2,3},{3,2},{4,5},{5,4},{6,7},{7,6},{8,9},{9,8},{10,11... | collective-permute-start | bytes 5308424 | tf_op jit(solution)/shard_map/ppermute | solution.py:246

commit v5 on v4

--- a/solution.py
+++ b/solution.py
@@ -10,7 +10,7 @@
 SENT = 18
 ROOM = 24
 X, Y = 4, 8
-ATTEND_VMEM = 48
+PROJECT_VMEM = 48
 F32, BF16, I32 = jnp.float32, jnp.bfloat16, jnp.int32
 
 
@@ -26,22 +26,28 @@
     return lax.dot_general(a, b, (((ca,), (cb,)), ((), ())), preferred_element_type=F32)
 
 
-def send_kernel(patches, route, slot, out):
+def send_kernel(patches_in, route_in, slot_in, out, patches, route, slot, done):
+    pairs = ((route_in, route), (slot_in, slot), (patches_in, patches))
+    copies = [pltpu.make_async_copy(a, b, done.at[i]) for i, (a, b) in enumerate(pairs)]
+    for copy in copies:
+        copy.start()
+    for copy in copies:
+        copy.wait()
     rows = patches.shape[0]
     owners = out.shape[0] // ROOM
     pack = route[...]
     place = slot[...]
-    matches = hot(pack == iota((rows, owners), 1))
-    before = mm(hot(iota((rows, rows), 0) > iota((rows, rows), 1)), matches)
-    position = jnp.sum(before * matches.astype(F32), axis=1, keepdims=True).astype(I32)
-    spread = hot(pack * ROOM + position == iota((rows, owners * ROOM), 1))
-    total = mm(spread, patches[...], 0, 0)
-    held = hot(position == iota((rows, 256), 1)).astype(F32)
-    high = (held * ((place >> 1) + 1).astype(F32)).astype(BF16)
-    low = (held * (place & 1).astype(F32)).astype(BF16)
+    matches = hot(pack == iota((owners, rows), 0))
+    before = mm(matches, hot(iota((rows, rows), 0) < iota((rows, rows), 1)))
+    matches = matches.astype(F32)
+    position = jnp.sum(before * matches, axis=0, keepdims=True).astype(I32)
+    total = mm(hot(pack * ROOM + position == iota((owners * ROOM, rows), 0)), patches[...])
+    held = hot(position == iota((256, rows), 0))
+    high = (matches * ((place >> 1) + 1).astype(F32)).astype(BF16)
+    low = (matches * (place & 1).astype(F32)).astype(BF16)
     line, owner = iota((owners * ROOM, owners), 0), iota((owners * ROOM, owners), 1)
     for row, part in ((SENT, high), (SENT + 1, low)):
-        total += mm(hot(line == owner * ROOM + row), mm(matches, part, 0, 0).astype(BF16))
+        total += mm(hot(line == owner * ROOM + row), mm(part, held, 1, 1).astype(BF16))
     out[...] = total.astype(BF16)
 
 
@@ -89,48 +95,46 @@
     return image, index - base + CAP * image
 
 
-def attend_kernel(
-    where, base, up, down, far, far_up, far_down, weight, cotangent, offsets, attention, grads, total
-):
+def project_kernel(where, base, up, down, weight, far_weight, own, far):
     step = pl.program_id(0)
-    core = where[0]
-    part = mm(base[0], weight[0, where[1], core]) + mm(far[0], weight[0, where[1], 1 - core])
-    part += mm(up[0], weight[0, where[2], core]) + mm(far_up[0], weight[0, where[2], 1 - core])
-    part += mm(down[0], weight[0, where[3], core]) + mm(far_down[0], weight[0, where[3], 1 - core])
-
-    @pl.when(step == 0)
-    def _():
-        total[...] = part
-
-    @pl.when(step > 0)
-    def _():
-        total[...] += part
-
-    @pl.when(step == pl.num_programs(0) - 1)
-    def _():
-        rows, slots = total.shape[0], attention.shape[0]
-        offs = offsets[...]
-        image_col, slot_col = places(iota((rows, 1), 0), offs)
-        image_row, slot_row = places(iota((1, rows), 1), offs)
-        same = image_col == image_row
-        cot = mm(hot(slot_col == iota((rows, slots), 1)), cotangent[...]).astype(BF16)
-        rounded = total[...].astype(BF16)
-        query, key, value = rounded[:, :HD], rounded[:, HD : 2 * HD], rounded[:, 2 * HD :]
-        scale = HD ** (-0.5)
-        scores = mm(query, key, 1, 1) * scale
-        expscore = jnp.where(same, jnp.exp(jnp.where(same, scores, 0.0)), 0.0)
-        softmax = expscore / jnp.sum(expscore, axis=1, keepdims=True)
-        weights = softmax.astype(BF16)
-        result = mm(weights, value).astype(BF16)
-        attention[...] = mm(hot(iota((slots, rows), 0) == slot_row), result).astype(BF16)
-        d_value = mm(weights, cot, 0, 0)
-        d_weights = mm(cot, value, 1, 1).astype(BF16).astype(F32)
-        d_weights = jnp.where(same, d_weights, 0.0)
-        inner = jnp.sum(d_weights * softmax, axis=1, keepdims=True)
-        d_scores = (softmax * (d_weights - inner) * scale).astype(BF16)
-        grads[:, :HD] = mm(d_scores, key).astype(BF16)
-        grads[:, HD : 2 * HD] = mm(d_scores, query, 0, 0).astype(BF16)
-        grads[:, 2 * HD :] = d_value.astype(BF16)
+    for block, out in ((weight, own), (far_weight, far)):
+        part = mm(base[0], block[0, where[1], 0])
+        part += mm(up[0], block[0, where[2], 0])
+        part += mm(down[0], block[0, where[3], 0])
+
+        @pl.when(step == 0)
+        def _(part=part, out=out):
+            out[...] = part
+
+        @pl.when(step > 0)
+        def _(part=part, out=out):
+            out[...] += part
+
+
+def attend_kernel(own, far, cotangent, offsets, attention, grads):
+    rows, slots = grads.shape[0], attention.shape[0]
+    offs = offsets[...]
+    image_col, slot_col = places(iota((rows, 1), 0), offs)
+    image_row, slot_row = places(iota((1, rows), 1), offs)
+    same = image_col == image_row
+    cot = mm(hot(slot_col == iota((rows, slots), 1)), cotangent[...]).astype(BF16)
+    rounded = (own[...] + far[...]).astype(BF16)
+    query, key, value = rounded[:, :HD], rounded[:, HD : 2 * HD], rounded[:, 2 * HD :]
+    scale = HD ** (-0.5)
+    scores = mm(query, key, 1, 1) * scale
+    expscore = jnp.where(same, jnp.exp(jnp.where(same, scores, 0.0)), 0.0)
+    softmax = expscore / jnp.sum(expscore, axis=1, keepdims=True)
+    weights = softmax.astype(BF16)
+    result = mm(weights, value).astype(BF16)
+    attention[...] = mm(hot(iota((slots, rows), 0) == slot_row), result).astype(BF16)
+    d_value = mm(weights, cot, 0, 0)
+    d_weights = mm(cot, value, 1, 1).astype(BF16).astype(F32)
+    d_weights = jnp.where(same, d_weights, 0.0)
+    inner = jnp.sum(d_weights * softmax, axis=1, keepdims=True)
+    d_scores = (softmax * (d_weights - inner) * scale).astype(BF16)
+    grads[:, :HD] = mm(d_scores, key).astype(BF16)
+    grads[:, HD : 2 * HD] = mm(d_scores, query, 0, 0).astype(BF16)
+    grads[:, 2 * HD :] = d_value.astype(BF16)
 
 
 PICKS = (((0, 1), (4, 1), (5, 2), (3, 2)), ((2, 3), (0, 3), (1, 4), (5, 4)))
@@ -219,11 +223,17 @@
     outgoing = pl.pallas_call(
         send_kernel,
         out_shape=jax.ShapeDtypeStruct((owners * ROOM, width), BF16),
-        in_specs=[VMEM] * 3,
+        in_specs=[pl.BlockSpec(memory_space=pl.ANY)] * 3,
         out_specs=VMEM,
+        scratch_shapes=[
+            pltpu.VMEM((rows, width), BF16),
+            pltpu.VMEM((1, rows), I32),
+            pltpu.VMEM((1, rows), I32),
+            pltpu.SemaphoreType.DMA((3,)),
+        ],
         compiler_params=params(),
         name="send",
-    )(patches, pack_route, pack_slot)
+    )(patches, pack_route.reshape(1, rows), pack_slot.reshape(1, rows))
     arrived = lax.all_to_all(outgoing.reshape(owners, ROOM, width), "dp", 0, 0, tiled=True)
     compact, offsets = pl.pallas_call(
         receive_kernel,
@@ -245,10 +255,32 @@
     def swap(block):
         return lax.ppermute(block, "mp", [(k, k ^ 1) for k in range(heads)])
 
+    far_weight = swap(project_weight)
     base = lax.all_gather(compact, "mp", axis=0, axis_index_groups=thirds)
-    up, down, far = shift(base, 2), shift(base, -2), swap(base)
-    up, down, far = lax.optimization_barrier((up, down, far))
-    far_up, far_down = swap(up), swap(down)
+    up, down = shift(base, 2), shift(base, -2)
+
+    steps = heads // 6
+    block = pl.BlockSpec((1, rows, width), lambda k, where: (k, 0, 0))
+    weight_block = pl.BlockSpec((1, 3, 1, width, cols), lambda k, where: (k, 0, where[0], 0, 0))
+    result = pl.BlockSpec((rows, cols), lambda k, where: (0, 0))
+    own, far = pl.pallas_call(
+        project_kernel,
+        grid_spec=pltpu.PrefetchScalarGridSpec(
+            num_scalar_prefetch=1,
+            grid=(steps,),
+            in_specs=[block] * 3 + [weight_block] * 2,
+            out_specs=(result, result),
+        ),
+        out_shape=(jax.ShapeDtypeStruct((rows, cols), F32),) * 2,
+        compiler_params=pltpu.CompilerParams(vmem_limit_bytes=PROJECT_VMEM * 1024 * 1024),
+        cost_estimate=cost(2 * heads * rows * width * cols, 9 * 1024 * 1024),
+        name="project",
+    )(
+        where, base, up, down,
+        project_weight.reshape(steps, 3, 2, width, cols),
+        far_weight.reshape(steps, 3, 2, width, cols),
+    )
+    own_far = swap(far)
     outbound = pl.pallas_call(
         split_kernel,
         out_shape=jax.ShapeDtypeStruct((X, rows, 768), BF16),
@@ -259,37 +291,18 @@
         name="split",
     )(where, base, up, down)
     near = lax.all_to_all(outbound, "dp", 0, 0, axis_index_groups=along_x, tiled=True)
-
-    steps = heads // 6
-    block = pl.BlockSpec((1, rows, width), lambda k, where: (k, 0, 0))
     attention, grads = pl.pallas_call(
         attend_kernel,
-        grid_spec=pltpu.PrefetchScalarGridSpec(
-            num_scalar_prefetch=1,
-            grid=(steps,),
-            in_specs=[block] * 6
-            + [
-                pl.BlockSpec((1, 3, 2, width, cols), lambda k, where: (k, 0, 0, 0, 0)),
-                pl.BlockSpec((slots, HD), lambda k, where: (0, 0)),
-                pl.BlockSpec((8, 128), lambda k, where: (0, 0)),
-            ],
-            out_specs=(
-                pl.BlockSpec((slots, HD), lambda k, where: (0, 0)),
-                pl.BlockSpec((rows, cols), lambda k, where: (0, 0)),
-            ),
-            scratch_shapes=[pltpu.VMEM((rows, cols), F32)],
-        ),
         out_shape=(
             jax.ShapeDtypeStruct((slots, HD), BF16),
             jax.ShapeDtypeStruct((rows, cols), BF16),
         ),
-        compiler_params=pltpu.CompilerParams(vmem_limit_bytes=ATTEND_VMEM * 1024 * 1024),
-        cost_estimate=cost(2 * heads * rows * width * cols, 9 * 1024 * 1024),
+        in_specs=[VMEM] * 4,
+        out_specs=(VMEM, VMEM),
+        compiler_params=params(),
+        cost_estimate=cost(2 * 9 * rows * rows * HD, 2 * 1024 * 1024),
         name="attend",
-    )(
-        where, base, up, down, far, far_up, far_down,
-        project_weight.reshape(steps, 3, 2, width, cols), cotangent, offsets,
-    )
+    )(own, own_far, cotangent, offsets)
 
     all_grads = lax.all_gather(grads, "dp", axis=0, axis_index_groups=along_x)
     near, all_grads = lax.optimization_barrier((near, all_grads))

time: 171 us -> 167 us (0.977)
  starting transfers between devices: 27.9 us -> 30.9 us
  waiting for transfers between devices: 20.9 us -> 18.2 us
  blocking collectives: 99.8 us -> 97.5 us
  local copies, waits for them, and re-layouts: 4.58 us -> 2.35 us
    ppermute x4 -> x3, starting transfers between devices: 14.8 us -> 20.4 us  [swap(): return lax.ppermute(block, 'mp', [(k, k ^ 1) for k in range(heads)])]
    all_to_all x1, blocking collectives: 21.8 us -> 17.5 us  [shards(): lax.all_to_all(outgoing.reshape(owners, ROOM, width), 'dp', 0, 0, tiled=T...]
    ppermute x2, starting transfers between devices: 9.55 us -> 6.48 us  [shift(): lax.ppermute(block, 'mp', [(k, (k + by) % heads) for k in range(heads)])]
    all_gather x1, blocking collectives: 15.6 us -> 18.4 us  [shards(): all_grads = lax.all_gather(grads, 'dp', axis=0, axis_index_groups=along_x)]
    unnamed x10 -> x8, local copies, waits for them, and re-layouts: 4.49 us -> 2.27 us
    ppermute x2, waiting for transfers between devices: 15.6 us -> 13.5 us  [shift(): lax.ppermute(block, 'mp', [(k, (k + by) % heads) for k in range(heads)])]
    ppermute x4 -> x3, waiting for transfers between devices: 5.26 us -> 4.7 us  [swap(): return lax.ppermute(block, 'mp', [(k, k ^ 1) for k in range(heads)])]
    pallas_call x1 -> x2, Pallas kernels: 7.36 us -> 7.48 us  [the longest x1 5.79 us: shards(): pl.pallas_call(project_kernel, grid_spec=pltpu.PrefetchScalarGridSpec(num...]
  transfers between devices with their start and end apart: 7 -> 6, of which waited for: 4 -> 4; matrix products, arithmetic and copies ran while one was open for 0% -> 0% of each run, Pallas kernels for 4% -> 7%
where the time goes in v5:
time: 167 us
  blocking collectives  97.5 us (58%)
  starting transfers between devices  30.9 us (19%)
  waiting for transfers between devices  18.2 us (11%)
  Pallas kernels  16.7 us (10%)
  local copies, waits for them, and re-layouts  2.35 us (1%)
    all_to_all x1, blocking collectives, shards(): lax.all_to_all(terms, 'dp', 0, 0, axis_index_groups=along_y, tiled=True)  33.8 us
    all_gather x1, blocking collectives, shards(): base = lax.all_gather(compact, 'mp', axis=0, axis_index_groups=thirds)  27.8 us
    ppermute x3, starting transfers between devices, swap(): return lax.ppermute(block, 'mp', [(k, k ^ 1) for k in range(heads)])  20.4 us
    all_gather x1, blocking collectives, shards(): all_grads = lax.all_gather(grads, 'dp', axis=0, axis_index_groups=along_x)  18.4 us
    all_to_all x1, blocking collectives, shards(): lax.all_to_all(outgoing.reshape(owners, ROOM, width), 'dp', 0, 0, tiled=T...  17.5 us
    ppermute x2, waiting for transfers between devices, shift(): lax.ppermute(block, 'mp', [(k, (k + by) % heads) for k in range(heads)])  13.5 us
    ppermute x2, starting transfers between devices, shift(): lax.ppermute(block, 'mp', [(k, (k + by) % heads) for k in range(heads)])  6.48 us
    pallas_call x1, Pallas kernels, shards(): pl.pallas_call(project_kernel, grid_spec=pltpu.PrefetchScalarGridSpec(num...  5.79 us
  transfers between devices with their start and end apart: 6, of which 4 were waited for; matrix products, arithmetic and copies ran while one was open for 0% of the time, Pallas kernels for 7%

profile of v5, /device:TPU:1, one launch (start us, length us, event | category | flops | bytes accessed | tf_op | source)
XLA Modules:
  0.0 166.6 jit_solution(2770192447118140078)
XLA Ops:
  0.6 12.4 %collective-permute-start.2 = (bf16[6144,384]{1,0:T(8,128)(2,1)}, bf16[6144,384]{1,0:T(8,128)(2,1)}, u32[]{:S(2)}, u32[]{:S(2)}) collective-permute-start(bf16[6144,384]{1,0:T(8,128)(2,1)} %param.8), channel_id=1, source_target_pairs={{0,1},{1,0},{2,3},{3,2},{4,5},{5,4},{6,7},{7,6},{8,9},{9,8},{10,11... | collective-permute-start | bytes 14155784 | tf_op jit(solution)/shard_map/ppermute | solution.py:256
  13.1 0.0 copy-start
  13.1 0.9 copy-done
  14.0 0.0 copy-start.2
  14.0 0.7 copy-done.2
  14.7 0.0 copy-start.3
  14.7 0.7 copy-done.3
  15.3 1.4 send.1
  16.8 17.5 %all_to_all.15 = bf16[32,24,256]{2,1,0:T(8,128)(2,1)S(1)} all-to-all(bf16[32,24,256]{2,1,0:T(8,128)(2,1)S(1)} %bitcast.20), channel_id=1, replica_groups=mesh['dp'=32,'mp'=24] {'dp'}, dimensions={0} | all-to-all | bytes 786432 | tf_op jit(solution)/shard_map/all_to_all | solution.py:237
  34.3 1.2 receive.1
  35.5 27.8 %all-gather = bf16[1152,256]{1,0:T(8,128)(2,1)S(1)} all-gather(bf16[288,256]{1,0:T(8,128)(2,1)S(1)} %get-tuple-element.10), channel_id=2, replica_groups={{0,6,12,18},{1,7,13,19},{2,8,14,20},{3,9,15,21},{4,10,16,22},{5,11,17,2..., dimensions={0}, use_global_device_ids=true | all-gather | bytes 737280 | tf_op jit(solution)/shard_map/all_gather | solution.py:259
  63.3 4.4 %collective-permute-start = (bf16[4,288,256]{2,1,0:T(8,128)(2,1)S(1)}, bf16[4,288,256]{2,1,0:T(8,128)(2,1)S(1)}, u32[]{:S(2)}, u32[]{:S(2)}) collective-permute-start(bf16[4,288,256]{2,1,0:T(8,128)(2,1)S(1)} %bitcast.14), channel_id=1, source_target_pairs={{0,2},{1,3},{2,4},{3,5},{4,6},{5,7},{6,8},{7,9},{8,10},{9,11},{10,... | collective-permute-start | bytes 1769480 | tf_op jit(solution)/shard_map/ppermute | solution.py:253
  67.7 2.1 %collective-permute-start.1 = (bf16[4,288,256]{2,1,0:T(8,128)(2,1)S(1)}, bf16[4,288,256]{2,1,0:T(8,128)(2,1)S(1)}, u32[]{:S(2)}, u32[]{:S(2)}) collective-permute-start(bf16[4,288,256]{2,1,0:T(8,128)(2,1)S(1)} %bitcast.15), channel_id=1, source_target_pairs={{0,22},{1,23},{2,0},{3,1},{4,2},{5,3},{6,4},{7,5},{8,6},{9,7},{10,... | collective-permute-start | bytes 1769480 | tf_op jit(solution)/shard_map/ppermute | solution.py:253
  69.9 0.1 stack.31.where
  70.0 9.8 %collective-permute-done.up = bf16[4,288,256]{2,1,0:T(8,128)(2,1)S(1)} collective-permute-done((bf16[4,288,256]{2,1,0:T(8,128)(2,1)S(1)}, bf16[4,288,256]{2,1,0:T(8,128)(2,1)S(1)}, u32[]{:S(2)}, u32[]{:S(2)}) %collective-permute-start) | collective-permute-done | bytes 589856 | tf_op jit(solution)/shard_map/ppermute | solution.py:253
  79.8 3.7 %collective-permute-done.1.down = bf16[4,288,256]{2,1,0:T(8,128)(2,1)S(1)} collective-permute-done((bf16[4,288,256]{2,1,0:T(8,128)(2,1)S(1)}, bf16[4,288,256]{2,1,0:T(8,128)(2,1)S(1)}, u32[]{:S(2)}, u32[]{:S(2)}) %collective-permute-start.1) | collective-permute-done | bytes 589856 | tf_op jit(solution)/shard_map/ppermute | solution.py:253
  83.5 2.4 %split.1 = bf16[4,288,768]{2,1,0:T(8,128)(2,1)} custom-call(s32[6]{0:T(128)S(1)} %stack.31.where, bf16[4,288,256]{2,1,0:T(8,128)(2,1)S(1)} %bitcast.16, bf16[4,288,256]{2,1,0:T(8,128)(2,1)S(1)} %collective-permute-done.up, bf16[4,288,256]{2,1,0:T(8,128)(2,1)S(1)} %collective-permute-done.1.down), custom_call_target="tpu_custom_call" | custom-call | bytes 3538944 | tf_op jit(solution)/shard_map/split/pallas_call | solution.py:284
  85.9 4.1 %all-to-all-start.1 = ((bf16[4,288,768]{2,1,0:T(8,128)(2,1)}), bf16[4,288,768]{2,1,0:T(8,128)(2,1)S(1)}, u32[]{:S(2)}, u32[]{:S(2)}) async-start(bf16[4,288,768]{2,1,0:T(8,128)(2,1)} %split.1), calls=%async_computation.1 | async-start | bytes 3538944 | tf_op jit(solution)/shard_map/all_to_all | solution.py:293
  90.0 0.0 collective-permute-done.2
  90.0 0.0 copy-start.1
  90.0 5.8 %project.1 = (f32[288,384]{1,0:T(8,128)S(1)}, f32[288,384]{1,0:T(8,128)S(1)}) custom-call(s32[6]{0:T(128)S(1)} %stack.31.where, bf16[4,288,256]{2,1,0:T(8,128)(2,1)S(1)} %bitcast.17, bf16[4,288,256]{2,1,0:T(8,128)(2,1)S(1)} %collective-permute-done.up, bf16[4,288,256]{2,1,0:T(8,128)(2,1)S(1)} %collective-permute-done.1.down, ...), custom_call_target="tpu_custom_call" | custom-call | flops 1358954496 | bytes 9437184 | tf_op jit(solution)/shard_map/project/pallas_call | solution.py:266
  95.8 4.0 %collective-permute-start.3 = (f32[288,384]{1,0:T(8,128)S(1)}, f32[288,384]{1,0:T(8,128)S(1)}, u32[]{:S(2)}, u32[]{:S(2)}) collective-permute-start(f32[288,384]{1,0:T(8,128)S(1)} %get-tuple-element.12), channel_id=1, source_target_pairs={{0,1},{1,0},{2,3},{3,2},{4,5},{5,4},{6,7},{7,6},{8,9},{9,8},{10,11... | collective-permute-start | bytes 1327112 | tf_op jit(solution)/shard_map/ppermute | solution.py:256
  99.8 1.4 collective-permute-done.3.far
  101.2 0.0 copy-done.1
  101.2 1.7 %attend.1 = (bf16[384,128]{1,0:T(8,128)(2,1)}, bf16[288,384]{1,0:T(8,128)(2,1)S(1)}) custom-call(f32[288,384]{1,0:T(8,128)S(1)} %get-tuple-element.11.own, f32[288,384]{1,0:T(8,128)S(1)} %collective-permute-done.3.far, bf16[384,128]{1,0:T(8,128)(2,1)S(1)} %copy-done.1, s32[8,128]{1,0:T(8,128)S(1)} %get-tuple-element.13.offsets), custom_call_target="tpu_custom_call" | custom-call | flops 191102976 | bytes 2097152 | tf_op jit(solution)/shard_map/attend/pallas_call | solution.py:294
  102.9 18.4 %all-gather.1 = bf16[1152,384]{1,0:T(8,128)(2,1)S(1)} all-gather(bf16[288,384]{1,0:T(8,128)(2,1)S(1)} %get-tuple-element.15), channel_id=3, replica_groups={{0,24,48,72},{96,120,144,168},{192,216,240,264},{288,312,336,360},{384,..., dimensions={0}, use_global_device_ids=true | all-gather | bytes 1105920 | tf_op jit(solution)/shard_map/all_gather | solution.py:307
  121.3 0.0 all-to-all-done.1.near
  121.3 4.0 %collective-permute-start.4 = (bf16[4,288,768]{2,1,0:T(8,128)(2,1)S(1)}, bf16[4,288,768]{2,1,0:T(8,128)(2,1)S(1)}, u32[]{:S(2)}, u32[]{:S(2)}) collective-permute-start(bf16[4,288,768]{2,1,0:T(8,128)(2,1)S(1)} %all-to-all-done.1.near), channel_id=1, source_target_pairs={{0,1},{1,0},{2,3},{3,2},{4,5},{5,4},{6,7},{7,6},{8,9},{9,8},{10,11... | collective-permute-start | bytes 5308424 | tf_op jit(solution)/shard_map/ppermute | solution.py:256
  125.3 3.3 %collective-permute-done.4.cross = bf16[4,288,768]{2,1,0:T(8,128)(2,1)S(1)} collective-permute-done((bf16[4,288,768]{2,1,0:T(8,128)(2,1)S(1)}, bf16[4,288,768]{2,1,0:T(8,128)(2,1)S(1)}, u32[]{:S(2)}, u32[]{:S(2)}) %collective-permute-start.4) | collective-permute-done | bytes 1769504 | tf_op jit(solution)/shard_map/ppermute | solution.py:256
  128.6 2.7 %weight.1 = bf16[8,192,384]{2,1,0:T(8,128)(2,1)S(1)} custom-call(s32[6]{0:T(128)S(1)} %stack.31.where, bf16[4,288,768]{2,1,0:T(8,128)(2,1)S(1)} %all-to-all-done.1.near, bf16[4,288,768]{2,1,0:T(8,128)(2,1)S(1)} %collective-permute-done.4.cross, bf16[4,288,384]{2,1,0:T(8,128)(2,1)S(1)} %bitcast.18), custom_call_target="tpu_custom_call" | custom-call | flops 1358954496 | bytes 6291456 | tf_op jit(solution)/shard_map/weight/pallas_call | solution.py:310
  131.3 33.8 %all_to_all.16.terms = bf16[8,192,384]{2,1,0:T(8,128)(2,1)S(1)} all-to-all(bf16[8,192,384]{2,1,0:T(8,128)(2,1)S(1)} %weight.1), channel_id=1, replica_groups={{0,96,192,288,384,480,576,672},{24,120,216,312,408,504,600,696},{48,144..., dimensions={0} | all-to-all | bytes 2359296 | tf_op jit(solution)/shard_map/all_to_all | solution.py:319
  165.1 1.5 sum.1
Async XLA Ops:
  0.6 89.4 %collective-permute-start.2 = (bf16[6144,384]{1,0:T(8,128)(2,1)}, bf16[6144,384]{1,0:T(8,128)(2,1)}, u32[]{:S(2)}, u32[]{:S(2)}) collective-permute-start(bf16[6144,384]{1,0:T(8,128)(2,1)} %param.8), channel_id=1, source_target_pairs={{0,1},{1,0},{2,3},{3,2},{4,5},{5,4},{6,7},{7,6},{8,9},{9,8},{10,11... | collective-permute-start | bytes 14155784 | tf_op jit(solution)/shard_map/ppermute | solution.py:256
  13.1 0.9 copy-start
  14.0 0.7 copy-start.2
  14.7 0.7 copy-start.3
  63.3 16.5 %collective-permute-start = (bf16[4,288,256]{2,1,0:T(8,128)(2,1)S(1)}, bf16[4,288,256]{2,1,0:T(8,128)(2,1)S(1)}, u32[]{:S(2)}, u32[]{:S(2)}) collective-permute-start(bf16[4,288,256]{2,1,0:T(8,128)(2,1)S(1)} %bitcast.14), channel_id=1, source_target_pairs={{0,2},{1,3},{2,4},{3,5},{4,6},{5,7},{6,8},{7,9},{8,10},{9,11},{10,... | collective-permute-start | bytes 1769480 | tf_op jit(solution)/shard_map/ppermute | solution.py:253
  67.7 15.8 %collective-permute-start.1 = (bf16[4,288,256]{2,1,0:T(8,128)(2,1)S(1)}, bf16[4,288,256]{2,1,0:T(8,128)(2,1)S(1)}, u32[]{:S(2)}, u32[]{:S(2)}) collective-permute-start(bf16[4,288,256]{2,1,0:T(8,128)(2,1)S(1)} %bitcast.15), channel_id=1, source_target_pairs={{0,22},{1,23},{2,0},{3,1},{4,2},{5,3},{6,4},{7,5},{8,6},{9,7},{10,... | collective-permute-start | bytes 1769480 | tf_op jit(solution)/shard_map/ppermute | solution.py:253
  85.9 35.4 %all-to-all-start.1 = ((bf16[4,288,768]{2,1,0:T(8,128)(2,1)}), bf16[4,288,768]{2,1,0:T(8,128)(2,1)S(1)}, u32[]{:S(2)}, u32[]{:S(2)}) async-start(bf16[4,288,768]{2,1,0:T(8,128)(2,1)} %split.1), calls=%async_computation.1 | async-start | bytes 3538944 | tf_op jit(solution)/shard_map/all_to_all | solution.py:293
  90.0 11.2 %copy-start.1 = (bf16[384,128]{1,0:T(8,128)(2,1)S(1)}, bf16[384,128]{1,0:T(8,128)(2,1)}, u32[]{:S(2)}) copy-start(bf16[384,128]{1,0:T(8,128)(2,1)} %cotangent.1) | copy-start | bytes 294916
  95.8 5.4 %collective-permute-start.3 = (f32[288,384]{1,0:T(8,128)S(1)}, f32[288,384]{1,0:T(8,128)S(1)}, u32[]{:S(2)}, u32[]{:S(2)}) collective-permute-start(f32[288,384]{1,0:T(8,128)S(1)} %get-tuple-element.12), channel_id=1, source_target_pairs={{0,1},{1,0},{2,3},{3,2},{4,5},{5,4},{6,7},{7,6},{8,9},{9,8},{10,11... | collective-permute-start | bytes 1327112 | tf_op jit(solution)/shard_map/ppermute | solution.py:256
  121.3 7.3 %collective-permute-start.4 = (bf16[4,288,768]{2,1,0:T(8,128)(2,1)S(1)}, bf16[4,288,768]{2,1,0:T(8,128)(2,1)S(1)}, u32[]{:S(2)}, u32[]{:S(2)}) collective-permute-start(bf16[4,288,768]{2,1,0:T(8,128)(2,1)S(1)} %all-to-all-done.1.near), channel_id=1, source_target_pairs={{0,1},{1,0},{2,3},{3,2},{4,5},{5,4},{6,7},{7,6},{8,9},{9,8},{10,11... | collective-permute-start | bytes 5308424 | tf_op jit(solution)/shard_map/ppermute | solution.py:256

commit v6 on v5

--- a/solution.py
+++ b/solution.py
@@ -11,6 +11,7 @@
 ROOM = 24
 X, Y = 4, 8
 PROJECT_VMEM = 48
+SEND_VMEM = 60
 F32, BF16, I32 = jnp.float32, jnp.bfloat16, jnp.int32
 
 
@@ -95,20 +96,28 @@
     return image, index - base + CAP * image
 
 
+def by_turn(base, up, down):
+    return ((base, down, up), (up, base, down), (down, up, base))
+
+
 def project_kernel(where, base, up, down, weight, far_weight, own, far):
     step = pl.program_id(0)
-    for block, out in ((weight, own), (far_weight, far)):
-        part = mm(base[0], block[0, where[1], 0])
-        part += mm(up[0], block[0, where[2], 0])
-        part += mm(down[0], block[0, where[3], 0])
-
-        @pl.when(step == 0)
-        def _(part=part, out=out):
-            out[...] = part
-
-        @pl.when(step > 0)
-        def _(part=part, out=out):
-            out[...] += part
+    depth = 3 * base.shape[2]
+    for turn, held in enumerate(by_turn(base, up, down)):
+
+        @pl.when(where[1] == turn)
+        def _(held=held):
+            left = jnp.concatenate([part[0] for part in held], axis=1)
+            for block, out in ((weight, own), (far_weight, far)):
+                term = mm(left, block[0, :, 0].reshape(depth, out.shape[1]))
+
+                @pl.when(step == 0)
+                def _(term=term, out=out):
+                    out[...] = term
+
+                @pl.when(step > 0)
+                def _(term=term, out=out):
+                    out[...] += term
 
 
 def attend_kernel(own, far, cotangent, offsets, attention, grads):
@@ -158,37 +167,45 @@
                 out[x, :, at + 256 : at + 384] = mm(both, (low, high)[x % 2]).astype(BF16)
 
     for side, picks in enumerate(PICKS):
-        for turn, held in enumerate(((base, down, up), (up, base, down), (down, up, base))):
+        for turn, held in enumerate(by_turn(base, up, down)):
 
             @pl.when((where[0] == side) & (where[1] == turn))
             def _(picks=picks, held=held):
                 spread(picks, held)
 
 
-def weight_kernel(where, near, cross, grads, out):
+def term_of(held, grads, a):
     depth = grads.shape[0] * grads.shape[1]
-    right = grads[...].reshape(depth, grads.shape[2])
-    for held, side in ((near, where[0]), (cross, 1 - where[0])):
+    left = held[:, :, a * 384 : a * 384 + 384].reshape(depth, 384)
+    return mm(left, grads[...].reshape(depth, grads.shape[2]), 0, 0).astype(BF16)
+
+
+def near_kernel(near, grads, out):
+    for a in range(2):
+        out[a] = term_of(near, grads, a)
+
+
+def weight_kernel(where, near_terms, cross, grads, out):
+    for source, side in ((0, where[0]), (1, 1 - where[0])):
         whole_side = jnp.where(where[4] == 1, 1 - side, side)
         for a in range(2):
-            left = held[:, :, a * 384 : a * 384 + 384].reshape(depth, 384)
-            term = mm(left, right, 0, 0).astype(BF16)
+            term = term_of(cross, grads, a) if source else near_terms[a]
             for b in range(2):
                 group = 2 * a + b
                 out[2 * group + whole_side, 0:128] = term[b * 128 : b * 128 + 128]
                 out[2 * group + side, 128:192] = term[256 + b * 64 : 320 + b * 64]
 
 
-def sum_kernel(where, terms, out):
+def sum_kernel(odd, terms, out):
     total = terms[0].astype(F32)
     for k in range(1, terms.shape[0]):
         total += terms[k].astype(F32)
 
-    @pl.when(where[5] == 0)
+    @pl.when(odd[0] == 0)
     def _():
         out[...] = total
 
-    @pl.when(where[5] == 1)
+    @pl.when(odd[0] == 1)
     def _():
         out[0:64] = total[128:192]
         out[64:192] = total[0:128]
@@ -215,7 +232,8 @@
     turn = (place // 2) % 3
     x_index = lax.axis_index("dp") % X
     inner = (x_index == 1) | (x_index == 2)
-    where = [place % 2, turn, (turn + 2) % 3, (turn + 1) % 3, inner, x_index % 2]
+    where = [place % 2, turn, (turn + 2) % 3, (turn + 1) % 3, inner]
+    odd = (lax.axis_index("dp") % 2).astype(I32).reshape(1)
     where = jnp.stack([value.astype(I32) for value in where])
     along_x = [[y * X + x for x in range(X)] for y in range(Y)]
     along_y = [[y * X + x for y in range(Y)] for x in range(X)]
@@ -231,7 +249,7 @@
             pltpu.VMEM((1, rows), I32),
             pltpu.SemaphoreType.DMA((3,)),
         ],
-        compiler_params=params(),
+        compiler_params=pltpu.CompilerParams(vmem_limit_bytes=SEND_VMEM * 1024 * 1024),
         name="send",
     )(patches, pack_route.reshape(1, rows), pack_slot.reshape(1, rows))
     arrived = lax.all_to_all(outgoing.reshape(owners, ROOM, width), "dp", 0, 0, tiled=True)
@@ -307,6 +325,15 @@
     all_grads = lax.all_gather(grads, "dp", axis=0, axis_index_groups=along_x)
     near, all_grads = lax.optimization_barrier((near, all_grads))
     cross = swap(near)
+    near_terms = pl.pallas_call(
+        near_kernel,
+        out_shape=jax.ShapeDtypeStruct((2, 384, cols), BF16),
+        in_specs=[VMEM] * 2,
+        out_specs=VMEM,
+        compiler_params=params(),
+        cost_estimate=cost(4 * rows * 1536 * cols, 3 * 1024 * 1024),
+        name="near",
+    )(near, all_grads)
     terms = pl.pallas_call(
         weight_kernel,
         out_shape=jax.ShapeDtypeStruct((Y, 192, cols), BF16),
@@ -315,7 +342,7 @@
         compiler_params=params(),
         cost_estimate=cost(2 * 4 * rows * 1536 * cols, 6 * 1024 * 1024),
         name="weight",
-    )(where, near, cross, all_grads)
+    )(where, near_terms, cross, all_grads)
     gathered = lax.all_to_all(terms, "dp", 0, 0, axis_index_groups=along_y, tiled=True)
     weight_grad = pl.pallas_call(
         sum_kernel,
@@ -324,7 +351,7 @@
         out_specs=VMEM,
         compiler_params=params(),
         name="sum",
-    )(where, gathered)
+    )(odd, gathered)
     return attention, weight_grad
 
 

time: 167 us -> 166 us (level)
  blocking collectives: 97.5 us -> 62.2 us
  waiting for transfers between devices: 18.2 us -> 46.4 us
  starting transfers between devices: 30.9 us -> 36.5 us
  local copies, waits for them, and re-layouts: 2.35 us -> 0.09 us
  Pallas kernels: 16.7 us -> 18.9 us
    all_to_all x1 -> x0, blocking collectives: 33.8 us -> none  [shards(): lax.all_to_all(terms, 'dp', 0, 0, axis_index_groups=along_y, tiled=True)]
    all_to_all x0 -> x1, waiting for transfers between devices: none -> 29.7 us  [shards(): lax.all_to_all(terms, 'dp', 0, 0, axis_index_groups=along_y, tiled=True)]
    all_to_all x0 -> x1, starting transfers between devices: none -> 3.56 us  [shards(): lax.all_to_all(terms, 'dp', 0, 0, axis_index_groups=along_y, tiled=True)]
    all_gather x1, blocking collectives: 27.8 us -> 25.3 us  [shards(): base = lax.all_gather(compact, 'mp', axis=0, axis_index_groups=thirds)]
    unnamed x8 -> x2, local copies, waits for them, and re-layouts: 2.27 us -> 0.01 us
  transfers between devices with their start and end apart: 6 -> 7, of which waited for: 4 -> 5; matrix products, arithmetic and copies ran while one was open for 0% -> 0% of each run, Pallas kernels for 7% -> 7%
where the time goes in v6:
time: 166 us; the launch traced here: 165 us
  blocking collectives  62.2 us (37%)
  waiting for transfers between devices  46.4 us (28%)
  starting transfers between devices  36.5 us (22%)
  Pallas kernels  18.9 us (11%)
    all_to_all x1, waiting for transfers between devices, shards(): lax.all_to_all(terms, 'dp', 0, 0, axis_index_groups=along_y, tiled=True)  29.7 us
    all_gather x1, blocking collectives, shards(): base = lax.all_gather(compact, 'mp', axis=0, axis_index_groups=thirds)  25.3 us
    ppermute x3, starting transfers between devices, swap(): return lax.ppermute(block, 'mp', [(k, k ^ 1) for k in range(heads)])  20.4 us
    all_to_all x1, blocking collectives, shards(): lax.all_to_all(outgoing.reshape(owners, ROOM, width), 'dp', 0, 0, tiled=T...  18.4 us
    all_gather x1, blocking collectives, shards(): all_grads = lax.all_gather(grads, 'dp', axis=0, axis_index_groups=along_x)  18.4 us
    ppermute x2, waiting for transfers between devices, shift(): lax.ppermute(block, 'mp', [(k, (k + by) % heads) for k in range(heads)])  13.3 us
    ppermute x2, starting transfers between devices, shift(): lax.ppermute(block, 'mp', [(k, (k + by) % heads) for k in range(heads)])  7.81 us
    pallas_call x1, Pallas kernels, shards(): pl.pallas_call(project_kernel, grid_spec=pltpu.PrefetchScalarGridSpec(num...  5.81 us
  transfers between devices with their start and end apart: 7, of which 5 were waited for; matrix products, arithmetic and copies ran while one was open for 0% of the time, Pallas kernels for 7%

profile of v6, /device:TPU:1, one launch (start us, length us, event | category | flops | bytes accessed | tf_op | source)
XLA Modules:
  0.0 165.0 jit_solution(1296739152025120382)
XLA Ops:
  0.6 12.4 %collective-permute-start.2 = (bf16[6144,384]{1,0:T(8,128)(2,1)}, bf16[6144,384]{1,0:T(8,128)(2,1)}, u32[]{:S(2)}, u32[]{:S(2)}) collective-permute-start(bf16[6144,384]{1,0:T(8,128)(2,1)} %param.8), channel_id=1, source_target_pairs={{0,1},{1,0},{2,3},{3,2},{4,5},{5,4},{6,7},{7,6},{8,9},{9,8},{10,11... | collective-permute-start | bytes 14155784 | tf_op jit(solution)/shard_map/ppermute | solution.py:274
  13.1 3.0 %send.1 = bf16[768,256]{1,0:T(8,128)(2,1)} custom-call(bf16[288,256]{1,0:T(8,128)(2,1)} %patches_in.1, s32[1,288]{1,0:T(1,128)} %bitcast.23, s32[1,288]{1,0:T(1,128)} %bitcast.24), custom_call_target="tpu_custom_call" | custom-call | tf_op jit(solution)/shard_map/send/pallas_call | solution.py:241
  16.0 18.4 %all_to_all.15 = bf16[32,24,256]{2,1,0:T(8,128)(2,1)S(1)} all-to-all(bf16[32,24,256]{2,1,0:T(8,128)(2,1)} %bitcast.22), channel_id=1, replica_groups=mesh['dp'=32,'mp'=24] {'dp'}, dimensions={0} | all-to-all | bytes 786432 | tf_op jit(solution)/shard_map/all_to_all | solution.py:255
  34.5 1.2 receive.1
  35.7 25.3 %all-gather = bf16[1152,256]{1,0:T(8,128)(2,1)S(1)} all-gather(bf16[288,256]{1,0:T(8,128)(2,1)S(1)} %get-tuple-element.10), channel_id=2, replica_groups={{0,6,12,18},{1,7,13,19},{2,8,14,20},{3,9,15,21},{4,10,16,22},{5,11,17,2..., dimensions={0}, use_global_device_ids=true | all-gather | bytes 737280 | tf_op jit(solution)/shard_map/all_gather | solution.py:277
  61.0 5.9 %collective-permute-start = (bf16[4,288,256]{2,1,0:T(8,128)(2,1)S(1)}, bf16[4,288,256]{2,1,0:T(8,128)(2,1)S(1)}, u32[]{:S(2)}, u32[]{:S(2)}) collective-permute-start(bf16[4,288,256]{2,1,0:T(8,128)(2,1)S(1)} %bitcast.14), channel_id=1, source_target_pairs={{0,2},{1,3},{2,4},{3,5},{4,6},{5,7},{6,8},{7,9},{8,10},{9,11},{10,... | collective-permute-start | bytes 1769480 | tf_op jit(solution)/shard_map/ppermute | solution.py:271
  66.9 1.9 %collective-permute-start.1 = (bf16[4,288,256]{2,1,0:T(8,128)(2,1)S(1)}, bf16[4,288,256]{2,1,0:T(8,128)(2,1)S(1)}, u32[]{:S(2)}, u32[]{:S(2)}) collective-permute-start(bf16[4,288,256]{2,1,0:T(8,128)(2,1)S(1)} %bitcast.15), channel_id=1, source_target_pairs={{0,22},{1,23},{2,0},{3,1},{4,2},{5,3},{6,4},{7,5},{8,6},{9,7},{10,... | collective-permute-start | bytes 1769480 | tf_op jit(solution)/shard_map/ppermute | solution.py:271
  68.9 0.1 stack.27.where
  69.0 9.7 %collective-permute-done.up = bf16[4,288,256]{2,1,0:T(8,128)(2,1)S(1)} collective-permute-done((bf16[4,288,256]{2,1,0:T(8,128)(2,1)S(1)}, bf16[4,288,256]{2,1,0:T(8,128)(2,1)S(1)}, u32[]{:S(2)}, u32[]{:S(2)}) %collective-permute-start) | collective-permute-done | bytes 589856 | tf_op jit(solution)/shard_map/ppermute | solution.py:271
  78.7 3.6 %collective-permute-done.1.down = bf16[4,288,256]{2,1,0:T(8,128)(2,1)S(1)} collective-permute-done((bf16[4,288,256]{2,1,0:T(8,128)(2,1)S(1)}, bf16[4,288,256]{2,1,0:T(8,128)(2,1)S(1)}, u32[]{:S(2)}, u32[]{:S(2)}) %collective-permute-start.1) | collective-permute-done | bytes 589856 | tf_op jit(solution)/shard_map/ppermute | solution.py:271
  82.3 2.4 %split.1 = bf16[4,288,768]{2,1,0:T(8,128)(2,1)} custom-call(s32[5]{0:T(128)S(1)} %stack.27.where, bf16[4,288,256]{2,1,0:T(8,128)(2,1)S(1)} %bitcast.16, bf16[4,288,256]{2,1,0:T(8,128)(2,1)S(1)} %collective-permute-done.up, bf16[4,288,256]{2,1,0:T(8,128)(2,1)S(1)} %collective-permute-done.1.down), custom_call_target="tpu_custom_call" | custom-call | bytes 3538944 | tf_op jit(solution)/shard_map/split/pallas_call | solution.py:302
  84.7 4.8 %all-to-all-start.1 = ((bf16[4,288,768]{2,1,0:T(8,128)(2,1)}), bf16[4,288,768]{2,1,0:T(8,128)(2,1)S(1)}, u32[]{:S(2)}, u32[]{:S(2)}) async-start(bf16[4,288,768]{2,1,0:T(8,128)(2,1)} %split.1), calls=%async_computation.1 | async-start | bytes 3538944 | tf_op jit(solution)/shard_map/all_to_all | solution.py:311
  89.5 0.0 collective-permute-done.2
  89.5 0.0 copy-start
  89.5 5.8 %project.1 = (f32[288,384]{1,0:T(8,128)S(1)}, f32[288,384]{1,0:T(8,128)S(1)}) custom-call(s32[5]{0:T(128)S(1)} %stack.27.where, bf16[4,288,256]{2,1,0:T(8,128)(2,1)S(1)} %bitcast.17, bf16[4,288,256]{2,1,0:T(8,128)(2,1)S(1)} %collective-permute-done.up, bf16[4,288,256]{2,1,0:T(8,128)(2,1)S(1)} %collective-permute-done.1.down, ...), custom_call_target="tpu_custom_call" | custom-call | flops 1358954496 | bytes 9437184 | tf_op jit(solution)/shard_map/project/pallas_call | solution.py:284
  95.3 3.9 %collective-permute-start.3 = (f32[288,384]{1,0:T(8,128)S(1)}, f32[288,384]{1,0:T(8,128)S(1)}, u32[]{:S(2)}, u32[]{:S(2)}) collective-permute-start(f32[288,384]{1,0:T(8,128)S(1)} %get-tuple-element.12), channel_id=1, source_target_pairs={{0,1},{1,0},{2,3},{3,2},{4,5},{5,4},{6,7},{7,6},{8,9},{9,8},{10,11... | collective-permute-start | bytes 1327112 | tf_op jit(solution)/shard_map/ppermute | solution.py:274
  99.3 1.4 collective-permute-done.3.far
  100.7 0.0 copy-done
  100.7 1.7 %attend.1 = (bf16[384,128]{1,0:T(8,128)(2,1)}, bf16[288,384]{1,0:T(8,128)(2,1)S(1)}) custom-call(f32[288,384]{1,0:T(8,128)S(1)} %get-tuple-element.11.own, f32[288,384]{1,0:T(8,128)S(1)} %collective-permute-done.3.far, bf16[384,128]{1,0:T(8,128)(2,1)S(1)} %copy-done, s32[8,128]{1,0:T(8,128)S(1)} %get-tuple-element.13.offsets), custom_call_target="tpu_custom_call" | custom-call | flops 191102976 | bytes 2097152 | tf_op jit(solution)/shard_map/attend/pallas_call | solution.py:312
  102.3 18.4 %all-gather.1 = bf16[1152,384]{1,0:T(8,128)(2,1)S(1)} all-gather(bf16[288,384]{1,0:T(8,128)(2,1)S(1)} %get-tuple-element.15), channel_id=3, replica_groups={{0,24,48,72},{96,120,144,168},{192,216,240,264},{288,312,336,360},{384,..., dimensions={0}, use_global_device_ids=true | all-gather | bytes 1105920 | tf_op jit(solution)/shard_map/all_gather | solution.py:325
  120.8 0.0 all-to-all-done.1.near
  120.8 4.0 %collective-permute-start.4 = (bf16[4,288,768]{2,1,0:T(8,128)(2,1)S(1)}, bf16[4,288,768]{2,1,0:T(8,128)(2,1)S(1)}, u32[]{:S(2)}, u32[]{:S(2)}) collective-permute-start(bf16[4,288,768]{2,1,0:T(8,128)(2,1)S(1)} %all-to-all-done.1.near), channel_id=1, source_target_pairs={{0,1},{1,0},{2,3},{3,2},{4,5},{5,4},{6,7},{7,6},{8,9},{9,8},{10,11... | collective-permute-start | bytes 5308424 | tf_op jit(solution)/shard_map/ppermute | solution.py:274
  124.8 1.2 near.1.near_terms
  126.0 2.1 %collective-permute-done.4.cross = bf16[4,288,768]{2,1,0:T(8,128)(2,1)S(1)} collective-permute-done((bf16[4,288,768]{2,1,0:T(8,128)(2,1)S(1)}, bf16[4,288,768]{2,1,0:T(8,128)(2,1)S(1)}, u32[]{:S(2)}, u32[]{:S(2)}) %collective-permute-start.4) | collective-permute-done | bytes 1769504 | tf_op jit(solution)/shard_map/ppermute | solution.py:274
  128.1 2.8 %weight.1 = bf16[8,192,384]{2,1,0:T(8,128)(2,1)} custom-call(s32[5]{0:T(128)S(1)} %stack.27.where, bf16[2,384,384]{2,1,0:T(8,128)(2,1)S(1)} %near.1.near_terms, bf16[4,288,768]{2,1,0:T(8,128)(2,1)S(1)} %collective-permute-done.4.cross, bf16[4,288,384]{2,1,0:T(8,128)(2,1)S(1)} %bitcast.19), custom_call_target="tpu_custom_call" | custom-call | flops 1358954496 | bytes 6291456 | tf_op jit(solution)/shard_map/weight/pallas_call | solution.py:337
  130.8 3.6 %all-to-all-start.2 = ((bf16[8,192,384]{2,1,0:T(8,128)(2,1)}), bf16[8,192,384]{2,1,0:T(8,128)(2,1)S(1)}, u32[]{:S(2)}, u32[]{:S(2)}) async-start(bf16[8,192,384]{2,1,0:T(8,128)(2,1)} %weight.1), calls=%async_computation.2 | async-start | bytes 2359296 | tf_op jit(solution)/shard_map/all_to_all | solution.py:346
  134.4 29.7 %all-to-all-done.2.terms = bf16[8,192,384]{2,1,0:T(8,128)(2,1)S(1)} async-done(((bf16[8,192,384]{2,1,0:T(8,128)(2,1)}), bf16[8,192,384]{2,1,0:T(8,128)(2,1)S(1)}, u32[]{:S(2)}, u32[]{:S(2)}) %all-to-all-start.2) | async-done | bytes 1179680 | tf_op jit(solution)/shard_map/all_to_all | solution.py:346
  164.1 0.9 sum.1
Async XLA Ops:
  0.6 88.9 %collective-permute-start.2 = (bf16[6144,384]{1,0:T(8,128)(2,1)}, bf16[6144,384]{1,0:T(8,128)(2,1)}, u32[]{:S(2)}, u32[]{:S(2)}) collective-permute-start(bf16[6144,384]{1,0:T(8,128)(2,1)} %param.8), channel_id=1, source_target_pairs={{0,1},{1,0},{2,3},{3,2},{4,5},{5,4},{6,7},{7,6},{8,9},{9,8},{10,11... | collective-permute-start | bytes 14155784 | tf_op jit(solution)/shard_map/ppermute | solution.py:274
  61.0 17.7 %collective-permute-start = (bf16[4,288,256]{2,1,0:T(8,128)(2,1)S(1)}, bf16[4,288,256]{2,1,0:T(8,128)(2,1)S(1)}, u32[]{:S(2)}, u32[]{:S(2)}) collective-permute-start(bf16[4,288,256]{2,1,0:T(8,128)(2,1)S(1)} %bitcast.14), channel_id=1, source_target_pairs={{0,2},{1,3},{2,4},{3,5},{4,6},{5,7},{6,8},{7,9},{8,10},{9,11},{10,... | collective-permute-start | bytes 1769480 | tf_op jit(solution)/shard_map/ppermute | solution.py:271
  66.9 15.4 %collective-permute-start.1 = (bf16[4,288,256]{2,1,0:T(8,128)(2,1)S(1)}, bf16[4,288,256]{2,1,0:T(8,128)(2,1)S(1)}, u32[]{:S(2)}, u32[]{:S(2)}) collective-permute-start(bf16[4,288,256]{2,1,0:T(8,128)(2,1)S(1)} %bitcast.15), channel_id=1, source_target_pairs={{0,22},{1,23},{2,0},{3,1},{4,2},{5,3},{6,4},{7,5},{8,6},{9,7},{10,... | collective-permute-start | bytes 1769480 | tf_op jit(solution)/shard_map/ppermute | solution.py:271
  84.7 36.1 %all-to-all-start.1 = ((bf16[4,288,768]{2,1,0:T(8,128)(2,1)}), bf16[4,288,768]{2,1,0:T(8,128)(2,1)S(1)}, u32[]{:S(2)}, u32[]{:S(2)}) async-start(bf16[4,288,768]{2,1,0:T(8,128)(2,1)} %split.1), calls=%async_computation.1 | async-start | bytes 3538944 | tf_op jit(solution)/shard_map/all_to_all | solution.py:311
  89.5 11.2 %copy-start = (bf16[384,128]{1,0:T(8,128)(2,1)S(1)}, bf16[384,128]{1,0:T(8,128)(2,1)}, u32[]{:S(2)}) copy-start(bf16[384,128]{1,0:T(8,128)(2,1)} %cotangent.1) | copy-start | bytes 294916
  95.3 5.3 %collective-permute-start.3 = (f32[288,384]{1,0:T(8,128)S(1)}, f32[288,384]{1,0:T(8,128)S(1)}, u32[]{:S(2)}, u32[]{:S(2)}) collective-permute-start(f32[288,384]{1,0:T(8,128)S(1)} %get-tuple-element.12), channel_id=1, source_target_pairs={{0,1},{1,0},{2,3},{3,2},{4,5},{5,4},{6,7},{7,6},{8,9},{9,8},{10,11... | collective-permute-start | bytes 1327112 | tf_op jit(solution)/shard_map/ppermute | solution.py:274
  120.8 7.3 %collective-permute-start.4 = (bf16[4,288,768]{2,1,0:T(8,128)(2,1)S(1)}, bf16[4,288,768]{2,1,0:T(8,128)(2,1)S(1)}, u32[]{:S(2)}, u32[]{:S(2)}) collective-permute-start(bf16[4,288,768]{2,1,0:T(8,128)(2,1)S(1)} %all-to-all-done.1.near), channel_id=1, source_target_pairs={{0,1},{1,0},{2,3},{3,2},{4,5},{5,4},{6,7},{7,6},{8,9},{9,8},{10,11... | collective-permute-start | bytes 5308424 | tf_op jit(solution)/shard_map/ppermute | solution.py:274
  130.8 33.2 %all-to-all-start.2 = ((bf16[8,192,384]{2,1,0:T(8,128)(2,1)}), bf16[8,192,384]{2,1,0:T(8,128)(2,1)S(1)}, u32[]{:S(2)}, u32[]{:S(2)}) async-start(bf16[8,192,384]{2,1,0:T(8,128)(2,1)} %weight.1), calls=%async_computation.2 | async-start | bytes 2359296 | tf_op jit(solution)/shard_map/all_to_all | solution.py:346

commit v7 on v6

--- a/solution.py
+++ b/solution.py
@@ -159,12 +159,10 @@
             return held[t // 2][group, :, (t % 2) * 128 : (t % 2) * 128 + 128]
 
         for x, (whole, cut) in enumerate(picks):
-            for a in range(2):
-                at = a * 384
-                out[x, :, at : at + 128] = tile(2 * a, whole)
-                out[x, :, at + 128 : at + 256] = tile(2 * a + 1, whole)
-                both = jnp.concatenate([tile(2 * a, cut), tile(2 * a + 1, cut)], axis=1)
-                out[x, :, at + 256 : at + 384] = mm(both, (low, high)[x % 2]).astype(BF16)
+            out[x, :, 0:128] = tile(0, whole)
+            out[x, :, 128:256] = tile(1, whole)
+            both = jnp.concatenate([tile(0, cut), tile(1, cut)], axis=1)
+            out[x, :, 256:384] = mm(both, (low, high)[x % 2]).astype(BF16)
 
     for side, picks in enumerate(PICKS):
         for turn, held in enumerate(by_turn(base, up, down)):
@@ -186,14 +184,11 @@
 
 
 def weight_kernel(where, near_terms, cross, grads, out):
-    for source, side in ((0, where[0]), (1, 1 - where[0])):
+    for term, side in ((near_terms[0], where[0]), (term_of(cross, grads, 0), 1 - where[0])):
         whole_side = jnp.where(where[4] == 1, 1 - side, side)
-        for a in range(2):
-            term = term_of(cross, grads, a) if source else near_terms[a]
-            for b in range(2):
-                group = 2 * a + b
-                out[2 * group + whole_side, 0:128] = term[b * 128 : b * 128 + 128]
-                out[2 * group + side, 128:192] = term[256 + b * 64 : 320 + b * 64]
+        for b in range(2):
+            out[2 * b + whole_side, 0:128] = term[b * 128 : b * 128 + 128]
+            out[2 * b + side, 128:192] = term[256 + b * 64 : 320 + b * 64]
 
 
 def sum_kernel(odd, terms, out):
@@ -299,11 +294,16 @@
         far_weight.reshape(steps, 3, 2, width, cols),
     )
     own_far = swap(far)
+    pair = pl.BlockSpec((2, rows, width), lambda a, where: (a, 0, 0))
     outbound = pl.pallas_call(
         split_kernel,
+        grid_spec=pltpu.PrefetchScalarGridSpec(
+            num_scalar_prefetch=1,
+            grid=(2,),
+            in_specs=[pair] * 3,
+            out_specs=pl.BlockSpec((X, rows, 384), lambda a, where: (0, 0, a)),
+        ),
         out_shape=jax.ShapeDtypeStruct((X, rows, 768), BF16),
-        in_specs=[SMEM] + [VMEM] * 3,
-        out_specs=VMEM,
         compiler_params=params(),
         cost_estimate=cost(0, 4 * rows * 768 * 4),
         name="split",
@@ -336,11 +336,19 @@
     )(near, all_grads)
     terms = pl.pallas_call(
         weight_kernel,
+        grid_spec=pltpu.PrefetchScalarGridSpec(
+            num_scalar_prefetch=1,
+            grid=(2,),
+            in_specs=[
+                pl.BlockSpec((1, 384, cols), lambda a, where: (a, 0, 0)),
+                pl.BlockSpec((X, rows, 384), lambda a, where: (0, 0, a)),
+                pl.BlockSpec((X, rows, cols), lambda a, where: (0, 0, 0)),
+            ],
+            out_specs=pl.BlockSpec((4, 192, cols), lambda a, where: (a, 0, 0)),
+        ),
         out_shape=jax.ShapeDtypeStruct((Y, 192, cols), BF16),
-        in_specs=[SMEM] + [VMEM] * 3,
-        out_specs=VMEM,
-        compiler_params=params(),
-        cost_estimate=cost(2 * 4 * rows * 1536 * cols, 6 * 1024 * 1024),
+        compiler_params=params(),
+        cost_estimate=cost(4 * rows * 1536 * cols, 6 * 1024 * 1024),
         name="weight",
     )(where, near_terms, cross, all_grads)
     gathered = lax.all_to_all(terms, "dp", 0, 0, axis_index_groups=along_y, tiled=True)

time: 166 us -> 166 us (level)
  no operation moved by 1% of the time
where the time goes in v7:
time: 166 us; the launch traced here: 165 us
  blocking collectives  62.2 us (37%)
  waiting for transfers between devices  46.4 us (28%)
  starting transfers between devices  36.5 us (22%)
  Pallas kernels  19.1 us (12%)
    all_to_all x1, waiting for transfers between devices, shards(): lax.all_to_all(terms, 'dp', 0, 0, axis_index_groups=along_y, tiled=True)  29.6 us
    all_gather x1, blocking collectives, shards(): base = lax.all_gather(compact, 'mp', axis=0, axis_index_groups=thirds)  25.3 us
    ppermute x3, starting transfers between devices, swap(): return lax.ppermute(block, 'mp', [(k, k ^ 1) for k in range(heads)])  20.4 us
    all_to_all x1, blocking collectives, shards(): lax.all_to_all(outgoing.reshape(owners, ROOM, width), 'dp', 0, 0, tiled=T...  18.4 us
    all_gather x1, blocking collectives, shards(): all_grads = lax.all_gather(grads, 'dp', axis=0, axis_index_groups=along_x)  18.4 us
    ppermute x2, waiting for transfers between devices, shift(): lax.ppermute(block, 'mp', [(k, (k + by) % heads) for k in range(heads)])  13.3 us
    ppermute x2, starting transfers between devices, shift(): lax.ppermute(block, 'mp', [(k, (k + by) % heads) for k in range(heads)])  7.81 us
    pallas_call x1, Pallas kernels, shards(): pl.pallas_call(project_kernel, grid_spec=pltpu.PrefetchScalarGridSpec(num...  5.81 us
  transfers between devices with their start and end apart: 7, of which 5 were waited for; matrix products, arithmetic and copies ran while one was open for 0% of the time, Pallas kernels for 7%

profile of v7, /device:TPU:1, one launch (start us, length us, event | category | flops | bytes accessed | tf_op | source)
XLA Modules:
  0.0 165.2 jit_solution(523508217734275293)
XLA Ops:
  0.6 12.4 %collective-permute-start.2 = (bf16[6144,384]{1,0:T(8,128)(2,1)}, bf16[6144,384]{1,0:T(8,128)(2,1)}, u32[]{:S(2)}, u32[]{:S(2)}) collective-permute-start(bf16[6144,384]{1,0:T(8,128)(2,1)} %param.8), channel_id=1, source_target_pairs={{0,1},{1,0},{2,3},{3,2},{4,5},{5,4},{6,7},{7,6},{8,9},{9,8},{10,11... | collective-permute-start | bytes 14155784 | tf_op jit(solution)/shard_map/ppermute | solution.py:269
  13.1 3.0 %send.1 = bf16[768,256]{1,0:T(8,128)(2,1)} custom-call(bf16[288,256]{1,0:T(8,128)(2,1)} %patches_in.1, s32[1,288]{1,0:T(1,128)} %bitcast.23, s32[1,288]{1,0:T(1,128)} %bitcast.24), custom_call_target="tpu_custom_call" | custom-call | tf_op jit(solution)/shard_map/send/pallas_call | solution.py:236
  16.0 18.4 %all_to_all.15 = bf16[32,24,256]{2,1,0:T(8,128)(2,1)S(1)} all-to-all(bf16[32,24,256]{2,1,0:T(8,128)(2,1)} %bitcast.22), channel_id=1, replica_groups=mesh['dp'=32,'mp'=24] {'dp'}, dimensions={0} | all-to-all | bytes 786432 | tf_op jit(solution)/shard_map/all_to_all | solution.py:250
  34.5 1.2 receive.1
  35.7 25.3 %all-gather = bf16[1152,256]{1,0:T(8,128)(2,1)S(1)} all-gather(bf16[288,256]{1,0:T(8,128)(2,1)S(1)} %get-tuple-element.10), channel_id=2, replica_groups={{0,6,12,18},{1,7,13,19},{2,8,14,20},{3,9,15,21},{4,10,16,22},{5,11,17,2..., dimensions={0}, use_global_device_ids=true | all-gather | bytes 737280 | tf_op jit(solution)/shard_map/all_gather | solution.py:272
  61.0 5.9 %collective-permute-start = (bf16[4,288,256]{2,1,0:T(8,128)(2,1)S(1)}, bf16[4,288,256]{2,1,0:T(8,128)(2,1)S(1)}, u32[]{:S(2)}, u32[]{:S(2)}) collective-permute-start(bf16[4,288,256]{2,1,0:T(8,128)(2,1)S(1)} %bitcast.16), channel_id=1, source_target_pairs={{0,2},{1,3},{2,4},{3,5},{4,6},{5,7},{6,8},{7,9},{8,10},{9,11},{10,... | collective-permute-start | bytes 1769480 | tf_op jit(solution)/shard_map/ppermute | solution.py:266
  66.9 1.9 %collective-permute-start.1 = (bf16[4,288,256]{2,1,0:T(8,128)(2,1)S(1)}, bf16[4,288,256]{2,1,0:T(8,128)(2,1)S(1)}, u32[]{:S(2)}, u32[]{:S(2)}) collective-permute-start(bf16[4,288,256]{2,1,0:T(8,128)(2,1)S(1)} %bitcast.17), channel_id=1, source_target_pairs={{0,22},{1,23},{2,0},{3,1},{4,2},{5,3},{6,4},{7,5},{8,6},{9,7},{10,... | collective-permute-start | bytes 1769480 | tf_op jit(solution)/shard_map/ppermute | solution.py:266
  68.9 0.1 stack.27.where
  69.0 9.7 %collective-permute-done.up = bf16[4,288,256]{2,1,0:T(8,128)(2,1)S(1)} collective-permute-done((bf16[4,288,256]{2,1,0:T(8,128)(2,1)S(1)}, bf16[4,288,256]{2,1,0:T(8,128)(2,1)S(1)}, u32[]{:S(2)}, u32[]{:S(2)}) %collective-permute-start) | collective-permute-done | bytes 589856 | tf_op jit(solution)/shard_map/ppermute | solution.py:266
  78.7 3.6 %collective-permute-done.1.down = bf16[4,288,256]{2,1,0:T(8,128)(2,1)S(1)} collective-permute-done((bf16[4,288,256]{2,1,0:T(8,128)(2,1)S(1)}, bf16[4,288,256]{2,1,0:T(8,128)(2,1)S(1)}, u32[]{:S(2)}, u32[]{:S(2)}) %collective-permute-start.1) | collective-permute-done | bytes 589856 | tf_op jit(solution)/shard_map/ppermute | solution.py:266
  82.3 2.4 %split.1 = bf16[4,288,768]{2,1,0:T(8,128)(2,1)} custom-call(s32[5]{0:T(128)S(1)} %stack.27.where, bf16[4,288,256]{2,1,0:T(8,128)(2,1)S(1)} %bitcast.18, bf16[4,288,256]{2,1,0:T(8,128)(2,1)S(1)} %collective-permute-done.up, bf16[4,288,256]{2,1,0:T(8,128)(2,1)S(1)} %collective-permute-done.1.down), custom_call_target="tpu_custom_call" | custom-call | bytes 3538944 | tf_op jit(solution)/shard_map/split/pallas_call | solution.py:298
  84.7 4.8 %all-to-all-start.1 = ((bf16[4,288,768]{2,1,0:T(8,128)(2,1)}), bf16[4,288,768]{2,1,0:T(8,128)(2,1)S(1)}, u32[]{:S(2)}, u32[]{:S(2)}) async-start(bf16[4,288,768]{2,1,0:T(8,128)(2,1)} %split.1), calls=%async_computation.1 | async-start | bytes 3538944 | tf_op jit(solution)/shard_map/all_to_all | solution.py:311
  89.5 0.0 collective-permute-done.2
  89.5 0.0 copy-start
  89.5 5.8 %project.1 = (f32[288,384]{1,0:T(8,128)S(1)}, f32[288,384]{1,0:T(8,128)S(1)}) custom-call(s32[5]{0:T(128)S(1)} %stack.27.where, bf16[4,288,256]{2,1,0:T(8,128)(2,1)S(1)} %bitcast.19, bf16[4,288,256]{2,1,0:T(8,128)(2,1)S(1)} %collective-permute-done.up, bf16[4,288,256]{2,1,0:T(8,128)(2,1)S(1)} %collective-permute-done.1.down, ...), custom_call_target="tpu_custom_call" | custom-call | flops 1358954496 | bytes 9437184 | tf_op jit(solution)/shard_map/project/pallas_call | solution.py:279
  95.3 3.9 %collective-permute-start.3 = (f32[288,384]{1,0:T(8,128)S(1)}, f32[288,384]{1,0:T(8,128)S(1)}, u32[]{:S(2)}, u32[]{:S(2)}) collective-permute-start(f32[288,384]{1,0:T(8,128)S(1)} %get-tuple-element.12), channel_id=1, source_target_pairs={{0,1},{1,0},{2,3},{3,2},{4,5},{5,4},{6,7},{7,6},{8,9},{9,8},{10,11... | collective-permute-start | bytes 1327112 | tf_op jit(solution)/shard_map/ppermute | solution.py:269
  99.2 1.4 collective-permute-done.3.far
  100.6 0.0 copy-done
  100.6 1.7 %attend.1 = (bf16[384,128]{1,0:T(8,128)(2,1)}, bf16[288,384]{1,0:T(8,128)(2,1)S(1)}) custom-call(f32[288,384]{1,0:T(8,128)S(1)} %get-tuple-element.11.own, f32[288,384]{1,0:T(8,128)S(1)} %collective-permute-done.3.far, bf16[384,128]{1,0:T(8,128)(2,1)S(1)} %copy-done, s32[8,128]{1,0:T(8,128)S(1)} %get-tuple-element.13.offsets), custom_call_target="tpu_custom_call" | custom-call | flops 191102976 | bytes 2097152 | tf_op jit(solution)/shard_map/attend/pallas_call | solution.py:312
  102.3 18.4 %all-gather.1 = bf16[1152,384]{1,0:T(8,128)(2,1)S(1)} all-gather(bf16[288,384]{1,0:T(8,128)(2,1)S(1)} %get-tuple-element.15), channel_id=3, replica_groups={{0,24,48,72},{96,120,144,168},{192,216,240,264},{288,312,336,360},{384,..., dimensions={0}, use_global_device_ids=true | all-gather | bytes 1105920 | tf_op jit(solution)/shard_map/all_gather | solution.py:325
  120.8 0.0 all-to-all-done.1.near
  120.8 4.0 %collective-permute-start.4 = (bf16[4,288,768]{2,1,0:T(8,128)(2,1)S(1)}, bf16[4,288,768]{2,1,0:T(8,128)(2,1)S(1)}, u32[]{:S(2)}, u32[]{:S(2)}) collective-permute-start(bf16[4,288,768]{2,1,0:T(8,128)(2,1)S(1)} %all-to-all-done.1.near), channel_id=1, source_target_pairs={{0,1},{1,0},{2,3},{3,2},{4,5},{5,4},{6,7},{7,6},{8,9},{9,8},{10,11... | collective-permute-start | bytes 5308424 | tf_op jit(solution)/shard_map/ppermute | solution.py:269
  124.8 1.2 near.1.near_terms
  125.9 2.1 %collective-permute-done.4.cross = bf16[4,288,768]{2,1,0:T(8,128)(2,1)S(1)} collective-permute-done((bf16[4,288,768]{2,1,0:T(8,128)(2,1)S(1)}, bf16[4,288,768]{2,1,0:T(8,128)(2,1)S(1)}, u32[]{:S(2)}, u32[]{:S(2)}) %collective-permute-start.4) | collective-permute-done | bytes 1769504 | tf_op jit(solution)/shard_map/ppermute | solution.py:269
  128.1 3.0 %weight.1 = bf16[8,192,384]{2,1,0:T(8,128)(2,1)} custom-call(s32[5]{0:T(128)S(1)} %stack.27.where, bf16[2,384,384]{2,1,0:T(8,128)(2,1)S(1)} %near.1.near_terms, bf16[4,288,768]{2,1,0:T(8,128)(2,1)S(1)} %collective-permute-done.4.cross, bf16[4,288,384]{2,1,0:T(8,128)(2,1)S(1)} %bitcast.15), custom_call_target="tpu_custom_call" | custom-call | flops 679477248 | bytes 6291456 | tf_op jit(solution)/shard_map/weight/pallas_call | solution.py:337
  131.0 3.6 %all-to-all-start.2 = ((bf16[8,192,384]{2,1,0:T(8,128)(2,1)}), bf16[8,192,384]{2,1,0:T(8,128)(2,1)S(1)}, u32[]{:S(2)}, u32[]{:S(2)}) async-start(bf16[8,192,384]{2,1,0:T(8,128)(2,1)} %weight.1), calls=%async_computation.2 | async-start | bytes 2359296 | tf_op jit(solution)/shard_map/all_to_all | solution.py:354
  134.6 29.6 %all-to-all-done.2.terms = bf16[8,192,384]{2,1,0:T(8,128)(2,1)S(1)} async-done(((bf16[8,192,384]{2,1,0:T(8,128)(2,1)}), bf16[8,192,384]{2,1,0:T(8,128)(2,1)S(1)}, u32[]{:S(2)}, u32[]{:S(2)}) %all-to-all-start.2) | async-done | bytes 1179680 | tf_op jit(solution)/shard_map/all_to_all | solution.py:354
  164.2 0.9 sum.1
Async XLA Ops:
  0.6 88.9 %collective-permute-start.2 = (bf16[6144,384]{1,0:T(8,128)(2,1)}, bf16[6144,384]{1,0:T(8,128)(2,1)}, u32[]{:S(2)}, u32[]{:S(2)}) collective-permute-start(bf16[6144,384]{1,0:T(8,128)(2,1)} %param.8), channel_id=1, source_target_pairs={{0,1},{1,0},{2,3},{3,2},{4,5},{5,4},{6,7},{7,6},{8,9},{9,8},{10,11... | collective-permute-start | bytes 14155784 | tf_op jit(solution)/shard_map/ppermute | solution.py:269
  61.0 17.7 %collective-permute-start = (bf16[4,288,256]{2,1,0:T(8,128)(2,1)S(1)}, bf16[4,288,256]{2,1,0:T(8,128)(2,1)S(1)}, u32[]{:S(2)}, u32[]{:S(2)}) collective-permute-start(bf16[4,288,256]{2,1,0:T(8,128)(2,1)S(1)} %bitcast.16), channel_id=1, source_target_pairs={{0,2},{1,3},{2,4},{3,5},{4,6},{5,7},{6,8},{7,9},{8,10},{9,11},{10,... | collective-permute-start | bytes 1769480 | tf_op jit(solution)/shard_map/ppermute | solution.py:266
  66.9 15.4 %collective-permute-start.1 = (bf16[4,288,256]{2,1,0:T(8,128)(2,1)S(1)}, bf16[4,288,256]{2,1,0:T(8,128)(2,1)S(1)}, u32[]{:S(2)}, u32[]{:S(2)}) collective-permute-start(bf16[4,288,256]{2,1,0:T(8,128)(2,1)S(1)} %bitcast.17), channel_id=1, source_target_pairs={{0,22},{1,23},{2,0},{3,1},{4,2},{5,3},{6,4},{7,5},{8,6},{9,7},{10,... | collective-permute-start | bytes 1769480 | tf_op jit(solution)/shard_map/ppermute | solution.py:266
  84.7 36.1 %all-to-all-start.1 = ((bf16[4,288,768]{2,1,0:T(8,128)(2,1)}), bf16[4,288,768]{2,1,0:T(8,128)(2,1)S(1)}, u32[]{:S(2)}, u32[]{:S(2)}) async-start(bf16[4,288,768]{2,1,0:T(8,128)(2,1)} %split.1), calls=%async_computation.1 | async-start | bytes 3538944 | tf_op jit(solution)/shard_map/all_to_all | solution.py:311
  89.5 11.2 %copy-start = (bf16[384,128]{1,0:T(8,128)(2,1)S(1)}, bf16[384,128]{1,0:T(8,128)(2,1)}, u32[]{:S(2)}) copy-start(bf16[384,128]{1,0:T(8,128)(2,1)} %cotangent.1) | copy-start | bytes 294916
  95.3 5.3 %collective-permute-start.3 = (f32[288,384]{1,0:T(8,128)S(1)}, f32[288,384]{1,0:T(8,128)S(1)}, u32[]{:S(2)}, u32[]{:S(2)}) collective-permute-start(f32[288,384]{1,0:T(8,128)S(1)} %get-tuple-element.12), channel_id=1, source_target_pairs={{0,1},{1,0},{2,3},{3,2},{4,5},{5,4},{6,7},{7,6},{8,9},{9,8},{10,11... | collective-permute-start | bytes 1327112 | tf_op jit(solution)/shard_map/ppermute | solution.py:269
  120.8 7.3 %collective-permute-start.4 = (bf16[4,288,768]{2,1,0:T(8,128)(2,1)S(1)}, bf16[4,288,768]{2,1,0:T(8,128)(2,1)S(1)}, u32[]{:S(2)}, u32[]{:S(2)}) collective-permute-start(bf16[4,288,768]{2,1,0:T(8,128)(2,1)S(1)} %all-to-all-done.1.near), channel_id=1, source_target_pairs={{0,1},{1,0},{2,3},{3,2},{4,5},{5,4},{6,7},{7,6},{8,9},{9,8},{10,11... | collective-permute-start | bytes 5308424 | tf_op jit(solution)/shard_map/ppermute | solution.py:269
  131.0 33.2 %all-to-all-start.2 = ((bf16[8,192,384]{2,1,0:T(8,128)(2,1)}), bf16[8,192,384]{2,1,0:T(8,128)(2,1)S(1)}, u32[]{:S(2)}, u32[]{:S(2)}) async-start(bf16[8,192,384]{2,1,0:T(8,128)(2,1)} %weight.1), calls=%async_computation.2 | async-start | bytes 2359296 | tf_op jit(solution)/shard_map/all_to_all | solution.py:354

commit v8 on v6

--- a/solution.py
+++ b/solution.py
@@ -100,16 +100,15 @@
     return ((base, down, up), (up, base, down), (down, up, base))
 
 
-def project_kernel(where, base, up, down, weight, far_weight, own, far):
+def project_kernel(where, base, up, down, *refs):
+    own, far = refs[6:]
     step = pl.program_id(0)
-    depth = 3 * base.shape[2]
     for turn, held in enumerate(by_turn(base, up, down)):
 
         @pl.when(where[1] == turn)
         def _(held=held):
-            left = jnp.concatenate([part[0] for part in held], axis=1)
-            for block, out in ((weight, own), (far_weight, far)):
-                term = mm(left, block[0, :, 0].reshape(depth, out.shape[1]))
+            for blocks, out in ((refs[:3], own), (refs[3:6], far)):
+                term = sum(mm(part[0], block[0, 0, 0]) for part, block in zip(held, blocks))
 
                 @pl.when(step == 0)
                 def _(term=term, out=out):
@@ -279,14 +278,17 @@
 
     steps = heads // 6
     block = pl.BlockSpec((1, rows, width), lambda k, where: (k, 0, 0))
-    weight_block = pl.BlockSpec((1, 3, 1, width, cols), lambda k, where: (k, 0, where[0], 0, 0))
+    weight_blocks = [
+        pl.BlockSpec((1, 1, 1, width, cols), lambda k, where, t=t: (k, t, where[0], 0, 0))
+        for t in range(3)
+    ]
     result = pl.BlockSpec((rows, cols), lambda k, where: (0, 0))
     own, far = pl.pallas_call(
         project_kernel,
         grid_spec=pltpu.PrefetchScalarGridSpec(
             num_scalar_prefetch=1,
             grid=(steps,),
-            in_specs=[block] * 3 + [weight_block] * 2,
+            in_specs=[block] * 3 + weight_blocks * 2,
             out_specs=(result, result),
         ),
         out_shape=(jax.ShapeDtypeStruct((rows, cols), F32),) * 2,
@@ -295,8 +297,8 @@
         name="project",
     )(
         where, base, up, down,
-        project_weight.reshape(steps, 3, 2, width, cols),
-        far_weight.reshape(steps, 3, 2, width, cols),
+        *[project_weight.reshape(steps, 3, 2, width, cols)] * 3,
+        *[far_weight.reshape(steps, 3, 2, width, cols)] * 3,
     )
     own_far = swap(far)
     outbound = pl.pallas_call(

time: 166 us -> 166 us (level)
  transfers between devices with their start and end apart: 7 -> 7, of which waited for: 5 -> 5; matrix products, arithmetic and copies ran while one was open for 0% -> 0% of each run, Pallas kernels for 7% -> 8%
where the time goes in v8:
time: 166 us; the launch traced here: 165 us
  blocking collectives  62 us (37%)
  waiting for transfers between devices  46.4 us (28%)
  starting transfers between devices  36.5 us (22%)
  Pallas kernels  19.1 us (12%)
    all_to_all x1, waiting for transfers between devices, shards(): lax.all_to_all(terms, 'dp', 0, 0, axis_index_groups=along_y, tiled=True)  29.7 us
    all_gather x1, blocking collectives, shards(): base = lax.all_gather(compact, 'mp', axis=0, axis_index_groups=thirds)  25.3 us
    ppermute x3, starting transfers between devices, swap(): return lax.ppermute(block, 'mp', [(k, k ^ 1) for k in range(heads)])  20.4 us
    all_to_all x1, blocking collectives, shards(): lax.all_to_all(outgoing.reshape(owners, ROOM, width), 'dp', 0, 0, tiled=T...  18.4 us
    all_gather x1, blocking collectives, shards(): all_grads = lax.all_gather(grads, 'dp', axis=0, axis_index_groups=along_x)  18.2 us
    ppermute x2, waiting for transfers between devices, shift(): lax.ppermute(block, 'mp', [(k, (k + by) % heads) for k in range(heads)])  13.3 us
    ppermute x2, starting transfers between devices, shift(): lax.ppermute(block, 'mp', [(k, (k + by) % heads) for k in range(heads)])  7.81 us
    pallas_call x1, Pallas kernels, shards(): pl.pallas_call(project_kernel, grid_spec=pltpu.PrefetchScalarGridSpec(num...  6 us
  transfers between devices with their start and end apart: 7, of which 5 were waited for; matrix products, arithmetic and copies ran while one was open for 0% of the time, Pallas kernels for 8%

profile of v8, /device:TPU:1, one launch (start us, length us, event | category | flops | bytes accessed | tf_op | source)
XLA Modules:
  0.0 165.0 jit_solution(8313028861192890162)
XLA Ops:
  0.6 12.4 %collective-permute-start.2 = (bf16[6144,384]{1,0:T(8,128)(2,1)}, bf16[6144,384]{1,0:T(8,128)(2,1)}, u32[]{:S(2)}, u32[]{:S(2)}) collective-permute-start(bf16[6144,384]{1,0:T(8,128)(2,1)} %param.8), channel_id=1, source_target_pairs={{0,1},{1,0},{2,3},{3,2},{4,5},{5,4},{6,7},{7,6},{8,9},{9,8},{10,11... | collective-permute-start | bytes 14155784 | tf_op jit(solution)/shard_map/ppermute | solution.py:273
  13.1 3.0 %send.1 = bf16[768,256]{1,0:T(8,128)(2,1)} custom-call(bf16[288,256]{1,0:T(8,128)(2,1)} %patches_in.1, s32[1,288]{1,0:T(1,128)} %bitcast.25, s32[1,288]{1,0:T(1,128)} %bitcast.26), custom_call_target="tpu_custom_call" | custom-call | tf_op jit(solution)/shard_map/send/pallas_call | solution.py:240
  16.0 18.4 %all_to_all.15 = bf16[32,24,256]{2,1,0:T(8,128)(2,1)S(1)} all-to-all(bf16[32,24,256]{2,1,0:T(8,128)(2,1)} %bitcast.24), channel_id=1, replica_groups=mesh['dp'=32,'mp'=24] {'dp'}, dimensions={0} | all-to-all | bytes 786432 | tf_op jit(solution)/shard_map/all_to_all | solution.py:254
  34.5 1.2 receive.1
  35.7 25.3 %all-gather = bf16[1152,256]{1,0:T(8,128)(2,1)S(1)} all-gather(bf16[288,256]{1,0:T(8,128)(2,1)S(1)} %get-tuple-element.10), channel_id=2, replica_groups={{0,6,12,18},{1,7,13,19},{2,8,14,20},{3,9,15,21},{4,10,16,22},{5,11,17,2..., dimensions={0}, use_global_device_ids=true | all-gather | bytes 737280 | tf_op jit(solution)/shard_map/all_gather | solution.py:276
  61.0 5.9 %collective-permute-start = (bf16[4,288,256]{2,1,0:T(8,128)(2,1)S(1)}, bf16[4,288,256]{2,1,0:T(8,128)(2,1)S(1)}, u32[]{:S(2)}, u32[]{:S(2)}) collective-permute-start(bf16[4,288,256]{2,1,0:T(8,128)(2,1)S(1)} %bitcast.14), channel_id=1, source_target_pairs={{0,2},{1,3},{2,4},{3,5},{4,6},{5,7},{6,8},{7,9},{8,10},{9,11},{10,... | collective-permute-start | bytes 1769480 | tf_op jit(solution)/shard_map/ppermute | solution.py:270
  66.9 1.9 %collective-permute-start.1 = (bf16[4,288,256]{2,1,0:T(8,128)(2,1)S(1)}, bf16[4,288,256]{2,1,0:T(8,128)(2,1)S(1)}, u32[]{:S(2)}, u32[]{:S(2)}) collective-permute-start(bf16[4,288,256]{2,1,0:T(8,128)(2,1)S(1)} %bitcast.15), channel_id=1, source_target_pairs={{0,22},{1,23},{2,0},{3,1},{4,2},{5,3},{6,4},{7,5},{8,6},{9,7},{10,... | collective-permute-start | bytes 1769480 | tf_op jit(solution)/shard_map/ppermute | solution.py:270
  68.9 0.1 stack.27.where
  69.0 9.7 %collective-permute-done.up = bf16[4,288,256]{2,1,0:T(8,128)(2,1)S(1)} collective-permute-done((bf16[4,288,256]{2,1,0:T(8,128)(2,1)S(1)}, bf16[4,288,256]{2,1,0:T(8,128)(2,1)S(1)}, u32[]{:S(2)}, u32[]{:S(2)}) %collective-permute-start) | collective-permute-done | bytes 589856 | tf_op jit(solution)/shard_map/ppermute | solution.py:270
  78.7 3.6 %collective-permute-done.1.down = bf16[4,288,256]{2,1,0:T(8,128)(2,1)S(1)} collective-permute-done((bf16[4,288,256]{2,1,0:T(8,128)(2,1)S(1)}, bf16[4,288,256]{2,1,0:T(8,128)(2,1)S(1)}, u32[]{:S(2)}, u32[]{:S(2)}) %collective-permute-start.1) | collective-permute-done | bytes 589856 | tf_op jit(solution)/shard_map/ppermute | solution.py:270
  82.3 2.4 %split.1 = bf16[4,288,768]{2,1,0:T(8,128)(2,1)} custom-call(s32[5]{0:T(128)S(1)} %stack.27.where, bf16[4,288,256]{2,1,0:T(8,128)(2,1)S(1)} %bitcast.16, bf16[4,288,256]{2,1,0:T(8,128)(2,1)S(1)} %collective-permute-done.up, bf16[4,288,256]{2,1,0:T(8,128)(2,1)S(1)} %collective-permute-done.1.down), custom_call_target="tpu_custom_call" | custom-call | bytes 3538944 | tf_op jit(solution)/shard_map/split/pallas_call | solution.py:304
  84.7 4.8 %all-to-all-start.1 = ((bf16[4,288,768]{2,1,0:T(8,128)(2,1)}), bf16[4,288,768]{2,1,0:T(8,128)(2,1)S(1)}, u32[]{:S(2)}, u32[]{:S(2)}) async-start(bf16[4,288,768]{2,1,0:T(8,128)(2,1)} %split.1), calls=%async_computation.1 | async-start | bytes 3538944 | tf_op jit(solution)/shard_map/all_to_all | solution.py:313
  89.5 0.0 collective-permute-done.2
  89.5 0.0 copy-start
  89.5 6.0 %project.1 = (f32[288,384]{1,0:T(8,128)S(1)}, f32[288,384]{1,0:T(8,128)S(1)}) custom-call(s32[5]{0:T(128)S(1)} %stack.27.where, bf16[4,288,256]{2,1,0:T(8,128)(2,1)S(1)} %bitcast.17, bf16[4,288,256]{2,1,0:T(8,128)(2,1)S(1)} %collective-permute-done.up, bf16[4,288,256]{2,1,0:T(8,128)(2,1)S(1)} %collective-permute-done.1.down, ...), custom_call_target="tpu_custom_call" | custom-call | flops 1358954496 | bytes 9437184 | tf_op jit(solution)/shard_map/project/pallas_call | solution.py:286
  95.5 3.9 %collective-permute-start.3 = (f32[288,384]{1,0:T(8,128)S(1)}, f32[288,384]{1,0:T(8,128)S(1)}, u32[]{:S(2)}, u32[]{:S(2)}) collective-permute-start(f32[288,384]{1,0:T(8,128)S(1)} %get-tuple-element.12), channel_id=1, source_target_pairs={{0,1},{1,0},{2,3},{3,2},{4,5},{5,4},{6,7},{7,6},{8,9},{9,8},{10,11... | collective-permute-start | bytes 1327112 | tf_op jit(solution)/shard_map/ppermute | solution.py:273
  99.4 1.4 collective-permute-done.3.far
  100.8 0.0 copy-done
  100.8 1.7 %attend.1 = (bf16[384,128]{1,0:T(8,128)(2,1)}, bf16[288,384]{1,0:T(8,128)(2,1)S(1)}) custom-call(f32[288,384]{1,0:T(8,128)S(1)} %get-tuple-element.11.own, f32[288,384]{1,0:T(8,128)S(1)} %collective-permute-done.3.far, bf16[384,128]{1,0:T(8,128)(2,1)S(1)} %copy-done, s32[8,128]{1,0:T(8,128)S(1)} %get-tuple-element.13.offsets), custom_call_target="tpu_custom_call" | custom-call | flops 191102976 | bytes 2097152 | tf_op jit(solution)/shard_map/attend/pallas_call | solution.py:314
  102.5 18.2 %all-gather.1 = bf16[1152,384]{1,0:T(8,128)(2,1)S(1)} all-gather(bf16[288,384]{1,0:T(8,128)(2,1)S(1)} %get-tuple-element.15), channel_id=3, replica_groups={{0,24,48,72},{96,120,144,168},{192,216,240,264},{288,312,336,360},{384,..., dimensions={0}, use_global_device_ids=true | all-gather | bytes 1105920 | tf_op jit(solution)/shard_map/all_gather | solution.py:327
  120.8 0.0 all-to-all-done.1.near
  120.8 4.0 %collective-permute-start.4 = (bf16[4,288,768]{2,1,0:T(8,128)(2,1)S(1)}, bf16[4,288,768]{2,1,0:T(8,128)(2,1)S(1)}, u32[]{:S(2)}, u32[]{:S(2)}) collective-permute-start(bf16[4,288,768]{2,1,0:T(8,128)(2,1)S(1)} %all-to-all-done.1.near), channel_id=1, source_target_pairs={{0,1},{1,0},{2,3},{3,2},{4,5},{5,4},{6,7},{7,6},{8,9},{9,8},{10,11... | collective-permute-start | bytes 5308424 | tf_op jit(solution)/shard_map/ppermute | solution.py:273
  124.8 1.2 near.1.near_terms
  126.0 2.1 %collective-permute-done.4.cross = bf16[4,288,768]{2,1,0:T(8,128)(2,1)S(1)} collective-permute-done((bf16[4,288,768]{2,1,0:T(8,128)(2,1)S(1)}, bf16[4,288,768]{2,1,0:T(8,128)(2,1)S(1)}, u32[]{:S(2)}, u32[]{:S(2)}) %collective-permute-start.4) | collective-permute-done | bytes 1769504 | tf_op jit(solution)/shard_map/ppermute | solution.py:273
  128.1 2.8 %weight.1 = bf16[8,192,384]{2,1,0:T(8,128)(2,1)} custom-call(s32[5]{0:T(128)S(1)} %stack.27.where, bf16[2,384,384]{2,1,0:T(8,128)(2,1)S(1)} %near.1.near_terms, bf16[4,288,768]{2,1,0:T(8,128)(2,1)S(1)} %collective-permute-done.4.cross, bf16[4,288,384]{2,1,0:T(8,128)(2,1)S(1)} %bitcast.19), custom_call_target="tpu_custom_call" | custom-call | flops 1358954496 | bytes 6291456 | tf_op jit(solution)/shard_map/weight/pallas_call | solution.py:339
  130.8 3.6 %all-to-all-start.2 = ((bf16[8,192,384]{2,1,0:T(8,128)(2,1)}), bf16[8,192,384]{2,1,0:T(8,128)(2,1)S(1)}, u32[]{:S(2)}, u32[]{:S(2)}) async-start(bf16[8,192,384]{2,1,0:T(8,128)(2,1)} %weight.1), calls=%async_computation.2 | async-start | bytes 2359296 | tf_op jit(solution)/shard_map/all_to_all | solution.py:348
  134.4 29.7 %all-to-all-done.2.terms = bf16[8,192,384]{2,1,0:T(8,128)(2,1)S(1)} async-done(((bf16[8,192,384]{2,1,0:T(8,128)(2,1)}), bf16[8,192,384]{2,1,0:T(8,128)(2,1)S(1)}, u32[]{:S(2)}, u32[]{:S(2)}) %all-to-all-start.2) | async-done | bytes 1179680 | tf_op jit(solution)/shard_map/all_to_all | solution.py:348
  164.1 0.9 sum.1
Async XLA Ops:
  0.6 88.9 %collective-permute-start.2 = (bf16[6144,384]{1,0:T(8,128)(2,1)}, bf16[6144,384]{1,0:T(8,128)(2,1)}, u32[]{:S(2)}, u32[]{:S(2)}) collective-permute-start(bf16[6144,384]{1,0:T(8,128)(2,1)} %param.8), channel_id=1, source_target_pairs={{0,1},{1,0},{2,3},{3,2},{4,5},{5,4},{6,7},{7,6},{8,9},{9,8},{10,11... | collective-permute-start | bytes 14155784 | tf_op jit(solution)/shard_map/ppermute | solution.py:273
  61.0 17.7 %collective-permute-start = (bf16[4,288,256]{2,1,0:T(8,128)(2,1)S(1)}, bf16[4,288,256]{2,1,0:T(8,128)(2,1)S(1)}, u32[]{:S(2)}, u32[]{:S(2)}) collective-permute-start(bf16[4,288,256]{2,1,0:T(8,128)(2,1)S(1)} %bitcast.14), channel_id=1, source_target_pairs={{0,2},{1,3},{2,4},{3,5},{4,6},{5,7},{6,8},{7,9},{8,10},{9,11},{10,... | collective-permute-start | bytes 1769480 | tf_op jit(solution)/shard_map/ppermute | solution.py:270
  66.9 15.4 %collective-permute-start.1 = (bf16[4,288,256]{2,1,0:T(8,128)(2,1)S(1)}, bf16[4,288,256]{2,1,0:T(8,128)(2,1)S(1)}, u32[]{:S(2)}, u32[]{:S(2)}) collective-permute-start(bf16[4,288,256]{2,1,0:T(8,128)(2,1)S(1)} %bitcast.15), channel_id=1, source_target_pairs={{0,22},{1,23},{2,0},{3,1},{4,2},{5,3},{6,4},{7,5},{8,6},{9,7},{10,... | collective-permute-start | bytes 1769480 | tf_op jit(solution)/shard_map/ppermute | solution.py:270
  84.7 36.1 %all-to-all-start.1 = ((bf16[4,288,768]{2,1,0:T(8,128)(2,1)}), bf16[4,288,768]{2,1,0:T(8,128)(2,1)S(1)}, u32[]{:S(2)}, u32[]{:S(2)}) async-start(bf16[4,288,768]{2,1,0:T(8,128)(2,1)} %split.1), calls=%async_computation.1 | async-start | bytes 3538944 | tf_op jit(solution)/shard_map/all_to_all | solution.py:313
  89.5 11.3 %copy-start = (bf16[384,128]{1,0:T(8,128)(2,1)S(1)}, bf16[384,128]{1,0:T(8,128)(2,1)}, u32[]{:S(2)}) copy-start(bf16[384,128]{1,0:T(8,128)(2,1)} %cotangent.1) | copy-start | bytes 294916
  95.5 5.3 %collective-permute-start.3 = (f32[288,384]{1,0:T(8,128)S(1)}, f32[288,384]{1,0:T(8,128)S(1)}, u32[]{:S(2)}, u32[]{:S(2)}) collective-permute-start(f32[288,384]{1,0:T(8,128)S(1)} %get-tuple-element.12), channel_id=1, source_target_pairs={{0,1},{1,0},{2,3},{3,2},{4,5},{5,4},{6,7},{7,6},{8,9},{9,8},{10,11... | collective-permute-start | bytes 1327112 | tf_op jit(solution)/shard_map/ppermute | solution.py:273
  120.8 7.3 %collective-permute-start.4 = (bf16[4,288,768]{2,1,0:T(8,128)(2,1)S(1)}, bf16[4,288,768]{2,1,0:T(8,128)(2,1)S(1)}, u32[]{:S(2)}, u32[]{:S(2)}) collective-permute-start(bf16[4,288,768]{2,1,0:T(8,128)(2,1)S(1)} %all-to-all-done.1.near), channel_id=1, source_target_pairs={{0,1},{1,0},{2,3},{3,2},{4,5},{5,4},{6,7},{7,6},{8,9},{9,8},{10,11... | collective-permute-start | bytes 5308424 | tf_op jit(solution)/shard_map/ppermute | solution.py:273
  130.8 33.2 %all-to-all-start.2 = ((bf16[8,192,384]{2,1,0:T(8,128)(2,1)}), bf16[8,192,384]{2,1,0:T(8,128)(2,1)S(1)}, u32[]{:S(2)}, u32[]{:S(2)}) async-start(bf16[8,192,384]{2,1,0:T(8,128)(2,1)} %weight.1), calls=%async_computation.2 | async-start | bytes 2359296 | tf_op jit(solution)/shard_map/all_to_all | solution.py:348
